TPU v7x, 256 devices: a whole 4x4x8 slice. The times are simulated.
256 devices in a mesh: coarse: 32 (over y, x, core), leaf: 8 (over z).
Axes of the slice: x: 4, y: 4, z: 8, core: 2. Of those that a mesh axis runs over, the one named last changes fastest.
Arguments:
- vectors: bfloat16 [64, 1048576], P(None, ('coarse', 'leaf')), may hold values from -6 to 6
- leaf_basis: bfloat16 [32, 1048576], P(None, ('coarse', 'leaf')), may hold values from -0.75 to 0.75
- near_blocks: bfloat16 [12, 64, 1048576], P(None, None, ('coarse', 'leaf')), may hold values from -0.21875 to 0.21875
- near_index: int32 [12, 16384], P(None, ('coarse', 'leaf')), may hold values from 0 to 16383, as said below
- leaf_transfer: bfloat16 [32, 32, 16384], P(None, None, ('coarse', 'leaf')), may hold values from -0.75 to 0.75
- node_transfer: bfloat16 [32, 32, 2048], P(None, None, ('coarse', 'leaf')), may hold values from -0.75 to 0.75
- device_transfer: bfloat16 [32, 32, 256], P(None, None, ('coarse', 'leaf')), may hold values from -0.75 to 0.75
- leaf_lists: int32 [16, 16384], P(None, ('coarse', 'leaf')), may hold values from 0 to 16383, as said below
- leaf_coupling: bfloat16 [16, 32, 32, 16384], P(None, None, None, ('coarse', 'leaf')), may hold values from -0.25 to 0.25
- node_lists: int32 [16, 2048], P(None, ('coarse', 'leaf')), may hold values from 0 to 2047, as said below
- node_coupling: bfloat16 [16, 32, 32, 2048], P(None, None, None, ('coarse', 'leaf')), may hold values from -0.25 to 0.25
- device_lists: int32 [16, 256], P(None, ('coarse', 'leaf')), may hold values from 0 to 255
- device_coupling: bfloat16 [16, 32, 32, 256], P(None, None, None, ('coarse', 'leaf')), may hold values from -0.25 to 0.25
- group_lists: int32 [8, 32], P(None, 'coarse'), may hold values from 0 to 31
- group_coupling: bfloat16 [8, 32, 32, 32], P(None, None, None, 'coarse'), may hold values from -0.375 to 0.375
Outputs:
- product: bfloat16 [64, 1048576], P(None, ('coarse', 'leaf'))
Inputs may be any that keep to these rules, and one draw needn't show every extreme that they name: `near_index`: leaves sit on a grid of 128 x 32 x 4. Device node b (b = x block * 8 + y block) holds the 4 x 4 x 4 leaves of its blocks; within it, node m = (i * 2 + j) * 2 + k is the node at node position (2 x block + i, 2 y block + j, k), and its child c = 4 a + 2 b + e the leaf at twice that position plus (a, b, e). Each entry names a leaf whose position differs from its column's leaf by at most one in each direction; slot 0 by one in every direction (reflected at the grid's faces). `leaf_lists`: positions as for near_index; each entry names a leaf not adjacent to its column's leaf whose parent node is the parent of that leaf or adjacent to it; entries of a column may repeat where the grid's faces leave fewer than 16 such leaves. `node_lists`: node positions as for near_index; each entry names a node not adjacent to its column's node whose position halved (rounded down) differs from the column node's halved position by at most one in each direction; entries may repeat near the grid's faces.
All inputs are finite; a program needn't handle non-finite values.
Results may differ from a plain program's by a relative error of at most 0.017.
Values may be sent and summed in bfloat16 or wider, within the bound.
No kernel may reach another device: no remote copies, remote signals or barrier semaphores. Data moves between devices by JAX's collectives and lax.ppermute only.
A program may use at most 192 MiB of HBM per device.

v0:
```python
import jax
import jax.numpy as jnp
from jax import lax
from jax.experimental import pallas as pl
from jax.experimental.pallas import tpu as pltpu
from jax.sharding import PartitionSpec as P

BF = jnp.bfloat16
F32 = jnp.float32
V1, C1, N1 = 512, 512, 128
V2, C2, N2 = 768, 1024, 384
ROWS1 = V1 + C1 + N1
ROWS2 = V2 + C2 + N2
TAB = 144
MB = 1024 * 1024


def dot(a, b, ca, cb):
    return lax.dot_general(a, b, (((ca,), (cb,)), ((), ())), preferred_element_type=F32)


def copies(pairs, sems):
    started = [pltpu.make_async_copy(src, dst, sems.at[i]) for i, (src, dst) in enumerate(pairs)]
    for c in started:
        c.start()
    return started


def eye(n):
    rows = lax.broadcasted_iota(jnp.int32, (n, n), 0)
    cols = lax.broadcasted_iota(jnp.int32, (n, n), 1)
    return jnp.where(rows == cols, 1.0, 0.0).astype(BF)


def diagonal_mask():
    rows = lax.broadcasted_iota(jnp.int32, (128, 256), 0)
    cols = lax.broadcasted_iota(jnp.int32, (128, 256), 1)
    return jnp.where((rows >> 5) == (cols >> 6), 1.0, 0.0).astype(BF)


def low_lanes(rows):
    return lax.broadcasted_iota(jnp.int32, (rows, 128), 1) < 64


def node_parts(node):
    block, rest = node >> 3, node & 7
    return 2 * (block >> 3) + (rest >> 2), 2 * (block & 7) + ((rest >> 1) & 1), rest & 1


def up_kernel(
    v_hbm, b_hbm, lt_hbm, nt_hbm, dt_hbm, pay, cown, nown, up, dn, tl, fup, fdn,
    ct, tls, ncs, lt, v, b, nt, dt, sems,
):
    loads = copies(
        [
            (lt_hbm, lt), (v_hbm, v), (b_hbm, b), (nt_hbm, nt), (dt_hbm, dt),
        ],
        sems,
    )
    ident = eye(64)
    loads[0].wait()
    for k in range(32):
        tls[pl.ds(k, 64, stride=32), :] = dot(
            ident, jnp.concatenate([lt[k], jnp.zeros((96, 64), BF)], axis=0), 1, 1
        )
    tl[...] = tls[...].astype(BF)
    for c in loads[1:]:
        c.wait()
    mask = diagonal_mask()
    for g in range(16):
        lanes = slice(g * 256, (g + 1) * 256)
        bg = b[:, lanes]
        bd = jnp.concatenate([bg, bg, bg, bg], axis=0) * mask
        c = dot(bd, v[:, lanes], 1, 1)
        ct[g * 128:(g + 1) * 128, :] = c.astype(BF)
        for h in range(2):
            pair = jnp.concatenate([c[h * 64:h * 64 + 32], c[h * 64 + 32:h * 64 + 64]], axis=1)
            cown[(2 * g + h) * 32:(2 * g + h + 1) * 32, :] = pair.astype(BF)
    for m in range(4):
        parts = []
        for n in (2 * m, 2 * m + 1):
            rows = slice(n * 256, (n + 1) * 256)
            nc = dot(tl[rows, :32], ct[rows, :], 0, 0)
            parts.append(nc)
            wide = jnp.concatenate([nc, nc], axis=1)
            ncs[pl.ds(n, 32, stride=8), :] = wide.astype(BF).astype(F32)
        nown[m * 32:(m + 1) * 32, :] = jnp.concatenate(parts, axis=1).astype(BF)
    dc = dot(nt[...], ncs[...].astype(BF), 0, 0)
    terms = dot(dt[...], dc.astype(BF), 0, 0)
    message = jnp.where(low_lanes(32), dc, terms).astype(BF)
    for z in range(8):
        pay[z] = message
    for j in range(2):
        for k in range(2):
            for bb in range(2):
                at = ((2 * j + k) * 2 + bb) * 64
                first = ((2 * j + k) * 8 + 2 * bb) * 64
                dn[at:at + 64, :] = v[:, first:first + 128]
                first += 36 * 64
                up[at:at + 64, :] = v[:, first:first + 128]
    for i in range(2):
        for a in range(2):
            for k in range(2):
                at = ((i * 2 + a) * 2 + k) * 64
                first = ((i * 4 + k) * 8 + 4 * a) * 64
                fdn[at:at + 64, :] = v[:, first:first + 128]
                first += 18 * 64
                fup[at:at + 64, :] = v[:, first:first + 128]
    dn[V1:V1 + C1, :] = cown[0:512, :]
    up[V1:V1 + C1, :] = cown[512:1024, :]
    dn[V1 + C1:, :] = nown[...]
    up[V1 + C1:, :] = nown[...]


def pack_kernel(fup, fdn, cown, nown, bef, aft, up, dn, sems):
    moves = []
    for out, face, j in ((up, fup, 1), (dn, fdn, 0)):
        rows = [(face, 0, 512)]
        for side in (bef, aft):
            rows += [(side, ((2 * j + k) * 2 + j) * 64, 64) for k in range(2)]
        rows += [(cown, (i * 2 + j) * 256, 256) for i in range(2)]
        rows += [(side, V1 + j * 256, 256) for side in (bef, aft)]
        rows += [(nown, 0, 128), (bef, V1 + C1, 128), (aft, V1 + C1, 128)]
        at = 0
        for side, first, count in rows:
            moves.append((side.at[pl.ds(first, count)], out.at[pl.ds(at, count)]))
            at += count
    for c in copies(moves, sems):
        c.wait()


def group_kernel(r, after, y):
    low = low_lanes(32)
    total = jnp.zeros((32, 128), F32)
    for m in range(4):
        lo, hi = r[2 * m].astype(F32), r[2 * m + 1].astype(F32)
        total = total + lo + hi
        y[m * 32:(m + 1) * 32, :] = jnp.where(low, lo, pltpu.roll(hi, 64, 1)).astype(BF)
    swapped = pltpu.roll(total, 64, 1)
    y[128:144, :] = jnp.where(low_lanes(16), swapped[0:16], total[16:32]).astype(BF)


def prep_kernel(
    near_in, leaf_in, node_in, s_hbm, sn_hbm, sd_hbm, sg_hbm,
    zl, zn, zd, zg, near_ix, leaf_ix, node_ix, zs, ns, s, sn, sd, sg, sems,
):
    loads = copies(
        [(s_hbm.at[:, pl.ds(8 * q, 8)], s.at[:, pl.ds(8 * q, 8)]) for q in range(4)]
        + [(sn_hbm, sn), (sd_hbm, sd), (sg_hbm, sg)],
        sems,
    )
    cp, lp = lax.axis_index("coarse"), lax.axis_index("leaf")
    num = near_in[...]
    px, py, pz = node_parts(num >> 3)
    lx = 2 * px + ((num >> 2) & 1) - 4 * cp + 1
    ly = 2 * py + ((num >> 1) & 1) - 4 * lp + 1
    near_ix[...] = jnp.clip((lx * 6 + ly) * 4 + 2 * pz + (num & 1), 0, 143)
    num = leaf_in[...]
    px, py, pz = node_parts(num >> 3)
    at = ((px - 2 * cp + 1) * 4 + (py - 2 * lp + 1)) * 2 + pz
    leaf_ix[...] = jnp.clip(at * 8 + (num & 7), 0, 255)
    px, py, pz = node_parts(node_in[...])
    at = ((px - 2 * cp + 2) * 6 + (py - 2 * lp + 2)) * 2 + pz
    node_ix[...] = jnp.clip(at, 0, 71)
    ident = eye(64)
    for j in range(32):
        if j % 8 == 0:
            loads[j // 8].wait()
        t = dot(ident, s[:, j].reshape(512, 64), 1, 1)
        for q in range(4):
            zs[q, pl.ds(j, 64, stride=32), :] = t[:, q * 128:(q + 1) * 128]
    for c in loads[4:]:
        c.wait()
    for q in range(4):
        zl[:, q * 128:(q + 1) * 128] = zs[q].astype(BF)
        parts = [sn[4 * q + i].astype(F32).reshape(256, 32) for i in range(4)]
        ns[...] = jnp.concatenate(parts, axis=1)
        for n in range(8):
            zn[n * 32:(n + 1) * 32, q * 128:(q + 1) * 128] = ns[pl.ds(n, 32, stride=8), :].astype(BF)
        parts = [sd[4 * q + i].astype(F32) for i in range(4)]
        zd[:, q * 128:(q + 1) * 128] = jnp.concatenate(parts, axis=1).astype(BF)
    for q in range(2):
        parts = [sg[4 * q + i].astype(F32) for i in range(4)]
        zg[:, q * 128:(q + 1) * 128] = jnp.concatenate(parts, axis=1).astype(BF)


def near_kernel(ix_any, v, bef, aft, lb, la, blocks_hbm, out, low, high, picked, ix, blocks, sems):
    loads = copies(
        [(ix_any, ix)]
        + [(blocks_hbm.at[:, pl.ds(512 * t, 512)], blocks.at[t]) for t in range(8)],
        sems,
    )
    mask = low_lanes(64)

    def table():
        def put(wx, wy, k, x):
            at = (wx * 6 + wy) * 4 + 2 * k
            x = x.astype(F32)
            swapped = pltpu.roll(x, 64, 1)
            low[at] = jnp.where(mask, x, 0.0).astype(BF)
            high[at] = jnp.where(mask, 0.0, swapped).astype(BF)
            low[at + 1] = jnp.where(mask, swapped, 0.0).astype(BF)
            high[at + 1] = jnp.where(mask, 0.0, x).astype(BF)

        for i in range(2):
            for j in range(2):
                for k in range(2):
                    for a in range(2):
                        for bb in range(2):
                            first = (((i * 2 + j) * 2 + k) * 8 + 4 * a + 2 * bb) * 64
                            put(1 + 2 * i + a, 1 + 2 * j + bb, k, v[:, first:first + 128])
        for side, wx in ((bef, 0), (aft, 5)):
            for j in range(2):
                for k in range(2):
                    for bb in range(2):
                        first = ((2 * j + k) * 2 + bb) * 64
                        put(wx, 1 + 2 * j + bb, k, side[first:first + 64, :])
        for side, wy in ((lb, 0), (la, 5)):
            for i in range(2):
                for a in range(2):
                    for k in range(2):
                        first = ((i * 2 + a) * 2 + k) * 64
                        put(1 + 2 * i + a, wy, k, side[first:first + 64, :])
            for wx, base in ((0, 8), (5, 10)):
                for k in range(2):
                    first = (base + k) * 64
                    put(wx, wy, k, side[first:first + 64, :])

    table()
    loads[0].wait()

    def chunk(t, carry):
        pltpu.make_async_copy(
            blocks_hbm.at[:, pl.ds(pl.multiple_of(512 * t, 512), 512)], blocks.at[t], sems.at[t + 1]
        ).wait()
        for q in range(4):
            for i in range(2):
                leaf = t * 8 + 2 * q + i
                for sp in range(6):
                    picked[q, i * 64:(i + 1) * 64, sp * 128:(sp + 1) * 128] = (
                        low[ix[2 * sp, leaf]] + high[ix[2 * sp + 1, leaf]]
                    )
            r = dot(picked[q], blocks[t, :, q * 128:(q + 1) * 128], 1, 0)
            lanes = pl.ds(pl.multiple_of(t * 512 + q * 128, 128), 128)
            out[:, lanes] = jnp.where(mask, r[:64], r[64:])
        return carry

    lax.fori_loop(0, 8, chunk, 0)


def far_kernel(
    li_any, mi_any, cown, nown, bef, aft, lb, la, zl, zn, far, nfar, cw, nw, li, mi, sems
):
    loads = copies([(li_any, li), (mi_any, mi)], sems)

    def put_leaves(nwx, nwy, k, side, first):
        for p in range(4):
            x = side[first + p * 32:first + (p + 1) * 32, :]
            at = ((nwx * 4 + nwy) * 2 + k) * 8 + 2 * p
            cw[at] = x
            cw[at + 1] = pltpu.roll(x.astype(F32), 64, 1).astype(BF)

    def put_nodes(nwx, nwy, side, first):
        x = side[first:first + 32, :]
        at = (nwx * 6 + nwy) * 2
        nw[at] = x
        nw[at + 1] = pltpu.roll(x.astype(F32), 64, 1).astype(BF)

    for i in range(2):
        for j in range(2):
            put_nodes(2 + i, 2 + j, nown, (i * 2 + j) * 32)
            put_nodes(i, 2 + j, bef, V1 + C1 + (i * 2 + j) * 32)
            put_nodes(4 + i, 2 + j, aft, V1 + C1 + (i * 2 + j) * 32)
            for side, base in ((lb, 0), (la, 4)):
                first = V2 + C2 + (i * 2 + j) * 32
                put_nodes(2 + i, base + j, side, first)
                put_nodes(i, base + j, side, first + 128)
                put_nodes(4 + i, base + j, side, first + 256)
            for k in range(2):
                put_leaves(1 + i, 1 + j, k, cown, ((i * 2 + j) * 2 + k) * 128)
    for j in range(2):
        for k in range(2):
            put_leaves(0, 1 + j, k, bef, V1 + (2 * j + k) * 128)
            put_leaves(3, 1 + j, k, aft, V1 + (2 * j + k) * 128)
    for side, nwy in ((lb, 0), (la, 3)):
        for k in range(2):
            for i in range(2):
                put_leaves(1 + i, nwy, k, side, V2 + (2 * i + k) * 128)
            put_leaves(0, nwy, k, side, V2 + 512 + k * 128)
            put_leaves(3, nwy, k, side, V2 + 768 + k * 128)

    for c in loads:
        c.wait()
    for n in range(8):
        block = jnp.concatenate([nw[mi[n, s]] for s in range(16)], axis=0)
        nfar[n * 32:(n + 1) * 32, :] = dot(zn[n * 32:(n + 1) * 32, :], block, 1, 0)

    def leaves(t, carry):
        for u in range(4):
            n = t * 4 + u
            block = jnp.concatenate([cw[li[s, n]] for s in range(16)], axis=0)
            rows = pl.ds(pl.multiple_of(n * 32, 32), 32)
            far[rows, :] = dot(zl[rows, :], block, 1, 0)
        return carry

    lax.fori_loop(0, 16, leaves, 0)


def table_kernel(y, received, after, own):
    half = y.shape[0]
    own[0:half, :] = y[...]
    own[half:, :] = received[...]


def down_kernel(dl, gl, own, other, zd, zg, dt, nt, tl, b, far, nfar, near, out, nds):
    cp = lax.axis_index("coarse")

    def pick(coarse, row, count):
        at = (coarse ^ cp) >> 1
        rows = pl.ds(pl.multiple_of(at * TAB + row, 16), count)
        same = ((coarse ^ cp) & 1) == 0
        return jnp.where(same, own[rows, :].astype(F32), other[rows, :].astype(F32))

    parts = []
    for s in range(8):
        x = pick(gl[0, s], 128, 16)
        parts += [x.astype(BF), pltpu.roll(x, 64, 1).astype(BF)]
    gf = dot(zg[...], jnp.concatenate(parts, axis=0), 1, 0).astype(BF)
    parts = []
    for s in range(16):
        d = dl[0, s]
        x = pick(d >> 3, ((d & 7) >> 1) * 32, 32)
        parts.append(jnp.where((d & 1) == 1, pltpu.roll(x, 64, 1), x).astype(BF))
    df = dot(zd[...], jnp.concatenate(parts, axis=0), 1, 0) + dot(dt[...], gf, 1, 0)
    nds[...] = dot(nt[...], df.astype(BF), 1, 0)
    mask = diagonal_mask()
    for n in range(8):
        nf = (nds[pl.ds(n, 32, stride=8), :] + nfar[n * 32:(n + 1) * 32, :]).astype(BF)
        rows = slice(n * 256, (n + 1) * 256)
        lf = (dot(tl[rows, :32], nf, 1, 0) + far[rows, :]).astype(BF)
        for h in range(2):
            g = 2 * n + h
            lanes = slice(g * 256, (g + 1) * 256)
            bg = b[:, lanes]
            bd = jnp.concatenate([bg, bg, bg, bg], axis=0) * mask
            x = dot(lf[h * 128:(h + 1) * 128, :64], bd, 0, 0)
            out[:, lanes] = (x + near[:, lanes]).astype(BF)


AN = pl.BlockSpec(memory_space=pl.ANY)
HB = pl.BlockSpec(memory_space=pltpu.HBM)
VM = pl.BlockSpec(memory_space=pltpu.VMEM)
SM = pl.BlockSpec(memory_space=pltpu.SMEM)


def shape(dims, dtype=BF):
    return jax.ShapeDtypeStruct(dims, dtype)


def params(mib):
    return pltpu.CompilerParams(vmem_limit_bytes=mib * MB)


def cost(flops, size):
    return pl.CostEstimate(flops=flops, bytes_accessed=size, transcendentals=0)


def body(
    vectors, leaf_basis, near_blocks, near_index, leaf_transfer, node_transfer, device_transfer,
    leaf_lists, leaf_coupling, node_lists, node_coupling, device_lists, device_coupling,
    group_lists, group_coupling,
):
    nt = jnp.transpose(node_transfer, (0, 2, 1)).reshape(256, 32)
    dt = device_transfer.reshape(32, 32)
    pay, cown, nown, up, dn, tl, fup, fdn = pl.pallas_call(
        up_kernel,
        out_shape=[
            shape((8, 32, 128)), shape((1024, 128)), shape((128, 128)),
            shape((ROWS1, 128)), shape((ROWS1, 128)), shape((2048, 128)),
            shape((512, 128)), shape((512, 128)),
        ],
        in_specs=[HB] * 5,
        out_specs=[VM] * 8,
        scratch_shapes=[
            pltpu.VMEM((2048, 64), BF), pltpu.VMEM((2048, 128), F32), pltpu.VMEM((256, 128), F32),
            pltpu.VMEM((32, 32, 64), BF), pltpu.VMEM((64, 4096), BF), pltpu.VMEM((32, 4096), BF),
            pltpu.VMEM((256, 32), BF), pltpu.VMEM((32, 32), BF), pltpu.SemaphoreType.DMA((5,)),
        ],
        compiler_params=params(58),
        cost_estimate=cost(10**9, 4 * 10**6),
        name="up_pass",
    )(vectors, leaf_basis, leaf_transfer, nt, dt)

    coarse, leafs = lax.axis_size("coarse"), lax.axis_size("leaf")
    r = lax.all_to_all(pay, "leaf", 0, 0, tiled=True)

    def shift(x, axis, step):
        size = lax.axis_size(axis)
        pairs = [(i, i + step) for i in range(size) if 0 <= i + step < size]
        return lax.ppermute(x, axis, pairs)

    bef, aft = shift(up, "coarse", 1), shift(dn, "coarse", -1)

    zl, zn, zd, zg, near_ix, leaf_ix, node_ix = pl.pallas_call(
        prep_kernel,
        out_shape=[
            shape((2048, 512)), shape((256, 512)), shape((32, 512)), shape((32, 256)),
            shape((12, 64), jnp.int32), shape((16, 64), jnp.int32), shape((8, 16), jnp.int32),
        ],
        in_specs=[VM] * 3 + [HB] * 4,
        out_specs=[VM] * 7,
        scratch_shapes=[
            pltpu.VMEM((4, 2048, 128), F32), pltpu.VMEM((256, 128), F32),
            pltpu.VMEM((16, 32, 32, 64), BF), pltpu.VMEM((16, 32, 8, 32), BF),
            pltpu.VMEM((16, 32, 32), BF), pltpu.VMEM((8, 32, 32), BF),
            pltpu.SemaphoreType.DMA((7,)),
        ],
        compiler_params=params(48),
        cost_estimate=cost(10**9, 8 * 10**6),
        name="coupling_layout",
    )(
        near_index, leaf_lists, node_lists.T, leaf_coupling, jnp.transpose(node_coupling, (0, 1, 3, 2)),
        device_coupling.reshape(16, 32, 32), group_coupling.reshape(8, 32, 32),
    )

    up2, dn2 = pl.pallas_call(
        pack_kernel,
        out_shape=[shape((ROWS2, 128))] * 2,
        in_specs=[HB] * 6,
        out_specs=[VM] * 2,
        scratch_shapes=[pltpu.SemaphoreType.DMA((24,))],
        compiler_params=params(58),
        cost_estimate=cost(1000, 10**6),
        name="halo_pack",
    )(fup, fdn, cown, nown, bef, aft)
    lb, la = shift(up2, "leaf", 1), shift(dn2, "leaf", -1)

    y = pl.pallas_call(
        group_kernel,
        out_shape=shape((TAB, 128)),
        in_specs=[VM, HB],
        out_specs=VM,
        compiler_params=params(8),
        cost_estimate=cost(1000, 10**5),
        name="group_sum",
    )(r, up2)
    flip = lambda x, bit: lax.ppermute(x, "coarse", [(i, i ^ bit) for i in range(coarse)])
    for bit in (2, 4, 8):
        y = jnp.concatenate([y, flip(y, bit)], axis=0)
    received = flip(y, 16)

    near = pl.pallas_call(
        near_kernel,
        out_shape=shape((64, 4096), F32),
        in_specs=[AN, VM, VM, VM, VM, VM, HB],
        out_specs=VM,
        scratch_shapes=[
            pltpu.VMEM((144, 64, 128), BF), pltpu.VMEM((144, 64, 128), BF),
            pltpu.VMEM((4, 128, 768), BF), pltpu.SMEM((12, 64), jnp.int32),
            pltpu.VMEM((8, 768, 512), BF), pltpu.SemaphoreType.DMA((9,)),
        ],
        compiler_params=params(48),
        cost_estimate=cost(4 * 10**9, 16 * 10**6),
        name="near_field",
    )(near_ix, vectors, bef, aft, lb, la, near_blocks.reshape(768, 4096))

    own = pl.pallas_call(
        table_kernel,
        out_shape=shape((16 * TAB, 128)),
        in_specs=[VM, VM, AN],
        out_specs=VM,
        compiler_params=params(8),
        cost_estimate=cost(1000, 10**6),
        name="table_join",
    )(y, received, near)
    other = flip(own, 1)

    far, nfar = pl.pallas_call(
        far_kernel,
        out_shape=[shape((2048, 128), F32), shape((256, 128), F32)],
        in_specs=[AN] * 2 + [VM] * 8,
        out_specs=[VM] * 2,
        scratch_shapes=[
            pltpu.VMEM((256, 32, 128), BF), pltpu.VMEM((72, 32, 128), BF),
            pltpu.SMEM((16, 64), jnp.int32), pltpu.SMEM((8, 16), jnp.int32),
            pltpu.SemaphoreType.DMA((2,)),
        ],
        compiler_params=params(32),
        cost_estimate=cost(4 * 10**9, 16 * 10**6),
        name="far_field",
    )(leaf_ix, node_ix, cown, nown, bef, aft, lb, la, zl, zn)

    return pl.pallas_call(
        down_kernel,
        out_shape=shape((64, 4096)),
        in_specs=[SM] * 2 + [VM] * 11,
        out_specs=VM,
        scratch_shapes=[pltpu.VMEM((256, 128), F32)],
        compiler_params=params(32),
        cost_estimate=cost(10**9, 4 * 10**6),
        name="down_pass",
    )(
        device_lists.reshape(1, 16), group_lists.reshape(1, 8), own, other, zd, zg, dt, nt, tl,
        leaf_basis, far, nfar, near,
    )


def solution(mesh):
    both = ("coarse", "leaf")
    placed = (
        P(None, both), P(None, both), P(None, None, both), P(None, both), P(None, None, both),
        P(None, None, both), P(None, None, both), P(None, both), P(None, None, None, both),
        P(None, both), P(None, None, None, both), P(None, both), P(None, None, None, both),
        P(None, "coarse"), P(None, None, None, "coarse"),
    )
    return jax.shard_map(
        body, mesh=mesh, in_specs=placed, out_specs=P(None, both), check_vma=False
    )
```

profile of v0, /device:TPU:1, one launch (start us, length us, event | category | flops | bytes accessed | tf_op | source)
XLA Modules:
  0.0 68.3 jit_solution(16247825729088038001)
XLA Ops:
  0.0 0.0 copy-start.10
  0.0 0.0 copy-start.9
  0.0 0.0 copy-start
  0.0 0.0 copy-start.16
  0.0 0.0 copy-start.14
  0.0 0.0 copy-start.13
  0.0 4.1 %up_pass.1 = (bf16[8,32,128]{2,1,0:T(8,128)(2,1)}, bf16[1024,128]{1,0:T(8,128)(2,1)}, bf16[128,128]{1,0:T(8,128)(2,1)}, bf16[1152,128]{1,0:T(8,128)(2,1)}, bf16[...) custom-call(bf16[64,4096]{1,0:T(8,128)(2,1)} %v.1, ...), custom_call_target="tpu_custom_call" | custom-call | flops 1000000000 | bytes 4000000 | tf_op jit(solution)/shard_map/up_pass/pallas_call | solution.py:375
  4.2 4.5 %collective-permute-start = (bf16[1152,128]{1,0:T(8,128)(2,1)}, bf16[1152,128]{1,0:T(8,128)(2,1)S(1)}, u32[]{:S(2)}, u32[]{:S(2)}) collective-permute-start(bf16[1152,128]{1,0:T(8,128)(2,1)} %get-tuple-element.29), channel_id=1, source_target_pairs={{0,8},{8,16},{16,24},{24,32},{32,40},{40,48},{48,56},{56,64},{64,7... | collective-permute-start | bytes 884744 | tf_op jit(solution)/shard_map/ppermute | solution.py:400
  8.7 1.9 %collective-permute-start.1 = (bf16[1152,128]{1,0:T(8,128)(2,1)}, bf16[1152,128]{1,0:T(8,128)(2,1)S(1)}, u32[]{:S(2)}, u32[]{:S(2)}) collective-permute-start(bf16[1152,128]{1,0:T(8,128)(2,1)} %get-tuple-element.30), channel_id=1, source_target_pairs={{8,0},{16,8},{24,16},{32,24},{40,32},{48,40},{56,48},{64,56},{72,6... | collective-permute-start | bytes 884744 | tf_op jit(solution)/shard_map/ppermute | solution.py:400
  10.6 0.0 copy-start.19
  10.6 8.3 %all-to-all-start = ((bf16[8,32,128]{2,1,0:T(8,128)(2,1)}), bf16[8,32,128]{2,1,0:T(8,128)(2,1)S(1)}, u32[]{:S(2)}, u32[]{:S(2)}) async-start(bf16[8,32,128]{2,1,0:T(8,128)(2,1)} %get-tuple-element.24), calls=%async_computation | async-start | bytes 131072 | tf_op jit(solution)/shard_map/all_to_all | solution.py:395
  18.9 0.0 collective-permute-done.bef
  19.0 0.0 copy-start.3
  19.0 0.0 collective-permute-done.1.aft
  19.0 0.0 copy-start.5
  19.0 0.7 copy-done.3
  19.7 0.1 copy-done.5
  19.8 2.5 %halo_pack.1 = (bf16[2176,128]{1,0:T(8,128)(2,1)}, bf16[2176,128]{1,0:T(8,128)(2,1)}) custom-call(bf16[512,128]{1,0:T(8,128)(2,1)} %get-tuple-element.25.fup, bf16[512,128]{1,0:T(8,128)(2,1)} %get-tuple-element.26.fdn, bf16[1024,128]{1,0:T(8,128)(2,1)} %get-tuple-element.27.cown, bf16[128,128]{1,0:T(8,128)(2,1)} %get-tuple-element.28.nown, ...), custom_call_target="tpu_custom_call" | custom-call | flops 1000 | bytes 1000000 | tf_op jit(solution)/shard_map/halo_pack/pallas_call | solution.py:426
  22.2 3.9 %all-to-all-done.r = bf16[8,32,128]{2,1,0:T(8,128)(2,1)S(1)} async-done(((bf16[8,32,128]{2,1,0:T(8,128)(2,1)}), bf16[8,32,128]{2,1,0:T(8,128)(2,1)S(1)}, u32[]{:S(2)}, u32[]{:S(2)}) %all-to-all-start) | async-done | bytes 65568 | tf_op jit(solution)/shard_map/all_to_all | solution.py:395
  26.2 0.0 copy-start.1
  26.2 1.1 %copy-done.1 = bf16[2176,128]{1,0:T(8,128)(2,1)S(1)} copy-done((bf16[2176,128]{1,0:T(8,128)(2,1)S(1)}, bf16[2176,128]{1,0:T(8,128)(2,1)}, u32[]{:S(2)}) %copy-start.1) | copy-done | bytes 557080
  27.2 0.0 copy-start.4
  27.2 0.1 group_sum.1
  27.3 1.4 %collective-permute-start.2 = (bf16[144,128]{1,0:T(8,128)(2,1)S(1)}, bf16[144,128]{1,0:T(8,128)(2,1)S(1)}, u32[]{:S(2)}, u32[]{:S(2)}) collective-permute-start(bf16[144,128]{1,0:T(8,128)(2,1)S(1)} %group_sum.1), channel_id=1, source_target_pairs={{0,16},{8,24},{16,0},{24,8},{32,48},{40,56},{48,32},{56,40},{64,80... | collective-permute-start | bytes 110600 | tf_op jit(solution)/shard_map/ppermute | solution.py:447
  28.7 1.5 %collective-permute-done.2 = bf16[144,128]{1,0:T(8,128)(2,1)S(1)} collective-permute-done((bf16[144,128]{1,0:T(8,128)(2,1)S(1)}, bf16[144,128]{1,0:T(8,128)(2,1)S(1)}, u32[]{:S(2)}, u32[]{:S(2)}) %collective-permute-start.2) | collective-permute-done | bytes 36896 | tf_op jit(solution)/shard_map/ppermute | solution.py:447
  30.2 2.4 %collective-permute-start.3 = (bf16[288,128]{1,0:T(8,128)(2,1)S(1)}, bf16[288,128]{1,0:T(8,128)(2,1)S(1)}, u32[]{:S(2)}, u32[]{:S(2)}) collective-permute-start(bf16[288,128]{1,0:T(8,128)(2,1)S(1)} %pad_maximum_fusion.2), channel_id=1, source_target_pairs={{0,32},{8,40},{16,48},{24,56},{32,0},{40,8},{48,16},{56,24},{64,96... | collective-permute-start | bytes 221192 | tf_op jit(solution)/shard_map/ppermute | solution.py:447
  32.7 1.3 %collective-permute-start.7 = (bf16[2176,128]{1,0:T(8,128)(2,1)}, bf16[2176,128]{1,0:T(8,128)(2,1)S(1)}, u32[]{:S(2)}, u32[]{:S(2)}) collective-permute-start(bf16[2176,128]{1,0:T(8,128)(2,1)} %get-tuple-element.33), channel_id=1, source_target_pairs={{1,0},{2,1},{3,2},{4,3},{5,4},{6,5},{7,6},{9,8},{10,9},{11,10},{12... | collective-permute-start | bytes 1671176 | tf_op jit(solution)/shard_map/ppermute | solution.py:400
  34.0 4.0 %collective-permute-start.6 = (bf16[2176,128]{1,0:T(8,128)(2,1)}, bf16[2176,128]{1,0:T(8,128)(2,1)S(1)}, u32[]{:S(2)}, u32[]{:S(2)}) collective-permute-start(bf16[2176,128]{1,0:T(8,128)(2,1)} %get-tuple-element.31.after), channel_id=1, source_target_pairs={{0,1},{1,2},{2,3},{3,4},{4,5},{5,6},{6,7},{8,9},{9,10},{10,11},{11... | collective-permute-start | bytes 1671176 | tf_op jit(solution)/shard_map/ppermute | solution.py:400
  38.0 0.0 collective-permute-done.3
  38.0 1.4 %collective-permute-start.4 = (bf16[576,128]{1,0:T(8,128)(2,1)S(1)}, bf16[576,128]{1,0:T(8,128)(2,1)S(1)}, u32[]{:S(2)}, u32[]{:S(2)}) collective-permute-start(bf16[576,128]{1,0:T(8,128)(2,1)S(1)} %pad_maximum_fusion.1), channel_id=1, source_target_pairs={{0,64},{8,72},{16,80},{24,88},{32,96},{40,104},{48,112},{56,120},{... | collective-permute-start | bytes 442376 | tf_op jit(solution)/shard_map/ppermute | solution.py:447
  39.4 0.0 copy-done.10
  39.4 0.0 copy-done.9
  39.4 0.0 copy-done
  39.4 0.0 copy-done.16
  39.4 0.0 copy-done.14
  39.4 0.0 copy-done.13
  39.4 7.0 %coupling_layout.1 = (bf16[2048,512]{1,0:T(8,128)(2,1)S(1)}, bf16[256,512]{1,0:T(8,128)(2,1)S(1)}, bf16[32,512]{1,0:T(8,128)(2,1)S(1)}, bf16[32,256]{1,0:T(8,128...) custom-call(s32[12,64]{1,0:T(8,128)S(1)} %copy-done.13, s32[16,64]{1,0:T(8,128)S(1)} %copy-done.14, ...), custom_call_target="tpu_custom_call" | custom-call | flops 1000000000 | bytes 8000000 | tf_op jit(solution)/shard_map/coupling_layout/pallas_call | solution.py:404
  46.5 0.0 collective-permute-done.4
  46.5 2.7 %collective-permute-start.5 = (bf16[1152,128]{1,0:T(8,128)(2,1)S(1)}, bf16[1152,128]{1,0:T(8,128)(2,1)S(1)}, u32[]{:S(2)}, u32[]{:S(2)}) collective-permute-start(bf16[1152,128]{1,0:T(8,128)(2,1)S(1)} %pad_maximum_fusion.y), channel_id=1, source_target_pairs={{0,128},{8,136},{16,144},{24,152},{32,160},{40,168},{48,176},{56,1... | collective-permute-start | bytes 884744 | tf_op jit(solution)/shard_map/ppermute | solution.py:447
  49.2 0.0 collective-permute-done.7.la
  49.2 0.0 collective-permute-done.6.lb
  49.2 0.0 copy-done.19
  49.3 0.0 copy-done.4
  49.3 0.0 copy-done.6
  49.3 0.0 copy-start.7
  49.3 0.0 copy-start.12
  49.3 6.2 %near_field.1.after.near = f32[64,4096]{1,0:T(8,128)S(1)} custom-call(s32[12,64]{1,0:T(8,128)S(1)} %get-tuple-element.32.ix_any, bf16[64,4096]{1,0:T(8,128)(2,1)S(1)} %copy-done.19, bf16[1152,128]{1,0:T(8,128)(2,1)S(1)} %copy-done.4, bf16[1152,128]{1,0:T(8,128)(2,1)S(1)} %copy-done.6, bf16[2176,128]{1,0:T(8,128)(2,1)S(1)} %collective-permute-done.6.lb, ...), custom_call_target="tpu_custom_call" | custom-call | flops 4000000000 | bytes 16000000 | tf_op jit(solution)/shard_map/near_field/pallas_call | solution.py:452
  55.5 0.0 collective-permute-done.5.received
  55.5 5.0 %collective-permute-start.8 = (bf16[2304,128]{1,0:T(8,128)(2,1)S(1)}, bf16[2304,128]{1,0:T(8,128)(2,1)S(1)}, u32[]{:S(2)}, u32[]{:S(2)}) collective-permute-start(bf16[2304,128]{1,0:T(8,128)(2,1)S(1)} %table_join.1.own), channel_id=1, source_target_pairs={{0,8},{8,0},{16,24},{24,16},{32,40},{40,32},{48,56},{56,48},{64,72... | collective-permute-start | bytes 1769480 | tf_op jit(solution)/shard_map/ppermute | solution.py:447
  60.5 0.0 copy-done.7
  60.5 0.0 copy-done.12
  60.5 0.0 copy-start.11
  60.5 0.0 copy-start.15
  60.5 0.0 copy-start.17
  60.6 0.0 copy-start.18
  60.6 5.0 %far_field.1 = (f32[2048,128]{1,0:T(8,128)S(1)}, f32[256,128]{1,0:T(8,128)S(1)}) custom-call(s32[16,64]{1,0:T(8,128)S(1)} %get-tuple-element.37.li_any, s32[8,16]{1,0:T(8,128)S(1)} %get-tuple-element.38.mi_any, bf16[1024,128]{1,0:T(8,128)(2,1)S(1)} %copy-done.7, bf16[128,128]{1,0:T(8,128)(2,1)S(1)} %copy-done.12, bf16[1152,128]{1,0:T(8,128)(2,1)S(1)} %copy-done.4, ...), custom_call_target="tpu_custom_call" | custom-call | flops 4000000000 | bytes 16000000 | tf_op jit(solution)/shard_map/far_field/pallas_call | solution.py:478
  65.6 0.0 collective-permute-done.8.other
  65.6 0.0 copy-done.2
  65.6 0.0 copy-done.8
  65.6 0.0 copy-done.11
  65.6 0.0 copy-done.15
  65.6 0.0 copy-done.17
  65.6 0.0 copy-done.18
  65.7 2.6 %down_pass.1 = bf16[64,4096]{1,0:T(8,128)(2,1)} custom-call(s32[1,16]{1,0:T(1,128)S(1)} %bitcast.19, s32[1,8]{1,0:T(1,128)S(1)} %bitcast.20, bf16[2304,128]{1,0:T(8,128)(2,1)S(1)} %table_join.1.own, bf16[2304,128]{1,0:T(8,128)(2,1)S(1)} %collective-permute-done.8.other, bf16[32,512]{1,0:T(8,128)(2,1)S(1)} %get-tuple-element.34.zd, ...), custom_call_target="tpu_custom_call" | custom-call | flops 1000000000 | bytes 4000000 | tf_op jit(solution)/shard_map/down_pass/pallas_call | solution.py:493
  (7 shorter events, 0.1 us)
Async XLA Ops:
  0.0 39.4 %copy-start.10 = (bf16[8,32,32,1]{2,1,3,0:T(8,128)(2,1)S(1)}, bf16[8,32,32,1]{2,1,3,0:T(8,128)(2,1)}, u32[]{:S(2)}) copy-start(bf16[8,32,32,1]{2,1,3,0:T(8,128)(2,1)} %param.29) | copy-start | bytes 49156
  0.0 39.4 %copy-start.9 = (bf16[16,32,32,1]{2,1,3,0:T(8,128)(2,1)S(1)}, bf16[16,32,32,1]{2,1,3,0:T(8,128)(2,1)}, u32[]{:S(2)}) copy-start(bf16[16,32,32,1]{2,1,3,0:T(8,128)(2,1)} %param.27) | copy-start | bytes 98308
  0.0 39.4 %copy-start = (bf16[16,32,32,8]{2,3,1,0:T(8,128)(2,1)S(1)}, bf16[16,32,32,8]{2,3,1,0:T(8,128)(2,1)}, u32[]{:S(2)}) copy-start(bf16[16,32,32,8]{2,3,1,0:T(8,128)(2,1)} %param.25) | copy-start | bytes 786436
  0.0 39.4 %copy-start.16 = (s32[16,8]{0,1:T(8,128)S(1)}, s32[16,8]{0,1:T(8,128)}, u32[]{:S(2)}) copy-start(s32[16,8]{0,1:T(8,128)} %param.24) | copy-start | bytes 1540
  0.0 39.4 %copy-start.14 = (s32[16,64]{1,0:T(8,128)S(1)}, s32[16,64]{1,0:T(8,128)}, u32[]{:S(2)}) copy-start(s32[16,64]{1,0:T(8,128)} %leaf_in.1) | copy-start | bytes 12292
  0.0 39.4 %copy-start.13 = (s32[12,64]{1,0:T(8,128)S(1)}, s32[12,64]{1,0:T(8,128)}, u32[]{:S(2)}) copy-start(s32[12,64]{1,0:T(8,128)} %near_in.1) | copy-start | bytes 9220
  4.2 14.8 %collective-permute-start = (bf16[1152,128]{1,0:T(8,128)(2,1)}, bf16[1152,128]{1,0:T(8,128)(2,1)S(1)}, u32[]{:S(2)}, u32[]{:S(2)}) collective-permute-start(bf16[1152,128]{1,0:T(8,128)(2,1)} %get-tuple-element.29), channel_id=1, source_target_pairs={{0,8},{8,16},{16,24},{24,32},{32,40},{40,48},{48,56},{56,64},{64,7... | collective-permute-start | bytes 884744 | tf_op jit(solution)/shard_map/ppermute | solution.py:400
  8.7 10.3 %collective-permute-start.1 = (bf16[1152,128]{1,0:T(8,128)(2,1)}, bf16[1152,128]{1,0:T(8,128)(2,1)S(1)}, u32[]{:S(2)}, u32[]{:S(2)}) collective-permute-start(bf16[1152,128]{1,0:T(8,128)(2,1)} %get-tuple-element.30), channel_id=1, source_target_pairs={{8,0},{16,8},{24,16},{32,24},{40,32},{48,40},{56,48},{64,56},{72,6... | collective-permute-start | bytes 884744 | tf_op jit(solution)/shard_map/ppermute | solution.py:400
  10.6 38.6 %copy-start.19 = (bf16[64,4096]{1,0:T(8,128)(2,1)S(1)}, bf16[64,4096]{1,0:T(8,128)(2,1)}, u32[]{:S(2)}) copy-start(bf16[64,4096]{1,0:T(8,128)(2,1)} %v.1) | copy-start | bytes 1572868
  10.6 15.5 %all-to-all-start = ((bf16[8,32,128]{2,1,0:T(8,128)(2,1)}), bf16[8,32,128]{2,1,0:T(8,128)(2,1)S(1)}, u32[]{:S(2)}, u32[]{:S(2)}) async-start(bf16[8,32,128]{2,1,0:T(8,128)(2,1)} %get-tuple-element.24), calls=%async_computation | async-start | bytes 131072 | tf_op jit(solution)/shard_map/all_to_all | solution.py:395
  19.0 0.7 %copy-start.3 = (bf16[1152,128]{1,0:T(8,128)(2,1)}, bf16[1152,128]{1,0:T(8,128)(2,1)S(1)}, u32[]{:S(2)}) copy-start(bf16[1152,128]{1,0:T(8,128)(2,1)S(1)} %collective-permute-done.bef) | copy-start | bytes 884740
  19.0 0.8 %copy-start.5 = (bf16[1152,128]{1,0:T(8,128)(2,1)}, bf16[1152,128]{1,0:T(8,128)(2,1)S(1)}, u32[]{:S(2)}) copy-start(bf16[1152,128]{1,0:T(8,128)(2,1)S(1)} %collective-permute-done.1.aft) | copy-start | bytes 884740
  26.2 1.1 %copy-start.1 = (bf16[2176,128]{1,0:T(8,128)(2,1)S(1)}, bf16[2176,128]{1,0:T(8,128)(2,1)}, u32[]{:S(2)}) copy-start(bf16[2176,128]{1,0:T(8,128)(2,1)} %get-tuple-element.31.after) | copy-start | bytes 1671172
  27.2 22.0 %copy-start.4 = (bf16[1152,128]{1,0:T(8,128)(2,1)S(1)}, bf16[1152,128]{1,0:T(8,128)(2,1)}, u32[]{:S(2)}) copy-start(bf16[1152,128]{1,0:T(8,128)(2,1)} %copy-done.3) | copy-start | bytes 884740
  27.2 22.0 %copy-start.6 = (bf16[1152,128]{1,0:T(8,128)(2,1)S(1)}, bf16[1152,128]{1,0:T(8,128)(2,1)}, u32[]{:S(2)}) copy-start(bf16[1152,128]{1,0:T(8,128)(2,1)} %copy-done.5) | copy-start | bytes 884740
  27.3 2.9 %collective-permute-start.2 = (bf16[144,128]{1,0:T(8,128)(2,1)S(1)}, bf16[144,128]{1,0:T(8,128)(2,1)S(1)}, u32[]{:S(2)}, u32[]{:S(2)}) collective-permute-start(bf16[144,128]{1,0:T(8,128)(2,1)S(1)} %group_sum.1), channel_id=1, source_target_pairs={{0,16},{8,24},{16,0},{24,8},{32,48},{40,56},{48,32},{56,40},{64,80... | collective-permute-start | bytes 110600 | tf_op jit(solution)/shard_map/ppermute | solution.py:447
  30.2 7.8 %collective-permute-start.3 = (bf16[288,128]{1,0:T(8,128)(2,1)S(1)}, bf16[288,128]{1,0:T(8,128)(2,1)S(1)}, u32[]{:S(2)}, u32[]{:S(2)}) collective-permute-start(bf16[288,128]{1,0:T(8,128)(2,1)S(1)} %pad_maximum_fusion.2), channel_id=1, source_target_pairs={{0,32},{8,40},{16,48},{24,56},{32,0},{40,8},{48,16},{56,24},{64,96... | collective-permute-start | bytes 221192 | tf_op jit(solution)/shard_map/ppermute | solution.py:447
  32.7 16.6 %collective-permute-start.7 = (bf16[2176,128]{1,0:T(8,128)(2,1)}, bf16[2176,128]{1,0:T(8,128)(2,1)S(1)}, u32[]{:S(2)}, u32[]{:S(2)}) collective-permute-start(bf16[2176,128]{1,0:T(8,128)(2,1)} %get-tuple-element.33), channel_id=1, source_target_pairs={{1,0},{2,1},{3,2},{4,3},{5,4},{6,5},{7,6},{9,8},{10,9},{11,10},{12... | collective-permute-start | bytes 1671176 | tf_op jit(solution)/shard_map/ppermute | solution.py:400
  34.0 15.3 %collective-permute-start.6 = (bf16[2176,128]{1,0:T(8,128)(2,1)}, bf16[2176,128]{1,0:T(8,128)(2,1)S(1)}, u32[]{:S(2)}, u32[]{:S(2)}) collective-permute-start(bf16[2176,128]{1,0:T(8,128)(2,1)} %get-tuple-element.31.after), channel_id=1, source_target_pairs={{0,1},{1,2},{2,3},{3,4},{4,5},{5,6},{6,7},{8,9},{9,10},{10,11},{11... | collective-permute-start | bytes 1671176 | tf_op jit(solution)/shard_map/ppermute | solution.py:400
  38.0 8.5 %collective-permute-start.4 = (bf16[576,128]{1,0:T(8,128)(2,1)S(1)}, bf16[576,128]{1,0:T(8,128)(2,1)S(1)}, u32[]{:S(2)}, u32[]{:S(2)}) collective-permute-start(bf16[576,128]{1,0:T(8,128)(2,1)S(1)} %pad_maximum_fusion.1), channel_id=1, source_target_pairs={{0,64},{8,72},{16,80},{24,88},{32,96},{40,104},{48,112},{56,120},{... | collective-permute-start | bytes 442376 | tf_op jit(solution)/shard_map/ppermute | solution.py:447
  46.5 8.9 %collective-permute-start.5 = (bf16[1152,128]{1,0:T(8,128)(2,1)S(1)}, bf16[1152,128]{1,0:T(8,128)(2,1)S(1)}, u32[]{:S(2)}, u32[]{:S(2)}) collective-permute-start(bf16[1152,128]{1,0:T(8,128)(2,1)S(1)} %pad_maximum_fusion.y), channel_id=1, source_target_pairs={{0,128},{8,136},{16,144},{24,152},{32,160},{40,168},{48,176},{56,1... | collective-permute-start | bytes 884744 | tf_op jit(solution)/shard_map/ppermute | solution.py:447
  49.3 11.2 %copy-start.7 = (bf16[1024,128]{1,0:T(8,128)(2,1)S(1)}, bf16[1024,128]{1,0:T(8,128)(2,1)}, u32[]{:S(2)}) copy-start(bf16[1024,128]{1,0:T(8,128)(2,1)} %get-tuple-element.27.cown) | copy-start | bytes 786436
  49.3 11.2 %copy-start.12 = (bf16[128,128]{1,0:T(8,128)(2,1)S(1)}, bf16[128,128]{1,0:T(8,128)(2,1)}, u32[]{:S(2)}) copy-start(bf16[128,128]{1,0:T(8,128)(2,1)} %get-tuple-element.28.nown) | copy-start | bytes 98308
  55.5 10.1 %collective-permute-start.8 = (bf16[2304,128]{1,0:T(8,128)(2,1)S(1)}, bf16[2304,128]{1,0:T(8,128)(2,1)S(1)}, u32[]{:S(2)}, u32[]{:S(2)}) collective-permute-start(bf16[2304,128]{1,0:T(8,128)(2,1)S(1)} %table_join.1.own), channel_id=1, source_target_pairs={{0,8},{8,0},{16,24},{24,16},{32,40},{40,32},{48,56},{56,48},{64,72... | collective-permute-start | bytes 1769480 | tf_op jit(solution)/shard_map/ppermute | solution.py:447
  60.5 5.1 %copy-start.2 = (bf16[2048,128]{1,0:T(8,128)(2,1)S(1)}, bf16[2048,128]{1,0:T(8,128)(2,1)}, u32[]{:S(2)}) copy-start(bf16[2048,128]{1,0:T(8,128)(2,1)} %get-tuple-element.36.tl) | copy-start | bytes 1572868
  60.5 5.1 %copy-start.8 = (bf16[32,4096]{1,0:T(8,128)(2,1)S(1)}, bf16[32,4096]{1,0:T(8,128)(2,1)}, u32[]{:S(2)}) copy-start(bf16[32,4096]{1,0:T(8,128)(2,1)} %b.1) | copy-start | bytes 786436
  60.5 5.1 %copy-start.11 = (bf16[32,32,8]{1,2,0:T(8,128)(2,1)S(1)}, bf16[32,32,8]{1,2,0:T(8,128)(2,1)}, u32[]{:S(2)}) copy-start(bf16[32,32,8]{1,2,0:T(8,128)(2,1)} %param.20) | copy-start | bytes 49156
  60.5 5.1 %copy-start.15 = (bf16[32,32,1]{1,0,2:T(8,128)(2,1)S(1)}, bf16[32,32,1]{1,0,2:T(8,128)(2,1)}, u32[]{:S(2)}) copy-start(bf16[32,32,1]{1,0,2:T(8,128)(2,1)} %param.21) | copy-start | bytes 6148
  60.5 5.1 %copy-start.17 = (s32[16,1]{0,1:T(1,128)S(1)}, s32[16,1]{0,1:T(1,128)}, u32[]{:S(2)}) copy-start(s32[16,1]{0,1:T(1,128)} %param.26) | copy-start | bytes 196
  60.6 5.1 %copy-start.18 = (s32[8,1]{0,1:T(1,128)S(1)}, s32[8,1]{0,1:T(1,128)}, u32[]{:S(2)}) copy-start(s32[8,1]{0,1:T(1,128)} %param.28) | copy-start | bytes 100
where the time goes:
time: 68.6 us; the launch traced here: 68.3 us
  starting transfers between devices  33 us (48%)
  Pallas kernels  27.5 us (40%)
  waiting for transfers between devices  5.47 us (8%)
  local copies, waits for them, and re-layouts  1.92 us (3%)
    ppermute x5, starting transfers between devices, body(): lax.ppermute(x, 'coarse', [(i, i ^ bit) for i in range(coarse)])  12.9 us
    ppermute x4, starting transfers between devices, shift(): return lax.ppermute(x, axis, pairs)  11.7 us
    all_to_all x1, starting transfers between devices, body(): r = lax.all_to_all(pay, 'leaf', 0, 0, tiled=True)  8.31 us
    pallas_call x1, Pallas kernels, body(): pl.pallas_call(prep_kernel, out_shape=[shape((2048, 512)), shape((256, 51...  7.05 us
    pallas_call x1, Pallas kernels, body(): pl.pallas_call(near_kernel, out_shape=shape((64, 4096), F32), in_specs=[A...  6.16 us
    pallas_call x1, Pallas kernels, body(): pl.pallas_call(far_kernel, out_shape=[shape((2048, 128), F32), shape((256...  5 us
    pallas_call x1, Pallas kernels, body(): pl.pallas_call(up_kernel, out_shape=[shape((8, 32, 128)), shape((1024, 12...  4.12 us
    all_to_all x1, waiting for transfers between devices, body(): r = lax.all_to_all(pay, 'leaf', 0, 0, tiled=True)  3.94 us
  transfers between devices with their start and end apart: 10, of which 2 were waited for; matrix products, arithmetic and copies ran while one was open for 0% of the time, Pallas kernels for 30%

commit v1 on v0

--- a/solution.py
+++ b/solution.py
@@ -48,12 +48,14 @@
 
 
 def up_kernel(
-    v_hbm, b_hbm, lt_hbm, nt_hbm, dt_hbm, pay, cown, nown, up, dn, tl, fup, fdn,
-    ct, tls, ncs, lt, v, b, nt, dt, sems,
+    v_hbm, b_hbm, lt_hbm, nt_hbm, dt_hbm, near_hbm, leaf_hbm, node_hbm,
+    pay, cown, nown, ma, mb, tl, faces, near_ix, leaf_ix, node_ix,
+    ct, tls, ncs, lt, v, b, nt, dt, near_in, leaf_in, node_in, sems,
 ):
     loads = copies(
         [
             (lt_hbm, lt), (v_hbm, v), (b_hbm, b), (nt_hbm, nt), (dt_hbm, dt),
+            (near_hbm, near_in), (leaf_hbm, leaf_in), (node_hbm, node_in),
         ],
         sems,
     )
@@ -66,6 +68,19 @@
     tl[...] = tls[...].astype(BF)
     for c in loads[1:]:
         c.wait()
+    cp, lp = lax.axis_index("coarse"), lax.axis_index("leaf")
+    num = near_in[...]
+    px, py, pz = node_parts(num >> 3)
+    lx = 2 * px + ((num >> 2) & 1) - 4 * cp + 1
+    ly = 2 * py + ((num >> 1) & 1) - 4 * lp + 1
+    near_ix[...] = jnp.clip((lx * 6 + ly) * 4 + 2 * pz + (num & 1), 0, 143)
+    num = leaf_in[...]
+    px, py, pz = node_parts(num >> 3)
+    at = ((px - 2 * cp + 1) * 4 + (py - 2 * lp + 1)) * 2 + pz
+    leaf_ix[...] = jnp.clip(at * 8 + (num & 7), 0, 255)
+    px, py, pz = node_parts(node_in[...])
+    at = ((px - 2 * cp + 2) * 6 + (py - 2 * lp + 2)) * 2 + pz
+    node_ix[...] = jnp.clip(at, 0, 71)
     mask = diagonal_mask()
     for g in range(16):
         lanes = slice(g * 256, (g + 1) * 256)
@@ -90,43 +105,39 @@
     message = jnp.where(low_lanes(32), dc, terms).astype(BF)
     for z in range(8):
         pay[z] = message
+    for out, side in ((ma, 1 - (cp & 1)), (mb, cp & 1)):
+        for j in range(2):
+            for k in range(2):
+                for bb in range(2):
+                    at = ((2 * j + k) * 2 + bb) * 64
+                    first = ((2 * j + k) * 8 + 2 * bb) * 64 + side * 2304
+                    out[at:at + 64, :] = v[:, pl.ds(pl.multiple_of(first, 128), 128)]
+        out[V1:V1 + C1, :] = cown[pl.ds(pl.multiple_of(side * 512, 512), 512), :]
+        out[V1 + C1:, :] = nown[...]
     for j in range(2):
-        for k in range(2):
-            for bb in range(2):
-                at = ((2 * j + k) * 2 + bb) * 64
-                first = ((2 * j + k) * 8 + 2 * bb) * 64
-                dn[at:at + 64, :] = v[:, first:first + 128]
-                first += 36 * 64
-                up[at:at + 64, :] = v[:, first:first + 128]
-    for i in range(2):
-        for a in range(2):
-            for k in range(2):
-                at = ((i * 2 + a) * 2 + k) * 64
-                first = ((i * 4 + k) * 8 + 4 * a) * 64
-                fdn[at:at + 64, :] = v[:, first:first + 128]
-                first += 18 * 64
-                fup[at:at + 64, :] = v[:, first:first + 128]
-    dn[V1:V1 + C1, :] = cown[0:512, :]
-    up[V1:V1 + C1, :] = cown[512:1024, :]
-    dn[V1 + C1:, :] = nown[...]
-    up[V1 + C1:, :] = nown[...]
-
-
-def pack_kernel(fup, fdn, cown, nown, bef, aft, up, dn, sems):
-    moves = []
-    for out, face, j in ((up, fup, 1), (dn, fdn, 0)):
-        rows = [(face, 0, 512)]
-        for side in (bef, aft):
-            rows += [(side, ((2 * j + k) * 2 + j) * 64, 64) for k in range(2)]
+        for i in range(2):
+            for a in range(2):
+                for k in range(2):
+                    at = j * 512 + ((i * 2 + a) * 2 + k) * 64
+                    first = ((i * 4 + k) * 8 + 4 * a + 18 * j) * 64
+                    faces[at:at + 64, :] = v[:, first:first + 128]
+
+
+def pack_kernel(faces, cown, nown, ra, rb, qa, qb):
+    lp = lax.axis_index("leaf")
+    for out, j in ((qa, 1 - (lp & 1)), (qb, lp & 1)):
+        rows = [(faces, j * 512, 512)]
+        for side in (ra, rb):
+            rows += [(side, (5 * j + 2 * k) * 64, 64) for k in range(2)]
         rows += [(cown, (i * 2 + j) * 256, 256) for i in range(2)]
-        rows += [(side, V1 + j * 256, 256) for side in (bef, aft)]
-        rows += [(nown, 0, 128), (bef, V1 + C1, 128), (aft, V1 + C1, 128)]
+        rows += [(side, V1 + j * 256, 256) for side in (ra, rb)]
+        rows += [(nown, 0, 128), (ra, V1 + C1, 128), (rb, V1 + C1, 128)]
         at = 0
         for side, first, count in rows:
-            moves.append((side.at[pl.ds(first, count)], out.at[pl.ds(at, count)]))
+            if not isinstance(first, int):
+                first = pl.multiple_of(first, 64)
+            out[at:at + count, :] = side[pl.ds(first, count), :]
             at += count
-    for c in copies(moves, sems):
-        c.wait()
 
 
 def group_kernel(r, after, y):
@@ -140,39 +151,38 @@
     y[128:144, :] = jnp.where(low_lanes(16), swapped[0:16], total[16:32]).astype(BF)
 
 
-def prep_kernel(
-    near_in, leaf_in, node_in, s_hbm, sn_hbm, sd_hbm, sg_hbm,
-    zl, zn, zd, zg, near_ix, leaf_ix, node_ix, zs, ns, s, sn, sd, sg, sems,
-):
+def transpose_half(base, s_hbm, zl, zs, s, sems):
     loads = copies(
-        [(s_hbm.at[:, pl.ds(8 * q, 8)], s.at[:, pl.ds(8 * q, 8)]) for q in range(4)]
-        + [(sn_hbm, sn), (sd_hbm, sd), (sg_hbm, sg)],
+        [
+            (s_hbm.at[pl.ds(base, 8), pl.ds(8 * q, 8)], s.at[:, pl.ds(8 * q, 8)])
+            for q in range(4)
+        ],
         sems,
     )
-    cp, lp = lax.axis_index("coarse"), lax.axis_index("leaf")
-    num = near_in[...]
-    px, py, pz = node_parts(num >> 3)
-    lx = 2 * px + ((num >> 2) & 1) - 4 * cp + 1
-    ly = 2 * py + ((num >> 1) & 1) - 4 * lp + 1
-    near_ix[...] = jnp.clip((lx * 6 + ly) * 4 + 2 * pz + (num & 1), 0, 143)
-    num = leaf_in[...]
-    px, py, pz = node_parts(num >> 3)
-    at = ((px - 2 * cp + 1) * 4 + (py - 2 * lp + 1)) * 2 + pz
-    leaf_ix[...] = jnp.clip(at * 8 + (num & 7), 0, 255)
-    px, py, pz = node_parts(node_in[...])
-    at = ((px - 2 * cp + 2) * 6 + (py - 2 * lp + 2)) * 2 + pz
-    node_ix[...] = jnp.clip(at, 0, 71)
     ident = eye(64)
     for j in range(32):
         if j % 8 == 0:
             loads[j // 8].wait()
-        t = dot(ident, s[:, j].reshape(512, 64), 1, 1)
-        for q in range(4):
+        x = s[:, j].reshape(256, 64)
+        t = dot(ident, x, 1, 1) if j % 2 else x.T.astype(F32)
+        for q in range(2):
             zs[q, pl.ds(j, 64, stride=32), :] = t[:, q * 128:(q + 1) * 128]
-    for c in loads[4:]:
+    for q in range(2):
+        zl[:, q * 128:(q + 1) * 128] = zs[q].astype(BF)
+
+
+def first_layout_kernel(s_hbm, zl, zs, s, sems):
+    transpose_half(0, s_hbm, zl, zs, s, sems)
+
+
+def second_layout_kernel(
+    s_hbm, sn_hbm, sd_hbm, sg_hbm, zl, zn, zd, zg, zs, s, ns, sn, sd, sg, sems, more
+):
+    loads = copies([(sn_hbm, sn), (sd_hbm, sd), (sg_hbm, sg)], more)
+    transpose_half(8, s_hbm, zl, zs, s, sems)
+    for c in loads:
         c.wait()
     for q in range(4):
-        zl[:, q * 128:(q + 1) * 128] = zs[q].astype(BF)
         parts = [sn[4 * q + i].astype(F32).reshape(256, 32) for i in range(4)]
         ns[...] = jnp.concatenate(parts, axis=1)
         for n in range(8):
@@ -184,13 +194,14 @@
         zg[:, q * 128:(q + 1) * 128] = jnp.concatenate(parts, axis=1).astype(BF)
 
 
-def near_kernel(ix_any, v, bef, aft, lb, la, blocks_hbm, out, low, high, picked, ix, blocks, sems):
+def near_kernel(ix_any, v, ra, rb, qa, qb, blocks_hbm, out, low, high, picked, ix, blocks, sems):
     loads = copies(
         [(ix_any, ix)]
         + [(blocks_hbm.at[:, pl.ds(512 * t, 512)], blocks.at[t]) for t in range(8)],
         sems,
     )
     mask = low_lanes(64)
+    odd_c, odd_l = lax.axis_index("coarse") & 1, lax.axis_index("leaf") & 1
 
     def table():
         def put(wx, wy, k, x):
@@ -209,19 +220,19 @@
                         for bb in range(2):
                             first = (((i * 2 + j) * 2 + k) * 8 + 4 * a + 2 * bb) * 64
                             put(1 + 2 * i + a, 1 + 2 * j + bb, k, v[:, first:first + 128])
-        for side, wx in ((bef, 0), (aft, 5)):
+        for side, wx in ((ra, 5 - 5 * odd_c), (rb, 5 * odd_c)):
             for j in range(2):
                 for k in range(2):
                     for bb in range(2):
                         first = ((2 * j + k) * 2 + bb) * 64
                         put(wx, 1 + 2 * j + bb, k, side[first:first + 64, :])
-        for side, wy in ((lb, 0), (la, 5)):
+        for side, wy in ((qa, 5 - 5 * odd_l), (qb, 5 * odd_l)):
             for i in range(2):
                 for a in range(2):
                     for k in range(2):
                         first = ((i * 2 + a) * 2 + k) * 64
                         put(1 + 2 * i + a, wy, k, side[first:first + 64, :])
-            for wx, base in ((0, 8), (5, 10)):
+            for wx, base in ((5 - 5 * odd_c, 8), (5 * odd_c, 10)):
                 for k in range(2):
                     first = (base + k) * 64
                     put(wx, wy, k, side[first:first + 64, :])
@@ -249,16 +260,20 @@
 
 
 def far_kernel(
-    li_any, mi_any, cown, nown, bef, aft, lb, la, zl, zn, far, nfar, cw, nw, li, mi, sems
+    li_any, mi_any, cown, nown, ra, rb, qa, qb, za, zb, zn, far, nfar, low, high, nw, li, mi, sems
 ):
     loads = copies([(li_any, li), (mi_any, mi)], sems)
+    mask = low_lanes(32)
 
     def put_leaves(nwx, nwy, k, side, first):
         for p in range(4):
-            x = side[first + p * 32:first + (p + 1) * 32, :]
+            x = side[first + p * 32:first + (p + 1) * 32, :].astype(F32)
             at = ((nwx * 4 + nwy) * 2 + k) * 8 + 2 * p
-            cw[at] = x
-            cw[at + 1] = pltpu.roll(x.astype(F32), 64, 1).astype(BF)
+            swapped = pltpu.roll(x, 64, 1)
+            low[at] = jnp.where(mask, x, 0.0).astype(BF)
+            high[at] = jnp.where(mask, 0.0, swapped).astype(BF)
+            low[at + 1] = jnp.where(mask, swapped, 0.0).astype(BF)
+            high[at + 1] = jnp.where(mask, 0.0, x).astype(BF)
 
     def put_nodes(nwx, nwy, side, first):
         x = side[first:first + 32, :]
@@ -266,28 +281,30 @@
         nw[at] = x
         nw[at + 1] = pltpu.roll(x.astype(F32), 64, 1).astype(BF)
 
+    odd_c, odd_l = lax.axis_index("coarse") & 1, lax.axis_index("leaf") & 1
+    in_x, in_y = ((ra, 1 - odd_c), (rb, odd_c)), ((qa, 1 - odd_l), (qb, odd_l))
     for i in range(2):
         for j in range(2):
             put_nodes(2 + i, 2 + j, nown, (i * 2 + j) * 32)
-            put_nodes(i, 2 + j, bef, V1 + C1 + (i * 2 + j) * 32)
-            put_nodes(4 + i, 2 + j, aft, V1 + C1 + (i * 2 + j) * 32)
-            for side, base in ((lb, 0), (la, 4)):
+            for side, after in in_x:
+                put_nodes(4 * after + i, 2 + j, side, V1 + C1 + (i * 2 + j) * 32)
+            for side, after in in_y:
                 first = V2 + C2 + (i * 2 + j) * 32
-                put_nodes(2 + i, base + j, side, first)
-                put_nodes(i, base + j, side, first + 128)
-                put_nodes(4 + i, base + j, side, first + 256)
+                put_nodes(2 + i, 4 * after + j, side, first)
+                put_nodes(4 - 4 * odd_c + i, 4 * after + j, side, first + 128)
+                put_nodes(4 * odd_c + i, 4 * after + j, side, first + 256)
             for k in range(2):
                 put_leaves(1 + i, 1 + j, k, cown, ((i * 2 + j) * 2 + k) * 128)
     for j in range(2):
         for k in range(2):
-            put_leaves(0, 1 + j, k, bef, V1 + (2 * j + k) * 128)
-            put_leaves(3, 1 + j, k, aft, V1 + (2 * j + k) * 128)
-    for side, nwy in ((lb, 0), (la, 3)):
+            for side, after in in_x:
+                put_leaves(3 * after, 1 + j, k, side, V1 + (2 * j + k) * 128)
+    for side, after in in_y:
         for k in range(2):
             for i in range(2):
-                put_leaves(1 + i, nwy, k, side, V2 + (2 * i + k) * 128)
-            put_leaves(0, nwy, k, side, V2 + 512 + k * 128)
-            put_leaves(3, nwy, k, side, V2 + 768 + k * 128)
+                put_leaves(1 + i, 3 * after, k, side, V2 + (2 * i + k) * 128)
+            put_leaves(3 - 3 * odd_c, 3 * after, k, side, V2 + 512 + k * 128)
+            put_leaves(3 * odd_c, 3 * after, k, side, V2 + 768 + k * 128)
 
     for c in loads:
         c.wait()
@@ -297,13 +314,17 @@
 
     def leaves(t, carry):
         for u in range(4):
-            n = t * 4 + u
-            block = jnp.concatenate([cw[li[s, n]] for s in range(16)], axis=0)
-            rows = pl.ds(pl.multiple_of(n * 32, 32), 32)
-            far[rows, :] = dot(zl[rows, :], block, 1, 0)
+            n = t * 8 + 2 * u
+            block = jnp.concatenate(
+                [low[li[s, n]] + high[li[s, n + 1]] for s in range(16)], axis=0
+            )
+            rows = pl.ds(pl.multiple_of(n * 32, 64), 64)
+            r = dot(za[rows, :], block[:256], 1, 0) + dot(zb[rows, :], block[256:], 1, 0)
+            far[pl.ds(pl.multiple_of(n * 32, 32), 32), :] = r[:32]
+            far[pl.ds(pl.multiple_of(n * 32 + 32, 32), 32), :] = pltpu.roll(r[32:], 64, 1)
         return carry
 
-    lax.fori_loop(0, 16, leaves, 0)
+    lax.fori_loop(0, 8, leaves, 0)
 
 
 def table_kernel(y, received, after, own):
@@ -372,82 +393,104 @@
 ):
     nt = jnp.transpose(node_transfer, (0, 2, 1)).reshape(256, 32)
     dt = device_transfer.reshape(32, 32)
-    pay, cown, nown, up, dn, tl, fup, fdn = pl.pallas_call(
+    pay, cown, nown, ma, mb, tl, faces, near_ix, leaf_ix, node_ix = pl.pallas_call(
         up_kernel,
         out_shape=[
             shape((8, 32, 128)), shape((1024, 128)), shape((128, 128)),
             shape((ROWS1, 128)), shape((ROWS1, 128)), shape((2048, 128)),
-            shape((512, 128)), shape((512, 128)),
-        ],
-        in_specs=[HB] * 5,
-        out_specs=[VM] * 8,
+            shape((1024, 128)),
+            shape((12, 64), jnp.int32), shape((16, 64), jnp.int32), shape((8, 16), jnp.int32),
+        ],
+        in_specs=[HB] * 8,
+        out_specs=[VM] * 10,
         scratch_shapes=[
             pltpu.VMEM((2048, 64), BF), pltpu.VMEM((2048, 128), F32), pltpu.VMEM((256, 128), F32),
             pltpu.VMEM((32, 32, 64), BF), pltpu.VMEM((64, 4096), BF), pltpu.VMEM((32, 4096), BF),
-            pltpu.VMEM((256, 32), BF), pltpu.VMEM((32, 32), BF), pltpu.SemaphoreType.DMA((5,)),
+            pltpu.VMEM((256, 32), BF), pltpu.VMEM((32, 32), BF), pltpu.VMEM((12, 64), jnp.int32),
+            pltpu.VMEM((16, 64), jnp.int32), pltpu.VMEM((8, 16), jnp.int32),
+            pltpu.SemaphoreType.DMA((8,)),
         ],
         compiler_params=params(58),
-        cost_estimate=cost(10**9, 4 * 10**6),
+        cost_estimate=cost(10**6, 10**5),
         name="up_pass",
-    )(vectors, leaf_basis, leaf_transfer, nt, dt)
+    )(vectors, leaf_basis, leaf_transfer, nt, dt, near_index, leaf_lists, node_lists.T)
 
     coarse, leafs = lax.axis_size("coarse"), lax.axis_size("leaf")
     r = lax.all_to_all(pay, "leaf", 0, 0, tiled=True)
 
-    def shift(x, axis, step):
+    def swap(x, axis, first):
         size = lax.axis_size(axis)
-        pairs = [(i, i + step) for i in range(size) if 0 <= i + step < size]
-        return lax.ppermute(x, axis, pairs)
-
-    bef, aft = shift(up, "coarse", 1), shift(dn, "coarse", -1)
-
-    zl, zn, zd, zg, near_ix, leaf_ix, node_ix = pl.pallas_call(
-        prep_kernel,
-        out_shape=[
-            shape((2048, 512)), shape((256, 512)), shape((32, 512)), shape((32, 256)),
-            shape((12, 64), jnp.int32), shape((16, 64), jnp.int32), shape((8, 16), jnp.int32),
-        ],
-        in_specs=[VM] * 3 + [HB] * 4,
-        out_specs=[VM] * 7,
-        scratch_shapes=[
-            pltpu.VMEM((4, 2048, 128), F32), pltpu.VMEM((256, 128), F32),
-            pltpu.VMEM((16, 32, 32, 64), BF), pltpu.VMEM((16, 32, 8, 32), BF),
+        pairs = [(i, i + 1) for i in range(first, size - 1, 2)]
+        return lax.ppermute(x, axis, pairs + [(j, i) for i, j in pairs])
+
+    ra, rb = swap(ma, "coarse", 0), swap(mb, "coarse", 1)
+
+    half = [pltpu.VMEM((2, 2048, 128), F32), pltpu.VMEM((8, 32, 32, 64), BF)]
+    za = pl.pallas_call(
+        first_layout_kernel,
+        out_shape=shape((2048, 256)),
+        in_specs=[HB],
+        out_specs=VM,
+        scratch_shapes=half + [pltpu.SemaphoreType.DMA((4,))],
+        compiler_params=params(50),
+        cost_estimate=cost(1000, 1000000),
+        name="first_layout",
+    )(leaf_coupling)
+    zb, zn, zd, zg = pl.pallas_call(
+        second_layout_kernel,
+        out_shape=[shape((2048, 256)), shape((256, 512)), shape((32, 512)), shape((32, 256))],
+        in_specs=[HB] * 4,
+        out_specs=[VM] * 4,
+        scratch_shapes=half + [
+            pltpu.VMEM((256, 128), F32), pltpu.VMEM((16, 32, 8, 32), BF),
             pltpu.VMEM((16, 32, 32), BF), pltpu.VMEM((8, 32, 32), BF),
-            pltpu.SemaphoreType.DMA((7,)),
-        ],
-        compiler_params=params(48),
-        cost_estimate=cost(10**9, 8 * 10**6),
-        name="coupling_layout",
+            pltpu.SemaphoreType.DMA((4,)), pltpu.SemaphoreType.DMA((3,)),
+        ],
+        compiler_params=params(50),
+        cost_estimate=cost(1000, 1000000),
+        name="second_layout",
     )(
-        near_index, leaf_lists, node_lists.T, leaf_coupling, jnp.transpose(node_coupling, (0, 1, 3, 2)),
+        leaf_coupling, jnp.transpose(node_coupling, (0, 1, 3, 2)),
         device_coupling.reshape(16, 32, 32), group_coupling.reshape(8, 32, 32),
     )
 
-    up2, dn2 = pl.pallas_call(
+    sa, sb = pl.pallas_call(
         pack_kernel,
         out_shape=[shape((ROWS2, 128))] * 2,
-        in_specs=[HB] * 6,
+        in_specs=[VM] * 5,
         out_specs=[VM] * 2,
-        scratch_shapes=[pltpu.SemaphoreType.DMA((24,))],
-        compiler_params=params(58),
-        cost_estimate=cost(1000, 10**6),
+        compiler_params=params(8),
+        cost_estimate=cost(1000, 10000000),
         name="halo_pack",
-    )(fup, fdn, cown, nown, bef, aft)
-    lb, la = shift(up2, "leaf", 1), shift(dn2, "leaf", -1)
+    )(faces, cown, nown, ra, rb)
+    qa, qb = swap(sa, "leaf", 0), swap(sb, "leaf", 1)
 
     y = pl.pallas_call(
         group_kernel,
         out_shape=shape((TAB, 128)),
-        in_specs=[VM, HB],
+        in_specs=[VM, AN],
         out_specs=VM,
         compiler_params=params(8),
         cost_estimate=cost(1000, 10**5),
         name="group_sum",
-    )(r, up2)
+    )(r, za)
     flip = lambda x, bit: lax.ppermute(x, "coarse", [(i, i ^ bit) for i in range(coarse)])
-    for bit in (2, 4, 8):
-        y = jnp.concatenate([y, flip(y, bit)], axis=0)
-    received = flip(y, 16)
+
+    def join(first, second, after):
+        return pl.pallas_call(
+            table_kernel,
+            out_shape=shape((2 * first.shape[0], 128)),
+            in_specs=[VM, VM, AN],
+            out_specs=VM,
+            compiler_params=params(8),
+            cost_estimate=cost(1000, 10**5),
+            name="table_join",
+        )(first, second, after)
+
+
+    y = join(y, flip(y, 2), sa)
+    y = jnp.concatenate([y, flip(y, 4)], axis=0)
+    received = flip(y, 8)
 
     near = pl.pallas_call(
         near_kernel,
@@ -460,35 +503,31 @@
             pltpu.VMEM((8, 768, 512), BF), pltpu.SemaphoreType.DMA((9,)),
         ],
         compiler_params=params(48),
-        cost_estimate=cost(4 * 10**9, 16 * 10**6),
+        cost_estimate=cost(1000, 1000000),
         name="near_field",
-    )(near_ix, vectors, bef, aft, lb, la, near_blocks.reshape(768, 4096))
-
-    own = pl.pallas_call(
-        table_kernel,
-        out_shape=shape((16 * TAB, 128)),
-        in_specs=[VM, VM, AN],
-        out_specs=VM,
-        compiler_params=params(8),
-        cost_estimate=cost(1000, 10**6),
-        name="table_join",
-    )(y, received, near)
-    other = flip(own, 1)
+    )(near_ix, vectors, ra, rb, qa, qb, near_blocks.reshape(768, 4096))
+
+
+    y = join(y, received, zn)
+    received = flip(y, 16)
 
     far, nfar = pl.pallas_call(
         far_kernel,
         out_shape=[shape((2048, 128), F32), shape((256, 128), F32)],
-        in_specs=[AN] * 2 + [VM] * 8,
+        in_specs=[AN] * 2 + [VM] * 9,
         out_specs=[VM] * 2,
         scratch_shapes=[
-            pltpu.VMEM((256, 32, 128), BF), pltpu.VMEM((72, 32, 128), BF),
-            pltpu.SMEM((16, 64), jnp.int32), pltpu.SMEM((8, 16), jnp.int32),
+            pltpu.VMEM((256, 32, 128), BF), pltpu.VMEM((256, 32, 128), BF),
+            pltpu.VMEM((72, 32, 128), BF), pltpu.SMEM((16, 64), jnp.int32), pltpu.SMEM((8, 16), jnp.int32),
             pltpu.SemaphoreType.DMA((2,)),
         ],
         compiler_params=params(32),
-        cost_estimate=cost(4 * 10**9, 16 * 10**6),
+        cost_estimate=cost(1000, 1000000),
         name="far_field",
-    )(leaf_ix, node_ix, cown, nown, bef, aft, lb, la, zl, zn)
+    )(leaf_ix, node_ix, cown, nown, ra, rb, qa, qb, za, zb, zn)
+
+    own = join(y, received, near)
+    other = flip(own, 1)
 
     return pl.pallas_call(
         down_kernel,
@@ -497,7 +536,7 @@
         out_specs=VM,
         scratch_shapes=[pltpu.VMEM((256, 128), F32)],
         compiler_params=params(32),
-        cost_estimate=cost(10**9, 4 * 10**6),
+        cost_estimate=cost(10**6, 10**5),
         name="down_pass",
     )(
         device_lists.reshape(1, 16), group_lists.reshape(1, 8), own, other, zd, zg, dt, nt, tl,

time: 68.6 us -> 63.2 us (0.921)
  starting transfers between devices: 33 us -> 27.8 us
  Pallas kernels: 27.5 us -> 25.8 us
  local copies, waits for them, and re-layouts: 1.92 us -> 3.51 us
    ppermute x4, starting transfers between devices: 11.7 us -> 6.44 us  [swap(): return lax.ppermute(x, axis, pairs + [(j, i) for i, j in pairs])]
    pallas_call x1, Pallas kernels: 2.46 us -> 0.07 us  [body(): pl.pallas_call(pack_kernel, out_shape=[shape((ROWS2, 128))] * 2, in_specs...]
    unnamed x40 -> x34, local copies, waits for them, and re-layouts: 1.92 us -> 3.51 us
    ppermute x5, starting transfers between devices: 12.9 us -> 13.8 us  [body(): lax.ppermute(x, 'coarse', [(i, i ^ bit) for i in range(coarse)])]
    all_to_all x1, starting transfers between devices: 8.31 us -> 7.57 us  [body(): r = lax.all_to_all(pay, 'leaf', 0, 0, tiled=True)]
    pallas_call x3 -> x6, Pallas kernels: 7.17 us -> 7.6 us  [the longest x1 4.05 us: body(): pl.pallas_call(second_layout_kernel, out_shape=[shape((2048, 256)), shape...]
where the time goes in v1:
time: 63.2 us; the launch traced here: 62.8 us
  starting transfers between devices  27.8 us (44%)
  Pallas kernels  25.8 us (41%)
  waiting for transfers between devices  5.37 us (8%)
  local copies, waits for them, and re-layouts  3.51 us (6%)
    ppermute x5, starting transfers between devices, body(): lax.ppermute(x, 'coarse', [(i, i ^ bit) for i in range(coarse)])  13.8 us
    all_to_all x1, starting transfers between devices, body(): r = lax.all_to_all(pay, 'leaf', 0, 0, tiled=True)  7.57 us
    ppermute x4, starting transfers between devices, swap(): return lax.ppermute(x, axis, pairs + [(j, i) for i, j in pairs])  6.44 us
    pallas_call x1, Pallas kernels, body(): pl.pallas_call(near_kernel, out_shape=shape((64, 4096), F32), in_specs=[A...  6.14 us
    pallas_call x1, Pallas kernels, body(): pl.pallas_call(far_kernel, out_shape=[shape((2048, 128), F32), shape((256...  5.09 us
    pallas_call x1, Pallas kernels, body(): pl.pallas_call(up_kernel, out_shape=[shape((8, 32, 128)), shape((1024, 12...  4.26 us
    pallas_call x1, Pallas kernels, body(): pl.pallas_call(second_layout_kernel, out_shape=[shape((2048, 256)), shape...  4.05 us
    all_to_all x1, waiting for transfers between devices, body(): r = lax.all_to_all(pay, 'leaf', 0, 0, tiled=True)  3.81 us
  transfers between devices with their start and end apart: 10, of which 2 were waited for; matrix products, arithmetic and copies ran while one was open for 0% of the time, Pallas kernels for 30%

profile of v1, /device:TPU:1, one launch (start us, length us, event | category | flops | bytes accessed | tf_op | source)
XLA Modules:
  0.0 62.8 jit_solution(7620979317619162725)
XLA Ops:
  0.0 0.0 copy-start.2
  0.0 4.3 %up_pass.1 = (bf16[8,32,128]{2,1,0:T(8,128)(2,1)}, bf16[1024,128]{1,0:T(8,128)(2,1)}, bf16[128,128]{1,0:T(8,128)(2,1)}, bf16[1152,128]{1,0:T(8,128)(2,1)}, bf16[...) custom-call(bf16[64,4096]{1,0:T(8,128)(2,1)} %v.1, ...), custom_call_target="tpu_custom_call" | custom-call | flops 1000000 | bytes 100000 | tf_op jit(solution)/shard_map/up_pass/pallas_call | solution.py:396
  4.3 0.0 copy-start.1
  4.3 3.3 %collective-permute-start.1 = (bf16[1152,128]{1,0:T(8,128)(2,1)}, bf16[1152,128]{1,0:T(8,128)(2,1)S(1)}, u32[]{:S(2)}, u32[]{:S(2)}) collective-permute-start(bf16[1152,128]{1,0:T(8,128)(2,1)} %get-tuple-element.27), channel_id=1, source_target_pairs={{0,8},{16,24},{32,40},{48,56},{64,72},{80,88},{96,104},{112,120},{... | collective-permute-start | bytes 884744 | tf_op jit(solution)/shard_map/ppermute | solution.py:424
  7.6 1.9 %collective-permute-start.2 = (bf16[1152,128]{1,0:T(8,128)(2,1)}, bf16[1152,128]{1,0:T(8,128)(2,1)S(1)}, u32[]{:S(2)}, u32[]{:S(2)}) collective-permute-start(bf16[1152,128]{1,0:T(8,128)(2,1)} %get-tuple-element.28), channel_id=1, source_target_pairs={{8,16},{24,32},{40,48},{56,64},{72,80},{88,96},{104,112},{120,128}... | collective-permute-start | bytes 884744 | tf_op jit(solution)/shard_map/ppermute | solution.py:424
  9.5 7.6 %all-to-all-start = ((bf16[8,32,128]{2,1,0:T(8,128)(2,1)}), bf16[8,32,128]{2,1,0:T(8,128)(2,1)S(1)}, u32[]{:S(2)}, u32[]{:S(2)}) async-start(bf16[8,32,128]{2,1,0:T(8,128)(2,1)} %get-tuple-element.23), calls=%async_computation | async-start | bytes 131072 | tf_op jit(solution)/shard_map/all_to_all | solution.py:419
  17.1 0.0 copy-start
  17.1 0.0 copy-start.13
  17.1 3.4 %first_layout.1.after.za = bf16[2048,256]{1,0:T(8,128)(2,1)S(1)} custom-call(bf16[16,32,32,64]{3,2,1,0:T(8,128)(2,1)} %s_hbm.3), custom_call_target="tpu_custom_call" | custom-call | flops 1000 | bytes 1000000 | tf_op jit(solution)/shard_map/first_layout/pallas_call | solution.py:429
  20.5 3.8 %all-to-all-done.r = bf16[8,32,128]{2,1,0:T(8,128)(2,1)S(1)} async-done(((bf16[8,32,128]{2,1,0:T(8,128)(2,1)}), bf16[8,32,128]{2,1,0:T(8,128)(2,1)S(1)}, u32[]{:S(2)}, u32[]{:S(2)}) %all-to-all-start) | async-done | bytes 65568 | tf_op jit(solution)/shard_map/all_to_all | solution.py:419
  24.3 0.1 group_sum.1.y
  24.4 1.8 %collective-permute-start = (bf16[144,128]{1,0:T(8,128)(2,1)S(1)}, bf16[144,128]{1,0:T(8,128)(2,1)S(1)}, u32[]{:S(2)}, u32[]{:S(2)}) collective-permute-start(bf16[144,128]{1,0:T(8,128)(2,1)S(1)} %group_sum.1.y), channel_id=1, source_target_pairs={{0,16},{8,24},{16,0},{24,8},{32,48},{40,56},{48,32},{56,40},{64,80... | collective-permute-start | bytes 110600 | tf_op jit(solution)/shard_map/ppermute | solution.py:477
  26.2 0.0 collective-permute-done.1.ra
  26.3 0.0 collective-permute-done.2.rb
  26.3 0.0 copy-done.1
  26.3 0.0 copy-start.6
  26.3 0.9 %copy-done.6 = bf16[1024,128]{1,0:T(8,128)(2,1)S(1)} copy-done((bf16[1024,128]{1,0:T(8,128)(2,1)S(1)}, bf16[1024,128]{1,0:T(8,128)(2,1)}, u32[]{:S(2)}) %copy-start.6) | copy-done | bytes 262168
  27.2 0.0 copy-start.7
  27.2 0.8 %copy-done.7 = bf16[128,128]{1,0:T(8,128)(2,1)S(1)} copy-done((bf16[128,128]{1,0:T(8,128)(2,1)S(1)}, bf16[128,128]{1,0:T(8,128)(2,1)}, u32[]{:S(2)}) %copy-start.7) | copy-done | bytes 32792
  28.0 0.1 halo_pack.1
  28.0 0.0 collective-permute-done.received
  28.1 2.0 %collective-permute-start.3 = (bf16[288,128]{1,0:T(8,128)(2,1)S(1)}, bf16[288,128]{1,0:T(8,128)(2,1)S(1)}, u32[]{:S(2)}, u32[]{:S(2)}) collective-permute-start(bf16[288,128]{1,0:T(8,128)(2,1)S(1)} %table_join.3), channel_id=1, source_target_pairs={{0,32},{8,40},{16,48},{24,56},{32,0},{40,8},{48,16},{56,24},{64,96... | collective-permute-start | bytes 221192 | tf_op jit(solution)/shard_map/ppermute | solution.py:477
  30.1 0.5 collective-permute-start.6
  30.6 0.7 %collective-permute-start.7 = (bf16[2176,128]{1,0:T(8,128)(2,1)S(1)}, bf16[2176,128]{1,0:T(8,128)(2,1)S(1)}, u32[]{:S(2)}, u32[]{:S(2)}) collective-permute-start(bf16[2176,128]{1,0:T(8,128)(2,1)S(1)} %get-tuple-element.32), channel_id=1, source_target_pairs={{1,2},{3,4},{5,6},{2,1},{4,3},{6,5},{9,10},{11,12},{13,14},{10,9},... | collective-permute-start | bytes 1671176 | tf_op jit(solution)/shard_map/ppermute | solution.py:424
  31.3 1.5 %collective-permute-done.3 = bf16[288,128]{1,0:T(8,128)(2,1)S(1)} collective-permute-done((bf16[288,128]{1,0:T(8,128)(2,1)S(1)}, bf16[288,128]{1,0:T(8,128)(2,1)S(1)}, u32[]{:S(2)}, u32[]{:S(2)}) %collective-permute-start.3) | collective-permute-done | bytes 73760 | tf_op jit(solution)/shard_map/ppermute | solution.py:477
  32.9 1.3 %collective-permute-start.4 = (bf16[576,128]{1,0:T(8,128)(2,1)S(1)}, bf16[576,128]{1,0:T(8,128)(2,1)S(1)}, u32[]{:S(2)}, u32[]{:S(2)}) collective-permute-start(bf16[576,128]{1,0:T(8,128)(2,1)S(1)} %pad_maximum_fusion.y), channel_id=1, source_target_pairs={{0,64},{8,72},{16,80},{24,88},{32,96},{40,104},{48,112},{56,120},{... | collective-permute-start | bytes 442376 | tf_op jit(solution)/shard_map/ppermute | solution.py:477
  34.2 0.0 copy-done.2
  34.2 0.0 copy-start.9
  34.2 0.9 %copy-done.9 = bf16[16,32,32,1]{2,1,3,0:T(8,128)(2,1)S(1)} copy-done((bf16[16,32,32,1]{2,1,3,0:T(8,128)(2,1)S(1)}, bf16[16,32,32,1]{2,1,3,0:T(8,128)(2,1)}, u32[]{:S(2)}) %copy-start.9) | copy-done | bytes 32792
  35.1 0.0 copy-start.10
  35.1 0.8 %copy-done.10 = bf16[8,32,32,1]{2,1,3,0:T(8,128)(2,1)S(1)} copy-done((bf16[8,32,32,1]{2,1,3,0:T(8,128)(2,1)S(1)}, bf16[8,32,32,1]{2,1,3,0:T(8,128)(2,1)}, u32[]{:S(2)}) %copy-start.10) | copy-done | bytes 16408
  35.9 4.1 %second_layout.1 = (bf16[2048,256]{1,0:T(8,128)(2,1)S(1)}, bf16[256,512]{1,0:T(8,128)(2,1)S(1)}, bf16[32,512]{1,0:T(8,128)(2,1)S(1)}, bf16[32,256]{1,0:T(8,128)(2,1)S(1)}) custom-call(bf16[16,32,32,64]{3,2,1,0:T(8,128)(2,1)} %s_hbm.3, bf16[16,32,8,32]{3,2,1,0:T(8,128)(2,1)S(1)} %bitcast.11, bf16[16,32,32]{2,1,0:T(8,128)(2,1)S(1)} %bitcast.14, ...), custom_call_target="tpu_custom_call" | custom-call | flops 1000 | bytes 1000000 | tf_op jit(solution)/shard_map/second_layout/pallas_call | solution.py:439
  40.0 0.0 collective-permute-done.4.received
  40.0 0.0 copy-start.8
  40.0 0.0 copy-start.12
  40.0 0.0 copy-start.14
  40.0 2.7 %collective-permute-start.5 = (bf16[1152,128]{1,0:T(8,128)(2,1)S(1)}, bf16[1152,128]{1,0:T(8,128)(2,1)S(1)}, u32[]{:S(2)}, u32[]{:S(2)}) collective-permute-start(bf16[1152,128]{1,0:T(8,128)(2,1)S(1)} %table_join.4.y), channel_id=1, source_target_pairs={{0,128},{8,136},{16,144},{24,152},{32,160},{40,168},{48,176},{56,1... | collective-permute-start | bytes 884744 | tf_op jit(solution)/shard_map/ppermute | solution.py:477
  42.8 0.0 collective-permute-done.7.qb
  42.8 0.0 collective-permute-done.6.qa
  42.8 0.0 copy-done
  42.8 0.0 copy-done.13
  42.8 0.0 copy-start.3
  42.8 0.0 copy-start.4
  42.8 0.0 copy-start.5
  42.8 0.0 copy-start.11
  42.8 0.0 copy-start.15
  42.8 0.0 copy-start.16
  42.9 6.1 %near_field.1.after.near = f32[64,4096]{1,0:T(8,128)S(1)} custom-call(s32[12,64]{1,0:T(8,128)S(1)} %copy-done.13, bf16[64,4096]{1,0:T(8,128)(2,1)S(1)} %copy-done, bf16[1152,128]{1,0:T(8,128)(2,1)S(1)} %collective-permute-done.1.ra, bf16[1152,128]{1,0:T(8,128)(2,1)S(1)} %collective-permute-done.2.rb, bf16[2176,128]{1,0:T(8,128)(2,1)S(1)} %collective-permute-done.6.qa, ...), custom_call_target="tpu_custom_call" | custom-call | flops 1000 | bytes 1000000 | tf_op jit(solution)/shard_map/near_field/pallas_call | solution.py:495
  49.0 0.0 collective-permute-done.5.received
  49.1 6.0 %collective-permute-start.8 = (bf16[2304,128]{1,0:T(8,128)(2,1)S(1)}, bf16[2304,128]{1,0:T(8,128)(2,1)S(1)}, u32[]{:S(2)}, u32[]{:S(2)}) collective-permute-start(bf16[2304,128]{1,0:T(8,128)(2,1)S(1)} %table_join.5.own), channel_id=1, source_target_pairs={{0,8},{8,0},{16,24},{24,16},{32,40},{40,32},{48,56},{56,48},{64,72... | collective-permute-start | bytes 1769480 | tf_op jit(solution)/shard_map/ppermute | solution.py:477
  55.0 0.0 copy-done.8
  55.0 0.0 copy-done.12
  55.0 0.0 copy-done.14
  55.0 5.1 %far_field.1 = (f32[2048,128]{1,0:T(8,128)S(1)}, f32[256,128]{1,0:T(8,128)S(1)}) custom-call(s32[16,64]{1,0:T(8,128)S(1)} %copy-done.12, s32[8,16]{1,0:T(8,128)S(1)} %copy-done.14, bf16[1024,128]{1,0:T(8,128)(2,1)S(1)} %copy-done.1, bf16[128,128]{1,0:T(8,128)(2,1)S(1)} %copy-done.8, bf16[1152,128]{1,0:T(8,128)(2,1)S(1)} %collective-permute-done.1.ra, ...), custom_call_target="tpu_custom_call" | custom-call | flops 1000 | bytes 1000000 | tf_op jit(solution)/shard_map/far_field/pallas_call | solution.py:514
  60.1 0.0 collective-permute-done.8.other
  60.1 0.0 copy-done.3
  60.1 0.0 copy-done.4
  60.2 0.0 copy-done.5
  60.2 0.0 copy-done.11
  60.2 0.0 copy-done.15
  60.2 0.0 copy-done.16
  60.2 2.6 %down_pass.1 = bf16[64,4096]{1,0:T(8,128)(2,1)} custom-call(s32[1,16]{1,0:T(1,128)S(1)} %bitcast.18, s32[1,8]{1,0:T(1,128)S(1)} %bitcast.19, bf16[2304,128]{1,0:T(8,128)(2,1)S(1)} %table_join.5.own, bf16[2304,128]{1,0:T(8,128)(2,1)S(1)} %collective-permute-done.8.other, bf16[32,512]{1,0:T(8,128)(2,1)S(1)} %get-tuple-element.33.zd, ...), custom_call_target="tpu_custom_call" | custom-call | flops 1000000 | bytes 100000 | tf_op jit(solution)/shard_map/down_pass/pallas_call | solution.py:532
  (4 shorter events, 0.1 us)
Async XLA Ops:
  0.0 34.2 %copy-start.2 = (bf16[16,32,32,8]{2,3,1,0:T(8,128)(2,1)S(1)}, bf16[16,32,32,8]{2,3,1,0:T(8,128)(2,1)}, u32[]{:S(2)}) copy-start(bf16[16,32,32,8]{2,3,1,0:T(8,128)(2,1)} %param.25) | copy-start | bytes 786436
  4.3 22.0 %copy-start.1 = (bf16[1024,128]{1,0:T(8,128)(2,1)S(1)}, bf16[1024,128]{1,0:T(8,128)(2,1)}, u32[]{:S(2)}) copy-start(bf16[1024,128]{1,0:T(8,128)(2,1)} %get-tuple-element.25.cown) | copy-start | bytes 786436
  4.3 22.0 %collective-permute-start.1 = (bf16[1152,128]{1,0:T(8,128)(2,1)}, bf16[1152,128]{1,0:T(8,128)(2,1)S(1)}, u32[]{:S(2)}, u32[]{:S(2)}) collective-permute-start(bf16[1152,128]{1,0:T(8,128)(2,1)} %get-tuple-element.27), channel_id=1, source_target_pairs={{0,8},{16,24},{32,40},{48,56},{64,72},{80,88},{96,104},{112,120},{... | collective-permute-start | bytes 884744 | tf_op jit(solution)/shard_map/ppermute | solution.py:424
  7.6 18.6 %collective-permute-start.2 = (bf16[1152,128]{1,0:T(8,128)(2,1)}, bf16[1152,128]{1,0:T(8,128)(2,1)S(1)}, u32[]{:S(2)}, u32[]{:S(2)}) collective-permute-start(bf16[1152,128]{1,0:T(8,128)(2,1)} %get-tuple-element.28), channel_id=1, source_target_pairs={{8,16},{24,32},{40,48},{56,64},{72,80},{88,96},{104,112},{120,128}... | collective-permute-start | bytes 884744 | tf_op jit(solution)/shard_map/ppermute | solution.py:424
  9.5 14.8 %all-to-all-start = ((bf16[8,32,128]{2,1,0:T(8,128)(2,1)}), bf16[8,32,128]{2,1,0:T(8,128)(2,1)S(1)}, u32[]{:S(2)}, u32[]{:S(2)}) async-start(bf16[8,32,128]{2,1,0:T(8,128)(2,1)} %get-tuple-element.23), calls=%async_computation | async-start | bytes 131072 | tf_op jit(solution)/shard_map/all_to_all | solution.py:419
  17.1 25.7 %copy-start = (bf16[64,4096]{1,0:T(8,128)(2,1)S(1)}, bf16[64,4096]{1,0:T(8,128)(2,1)}, u32[]{:S(2)}) copy-start(bf16[64,4096]{1,0:T(8,128)(2,1)} %v.1) | copy-start | bytes 1572868
  17.1 25.7 %copy-start.13 = (s32[12,64]{1,0:T(8,128)S(1)}, s32[12,64]{1,0:T(8,128)}, u32[]{:S(2)}) copy-start(s32[12,64]{1,0:T(8,128)} %get-tuple-element.31.ix_any) | copy-start | bytes 9220
  24.4 3.6 %collective-permute-start = (bf16[144,128]{1,0:T(8,128)(2,1)S(1)}, bf16[144,128]{1,0:T(8,128)(2,1)S(1)}, u32[]{:S(2)}, u32[]{:S(2)}) collective-permute-start(bf16[144,128]{1,0:T(8,128)(2,1)S(1)} %group_sum.1.y), channel_id=1, source_target_pairs={{0,16},{8,24},{16,0},{24,8},{32,48},{40,56},{48,32},{56,40},{64,80... | collective-permute-start | bytes 110600 | tf_op jit(solution)/shard_map/ppermute | solution.py:477
  26.3 1.0 %copy-start.6 = (bf16[1024,128]{1,0:T(8,128)(2,1)S(1)}, bf16[1024,128]{1,0:T(8,128)(2,1)}, u32[]{:S(2)}) copy-start(bf16[1024,128]{1,0:T(8,128)(2,1)} %get-tuple-element.24.faces) | copy-start | bytes 786436
  27.2 0.8 %copy-start.7 = (bf16[128,128]{1,0:T(8,128)(2,1)S(1)}, bf16[128,128]{1,0:T(8,128)(2,1)}, u32[]{:S(2)}) copy-start(bf16[128,128]{1,0:T(8,128)(2,1)} %get-tuple-element.26.nown) | copy-start | bytes 98308
  28.1 4.8 %collective-permute-start.3 = (bf16[288,128]{1,0:T(8,128)(2,1)S(1)}, bf16[288,128]{1,0:T(8,128)(2,1)S(1)}, u32[]{:S(2)}, u32[]{:S(2)}) collective-permute-start(bf16[288,128]{1,0:T(8,128)(2,1)S(1)} %table_join.3), channel_id=1, source_target_pairs={{0,32},{8,40},{16,48},{24,56},{32,0},{40,8},{48,16},{56,24},{64,96... | collective-permute-start | bytes 221192 | tf_op jit(solution)/shard_map/ppermute | solution.py:477
  30.1 12.6 %collective-permute-start.6 = (bf16[2176,128]{1,0:T(8,128)(2,1)S(1)}, bf16[2176,128]{1,0:T(8,128)(2,1)S(1)}, u32[]{:S(2)}, u32[]{:S(2)}) collective-permute-start(bf16[2176,128]{1,0:T(8,128)(2,1)S(1)} %get-tuple-element.29.after), channel_id=1, source_target_pairs={{0,1},{2,3},{4,5},{6,7},{1,0},{3,2},{5,4},{7,6},{8,9},{10,11},{12,... | collective-permute-start | bytes 1671176 | tf_op jit(solution)/shard_map/ppermute | solution.py:424
  30.6 12.1 %collective-permute-start.7 = (bf16[2176,128]{1,0:T(8,128)(2,1)S(1)}, bf16[2176,128]{1,0:T(8,128)(2,1)S(1)}, u32[]{:S(2)}, u32[]{:S(2)}) collective-permute-start(bf16[2176,128]{1,0:T(8,128)(2,1)S(1)} %get-tuple-element.32), channel_id=1, source_target_pairs={{1,2},{3,4},{5,6},{2,1},{4,3},{6,5},{9,10},{11,12},{13,14},{10,9},... | collective-permute-start | bytes 1671176 | tf_op jit(solution)/shard_map/ppermute | solution.py:424
  32.9 7.1 %collective-permute-start.4 = (bf16[576,128]{1,0:T(8,128)(2,1)S(1)}, bf16[576,128]{1,0:T(8,128)(2,1)S(1)}, u32[]{:S(2)}, u32[]{:S(2)}) collective-permute-start(bf16[576,128]{1,0:T(8,128)(2,1)S(1)} %pad_maximum_fusion.y), channel_id=1, source_target_pairs={{0,64},{8,72},{16,80},{24,88},{32,96},{40,104},{48,112},{56,120},{... | collective-permute-start | bytes 442376 | tf_op jit(solution)/shard_map/ppermute | solution.py:477
  34.2 0.9 %copy-start.9 = (bf16[16,32,32,1]{2,1,3,0:T(8,128)(2,1)S(1)}, bf16[16,32,32,1]{2,1,3,0:T(8,128)(2,1)}, u32[]{:S(2)}) copy-start(bf16[16,32,32,1]{2,1,3,0:T(8,128)(2,1)} %param.27) | copy-start | bytes 98308
  35.1 0.8 %copy-start.10 = (bf16[8,32,32,1]{2,1,3,0:T(8,128)(2,1)S(1)}, bf16[8,32,32,1]{2,1,3,0:T(8,128)(2,1)}, u32[]{:S(2)}) copy-start(bf16[8,32,32,1]{2,1,3,0:T(8,128)(2,1)} %param.29) | copy-start | bytes 49156
  40.0 15.0 %copy-start.8 = (bf16[128,128]{1,0:T(8,128)(2,1)S(1)}, bf16[128,128]{1,0:T(8,128)(2,1)}, u32[]{:S(2)}) copy-start(bf16[128,128]{1,0:T(8,128)(2,1)} %get-tuple-element.26.nown) | copy-start | bytes 98308
  40.0 15.0 %copy-start.12 = (s32[16,64]{1,0:T(8,128)S(1)}, s32[16,64]{1,0:T(8,128)}, u32[]{:S(2)}) copy-start(s32[16,64]{1,0:T(8,128)} %get-tuple-element.36.li_any) | copy-start | bytes 12292
  40.0 15.0 %copy-start.14 = (s32[8,16]{1,0:T(8,128)S(1)}, s32[8,16]{1,0:T(8,128)}, u32[]{:S(2)}) copy-start(s32[8,16]{1,0:T(8,128)} %get-tuple-element.37.mi_any) | copy-start | bytes 1540
  40.0 9.0 %collective-permute-start.5 = (bf16[1152,128]{1,0:T(8,128)(2,1)S(1)}, bf16[1152,128]{1,0:T(8,128)(2,1)S(1)}, u32[]{:S(2)}, u32[]{:S(2)}) collective-permute-start(bf16[1152,128]{1,0:T(8,128)(2,1)S(1)} %table_join.4.y), channel_id=1, source_target_pairs={{0,128},{8,136},{16,144},{24,152},{32,160},{40,168},{48,176},{56,1... | collective-permute-start | bytes 884744 | tf_op jit(solution)/shard_map/ppermute | solution.py:477
  42.8 17.4 %copy-start.3 = (bf16[32,4096]{1,0:T(8,128)(2,1)S(1)}, bf16[32,4096]{1,0:T(8,128)(2,1)}, u32[]{:S(2)}) copy-start(bf16[32,4096]{1,0:T(8,128)(2,1)} %b.1) | copy-start | bytes 786436
  42.8 17.4 %copy-start.4 = (bf16[2048,128]{1,0:T(8,128)(2,1)S(1)}, bf16[2048,128]{1,0:T(8,128)(2,1)}, u32[]{:S(2)}) copy-start(bf16[2048,128]{1,0:T(8,128)(2,1)} %get-tuple-element.35.tl) | copy-start | bytes 1572868
  42.8 17.4 %copy-start.5 = (bf16[32,32,8]{1,2,0:T(8,128)(2,1)S(1)}, bf16[32,32,8]{1,2,0:T(8,128)(2,1)}, u32[]{:S(2)}) copy-start(bf16[32,32,8]{1,2,0:T(8,128)(2,1)} %param.20) | copy-start | bytes 49156
  42.8 17.4 %copy-start.11 = (bf16[32,32,1]{1,0,2:T(8,128)(2,1)S(1)}, bf16[32,32,1]{1,0,2:T(8,128)(2,1)}, u32[]{:S(2)}) copy-start(bf16[32,32,1]{1,0,2:T(8,128)(2,1)} %param.21) | copy-start | bytes 6148
  42.8 17.4 %copy-start.15 = (s32[16,1]{0,1:T(1,128)S(1)}, s32[16,1]{0,1:T(1,128)}, u32[]{:S(2)}) copy-start(s32[16,1]{0,1:T(1,128)} %param.26) | copy-start | bytes 196
  42.8 17.3 %copy-start.16 = (s32[8,1]{0,1:T(1,128)S(1)}, s32[8,1]{0,1:T(1,128)}, u32[]{:S(2)}) copy-start(s32[8,1]{0,1:T(1,128)} %param.28) | copy-start | bytes 100
  49.1 11.1 %collective-permute-start.8 = (bf16[2304,128]{1,0:T(8,128)(2,1)S(1)}, bf16[2304,128]{1,0:T(8,128)(2,1)S(1)}, u32[]{:S(2)}, u32[]{:S(2)}) collective-permute-start(bf16[2304,128]{1,0:T(8,128)(2,1)S(1)} %table_join.5.own), channel_id=1, source_target_pairs={{0,8},{8,0},{16,24},{24,16},{32,40},{40,32},{48,56},{56,48},{64,72... | collective-permute-start | bytes 1769480 | tf_op jit(solution)/shard_map/ppermute | solution.py:477

commit v2 on v1

--- a/solution.py
+++ b/solution.py
@@ -194,7 +194,7 @@
         zg[:, q * 128:(q + 1) * 128] = jnp.concatenate(parts, axis=1).astype(BF)
 
 
-def near_kernel(ix_any, v, ra, rb, qa, qb, blocks_hbm, out, low, high, picked, ix, blocks, sems):
+def near_kernel(ix_any, v, ra, rb, qa, qb, blocks_hbm, out, pieces, ix, blocks, sems):
     loads = copies(
         [(ix_any, ix)]
         + [(blocks_hbm.at[:, pl.ds(512 * t, 512)], blocks.at[t]) for t in range(8)],
@@ -206,12 +206,8 @@
     def table():
         def put(wx, wy, k, x):
             at = (wx * 6 + wy) * 4 + 2 * k
-            x = x.astype(F32)
-            swapped = pltpu.roll(x, 64, 1)
-            low[at] = jnp.where(mask, x, 0.0).astype(BF)
-            high[at] = jnp.where(mask, 0.0, swapped).astype(BF)
-            low[at + 1] = jnp.where(mask, swapped, 0.0).astype(BF)
-            high[at + 1] = jnp.where(mask, 0.0, x).astype(BF)
+            pieces[at] = x
+            pieces[at + 1] = pltpu.roll(x.astype(F32), 64, 1).astype(BF)
 
         for i in range(2):
             for j in range(2):
@@ -245,35 +241,36 @@
             blocks_hbm.at[:, pl.ds(pl.multiple_of(512 * t, 512), 512)], blocks.at[t], sems.at[t + 1]
         ).wait()
         for q in range(4):
+            lhs = []
             for i in range(2):
                 leaf = t * 8 + 2 * q + i
-                for sp in range(6):
-                    picked[q, i * 64:(i + 1) * 64, sp * 128:(sp + 1) * 128] = (
-                        low[ix[2 * sp, leaf]] + high[ix[2 * sp + 1, leaf]]
-                    )
-            r = dot(picked[q], blocks[t, :, q * 128:(q + 1) * 128], 1, 0)
+                lhs.append(jnp.concatenate(
+                    [
+                        jnp.where(mask, pieces[ix[2 * sp, leaf]], pieces[ix[2 * sp + 1, leaf] ^ 1])
+                        for sp in range(6)
+                    ],
+                    axis=1,
+                ))
+            r = dot(jnp.concatenate(lhs, axis=0), blocks[t, :, q * 128:(q + 1) * 128], 1, 0)
             lanes = pl.ds(pl.multiple_of(t * 512 + q * 128, 128), 128)
             out[:, lanes] = jnp.where(mask, r[:64], r[64:])
         return carry
 
-    lax.fori_loop(0, 8, chunk, 0)
+    lax.fori_loop(0, 8, chunk, 0, unroll=2)
 
 
 def far_kernel(
-    li_any, mi_any, cown, nown, ra, rb, qa, qb, za, zb, zn, far, nfar, low, high, nw, li, mi, sems
+    li_any, mi_any, cown, nown, ra, rb, qa, qb, za, zb, zn, far, nfar, pieces, nw, li, mi, sems
 ):
     loads = copies([(li_any, li), (mi_any, mi)], sems)
     mask = low_lanes(32)
 
     def put_leaves(nwx, nwy, k, side, first):
         for p in range(4):
-            x = side[first + p * 32:first + (p + 1) * 32, :].astype(F32)
+            x = side[first + p * 32:first + (p + 1) * 32, :]
             at = ((nwx * 4 + nwy) * 2 + k) * 8 + 2 * p
-            swapped = pltpu.roll(x, 64, 1)
-            low[at] = jnp.where(mask, x, 0.0).astype(BF)
-            high[at] = jnp.where(mask, 0.0, swapped).astype(BF)
-            low[at + 1] = jnp.where(mask, swapped, 0.0).astype(BF)
-            high[at + 1] = jnp.where(mask, 0.0, x).astype(BF)
+            pieces[at] = x
+            pieces[at + 1] = pltpu.roll(x.astype(F32), 64, 1).astype(BF)
 
     def put_nodes(nwx, nwy, side, first):
         x = side[first:first + 32, :]
@@ -316,7 +313,8 @@
         for u in range(4):
             n = t * 8 + 2 * u
             block = jnp.concatenate(
-                [low[li[s, n]] + high[li[s, n + 1]] for s in range(16)], axis=0
+                [jnp.where(mask, pieces[li[s, n]], pieces[li[s, n + 1] ^ 1]) for s in range(16)],
+                axis=0,
             )
             rows = pl.ds(pl.multiple_of(n * 32, 64), 64)
             r = dot(za[rows, :], block[:256], 1, 0) + dot(zb[rows, :], block[256:], 1, 0)
@@ -324,7 +322,7 @@
             far[pl.ds(pl.multiple_of(n * 32 + 32, 32), 32), :] = pltpu.roll(r[32:], 64, 1)
         return carry
 
-    lax.fori_loop(0, 8, leaves, 0)
+    lax.fori_loop(0, 8, leaves, 0, unroll=8)
 
 
 def table_kernel(y, received, after, own):
@@ -498,8 +496,7 @@
         in_specs=[AN, VM, VM, VM, VM, VM, HB],
         out_specs=VM,
         scratch_shapes=[
-            pltpu.VMEM((144, 64, 128), BF), pltpu.VMEM((144, 64, 128), BF),
-            pltpu.VMEM((4, 128, 768), BF), pltpu.SMEM((12, 64), jnp.int32),
+            pltpu.VMEM((144, 64, 128), BF), pltpu.SMEM((12, 64), jnp.int32),
             pltpu.VMEM((8, 768, 512), BF), pltpu.SemaphoreType.DMA((9,)),
         ],
         compiler_params=params(48),
@@ -517,8 +514,7 @@
         in_specs=[AN] * 2 + [VM] * 9,
         out_specs=[VM] * 2,
         scratch_shapes=[
-            pltpu.VMEM((256, 32, 128), BF), pltpu.VMEM((256, 32, 128), BF),
-            pltpu.VMEM((72, 32, 128), BF), pltpu.SMEM((16, 64), jnp.int32), pltpu.SMEM((8, 16), jnp.int32),
+            pltpu.VMEM((256, 32, 128), BF), pltpu.VMEM((72, 32, 128), BF), pltpu.SMEM((16, 64), jnp.int32), pltpu.SMEM((8, 16), jnp.int32),
             pltpu.SemaphoreType.DMA((2,)),
         ],
         compiler_params=params(32),

time: 63.2 us -> 60 us (0.949)
  Pallas kernels: 25.8 us -> 22.3 us
    pallas_call x1, Pallas kernels: 5.09 us -> 3.09 us  [body(): pl.pallas_call(far_kernel, out_shape=[shape((2048, 128), F32), shape((256...]
    pallas_call x1, Pallas kernels: 6.14 us -> 4.68 us  [body(): pl.pallas_call(near_kernel, out_shape=shape((64, 4096), F32), in_specs=[A...]
  transfers between devices with their start and end apart: 10 -> 10, of which waited for: 2 -> 3; matrix products, arithmetic and copies ran while one was open for 0% -> 0% of each run, Pallas kernels for 30% -> 26%
where the time goes in v2:
time: 60 us; the launch traced here: 59.5 us
  starting transfers between devices  27.4 us (46%)
  Pallas kernels  22.3 us (37%)
  waiting for transfers between devices  5.98 us (10%)
  local copies, waits for them, and re-layouts  3.51 us (6%)
    ppermute x5, starting transfers between devices, body(): lax.ppermute(x, 'coarse', [(i, i ^ bit) for i in range(coarse)])  13.4 us
    all_to_all x1, starting transfers between devices, body(): r = lax.all_to_all(pay, 'leaf', 0, 0, tiled=True)  7.57 us
    ppermute x4, starting transfers between devices, swap(): return lax.ppermute(x, axis, pairs + [(j, i) for i, j in pairs])  6.44 us
    pallas_call x1, Pallas kernels, body(): pl.pallas_call(near_kernel, out_shape=shape((64, 4096), F32), in_specs=[A...  4.68 us
    pallas_call x1, Pallas kernels, body(): pl.pallas_call(up_kernel, out_shape=[shape((8, 32, 128)), shape((1024, 12...  4.27 us
    pallas_call x1, Pallas kernels, body(): pl.pallas_call(second_layout_kernel, out_shape=[shape((2048, 256)), shape...  4.05 us
    all_to_all x1, waiting for transfers between devices, body(): r = lax.all_to_all(pay, 'leaf', 0, 0, tiled=True)  3.81 us
    unnamed x34, local copies, waits for them, and re-layouts  3.51 us
  transfers between devices with their start and end apart: 10, of which 3 were waited for; matrix products, arithmetic and copies ran while one was open for 0% of the time, Pallas kernels for 26%

profile of v2, /device:TPU:1, one launch (start us, length us, event | category | flops | bytes accessed | tf_op | source)
XLA Modules:
  0.0 59.5 jit_solution(1504343584835083658)
XLA Ops:
  0.0 0.0 copy-start.2
  0.0 4.3 %up_pass.1 = (bf16[8,32,128]{2,1,0:T(8,128)(2,1)}, bf16[1024,128]{1,0:T(8,128)(2,1)}, bf16[128,128]{1,0:T(8,128)(2,1)}, bf16[1152,128]{1,0:T(8,128)(2,1)}, bf16[...) custom-call(bf16[64,4096]{1,0:T(8,128)(2,1)} %v.1, ...), custom_call_target="tpu_custom_call" | custom-call | flops 1000000 | bytes 100000 | tf_op jit(solution)/shard_map/up_pass/pallas_call | solution.py:394
  4.3 0.0 copy-start.1
  4.3 3.3 %collective-permute-start.1 = (bf16[1152,128]{1,0:T(8,128)(2,1)}, bf16[1152,128]{1,0:T(8,128)(2,1)S(1)}, u32[]{:S(2)}, u32[]{:S(2)}) collective-permute-start(bf16[1152,128]{1,0:T(8,128)(2,1)} %get-tuple-element.27), channel_id=1, source_target_pairs={{0,8},{16,24},{32,40},{48,56},{64,72},{80,88},{96,104},{112,120},{... | collective-permute-start | bytes 884744 | tf_op jit(solution)/shard_map/ppermute | solution.py:422
  7.6 1.9 %collective-permute-start.2 = (bf16[1152,128]{1,0:T(8,128)(2,1)}, bf16[1152,128]{1,0:T(8,128)(2,1)S(1)}, u32[]{:S(2)}, u32[]{:S(2)}) collective-permute-start(bf16[1152,128]{1,0:T(8,128)(2,1)} %get-tuple-element.28), channel_id=1, source_target_pairs={{8,16},{24,32},{40,48},{56,64},{72,80},{88,96},{104,112},{120,128}... | collective-permute-start | bytes 884744 | tf_op jit(solution)/shard_map/ppermute | solution.py:422
  9.5 7.6 %all-to-all-start = ((bf16[8,32,128]{2,1,0:T(8,128)(2,1)}), bf16[8,32,128]{2,1,0:T(8,128)(2,1)S(1)}, u32[]{:S(2)}, u32[]{:S(2)}) async-start(bf16[8,32,128]{2,1,0:T(8,128)(2,1)} %get-tuple-element.23), calls=%async_computation | async-start | bytes 131072 | tf_op jit(solution)/shard_map/all_to_all | solution.py:417
  17.1 0.0 copy-start
  17.1 0.0 copy-start.13
  17.1 3.4 %first_layout.1.after.za = bf16[2048,256]{1,0:T(8,128)(2,1)S(1)} custom-call(bf16[16,32,32,64]{3,2,1,0:T(8,128)(2,1)} %s_hbm.3), custom_call_target="tpu_custom_call" | custom-call | flops 1000 | bytes 1000000 | tf_op jit(solution)/shard_map/first_layout/pallas_call | solution.py:427
  20.5 3.8 %all-to-all-done.r = bf16[8,32,128]{2,1,0:T(8,128)(2,1)S(1)} async-done(((bf16[8,32,128]{2,1,0:T(8,128)(2,1)}), bf16[8,32,128]{2,1,0:T(8,128)(2,1)S(1)}, u32[]{:S(2)}, u32[]{:S(2)}) %all-to-all-start) | async-done | bytes 65568 | tf_op jit(solution)/shard_map/all_to_all | solution.py:417
  24.3 0.1 group_sum.1.y
  24.4 1.8 %collective-permute-start = (bf16[144,128]{1,0:T(8,128)(2,1)S(1)}, bf16[144,128]{1,0:T(8,128)(2,1)S(1)}, u32[]{:S(2)}, u32[]{:S(2)}) collective-permute-start(bf16[144,128]{1,0:T(8,128)(2,1)S(1)} %group_sum.1.y), channel_id=1, source_target_pairs={{0,16},{8,24},{16,0},{24,8},{32,48},{40,56},{48,32},{56,40},{64,80... | collective-permute-start | bytes 110600 | tf_op jit(solution)/shard_map/ppermute | solution.py:475
  26.2 0.0 collective-permute-done.1.ra
  26.3 0.0 collective-permute-done.2.rb
  26.3 0.0 copy-done.1
  26.3 0.0 copy-start.6
  26.3 0.9 %copy-done.6 = bf16[1024,128]{1,0:T(8,128)(2,1)S(1)} copy-done((bf16[1024,128]{1,0:T(8,128)(2,1)S(1)}, bf16[1024,128]{1,0:T(8,128)(2,1)}, u32[]{:S(2)}) %copy-start.6) | copy-done | bytes 262168
  27.2 0.0 copy-start.7
  27.2 0.8 %copy-done.7 = bf16[128,128]{1,0:T(8,128)(2,1)S(1)} copy-done((bf16[128,128]{1,0:T(8,128)(2,1)S(1)}, bf16[128,128]{1,0:T(8,128)(2,1)}, u32[]{:S(2)}) %copy-start.7) | copy-done | bytes 32792
  28.0 0.1 halo_pack.1
  28.0 0.0 collective-permute-done.received
  28.1 2.0 %collective-permute-start.3 = (bf16[288,128]{1,0:T(8,128)(2,1)S(1)}, bf16[288,128]{1,0:T(8,128)(2,1)S(1)}, u32[]{:S(2)}, u32[]{:S(2)}) collective-permute-start(bf16[288,128]{1,0:T(8,128)(2,1)S(1)} %table_join.3), channel_id=1, source_target_pairs={{0,32},{8,40},{16,48},{24,56},{32,0},{40,8},{48,16},{56,24},{64,96... | collective-permute-start | bytes 221192 | tf_op jit(solution)/shard_map/ppermute | solution.py:475
  30.1 0.5 collective-permute-start.6
  30.6 0.7 %collective-permute-start.7 = (bf16[2176,128]{1,0:T(8,128)(2,1)S(1)}, bf16[2176,128]{1,0:T(8,128)(2,1)S(1)}, u32[]{:S(2)}, u32[]{:S(2)}) collective-permute-start(bf16[2176,128]{1,0:T(8,128)(2,1)S(1)} %get-tuple-element.32), channel_id=1, source_target_pairs={{1,2},{3,4},{5,6},{2,1},{4,3},{6,5},{9,10},{11,12},{13,14},{10,9},... | collective-permute-start | bytes 1671176 | tf_op jit(solution)/shard_map/ppermute | solution.py:422
  31.3 1.5 %collective-permute-done.3 = bf16[288,128]{1,0:T(8,128)(2,1)S(1)} collective-permute-done((bf16[288,128]{1,0:T(8,128)(2,1)S(1)}, bf16[288,128]{1,0:T(8,128)(2,1)S(1)}, u32[]{:S(2)}, u32[]{:S(2)}) %collective-permute-start.3) | collective-permute-done | bytes 73760 | tf_op jit(solution)/shard_map/ppermute | solution.py:475
  32.9 1.4 %collective-permute-start.4 = (bf16[576,128]{1,0:T(8,128)(2,1)S(1)}, bf16[576,128]{1,0:T(8,128)(2,1)S(1)}, u32[]{:S(2)}, u32[]{:S(2)}) collective-permute-start(bf16[576,128]{1,0:T(8,128)(2,1)S(1)} %pad_maximum_fusion.y), channel_id=1, source_target_pairs={{0,64},{8,72},{16,80},{24,88},{32,96},{40,104},{48,112},{56,120},{... | collective-permute-start | bytes 442376 | tf_op jit(solution)/shard_map/ppermute | solution.py:475
  34.3 0.0 copy-done.2
  34.3 0.0 copy-start.9
  34.3 0.9 %copy-done.9 = bf16[16,32,32,1]{2,1,3,0:T(8,128)(2,1)S(1)} copy-done((bf16[16,32,32,1]{2,1,3,0:T(8,128)(2,1)S(1)}, bf16[16,32,32,1]{2,1,3,0:T(8,128)(2,1)}, u32[]{:S(2)}) %copy-start.9) | copy-done | bytes 32792
  35.2 0.0 copy-start.10
  35.2 0.8 %copy-done.10 = bf16[8,32,32,1]{2,1,3,0:T(8,128)(2,1)S(1)} copy-done((bf16[8,32,32,1]{2,1,3,0:T(8,128)(2,1)S(1)}, bf16[8,32,32,1]{2,1,3,0:T(8,128)(2,1)}, u32[]{:S(2)}) %copy-start.10) | copy-done | bytes 16408
  36.0 4.1 %second_layout.1 = (bf16[2048,256]{1,0:T(8,128)(2,1)S(1)}, bf16[256,512]{1,0:T(8,128)(2,1)S(1)}, bf16[32,512]{1,0:T(8,128)(2,1)S(1)}, bf16[32,256]{1,0:T(8,128)(2,1)S(1)}) custom-call(bf16[16,32,32,64]{3,2,1,0:T(8,128)(2,1)} %s_hbm.3, bf16[16,32,8,32]{3,2,1,0:T(8,128)(2,1)S(1)} %bitcast.11, bf16[16,32,32]{2,1,0:T(8,128)(2,1)S(1)} %bitcast.14, ...), custom_call_target="tpu_custom_call" | custom-call | flops 1000 | bytes 1000000 | tf_op jit(solution)/shard_map/second_layout/pallas_call | solution.py:437
  40.1 0.0 collective-permute-done.4.received
  40.1 0.0 copy-start.8
  40.1 0.0 copy-start.12
  40.1 0.0 copy-start.14
  40.1 2.7 %collective-permute-start.5 = (bf16[1152,128]{1,0:T(8,128)(2,1)S(1)}, bf16[1152,128]{1,0:T(8,128)(2,1)S(1)}, u32[]{:S(2)}, u32[]{:S(2)}) collective-permute-start(bf16[1152,128]{1,0:T(8,128)(2,1)S(1)} %table_join.4.y), channel_id=1, source_target_pairs={{0,128},{8,136},{16,144},{24,152},{32,160},{40,168},{48,176},{56,1... | collective-permute-start | bytes 884744 | tf_op jit(solution)/shard_map/ppermute | solution.py:475
  42.9 0.0 collective-permute-done.7.qb
  42.9 0.0 collective-permute-done.6.qa
  42.9 0.0 copy-done
  42.9 0.0 copy-done.13
  42.9 0.0 copy-start.3
  42.9 0.0 copy-start.4
  42.9 0.0 copy-start.5
  42.9 0.0 copy-start.11
  42.9 0.0 copy-start.15
  42.9 0.0 copy-start.16
  42.9 4.7 %near_field.1.after.near = f32[64,4096]{1,0:T(8,128)S(1)} custom-call(s32[12,64]{1,0:T(8,128)S(1)} %copy-done.13, bf16[64,4096]{1,0:T(8,128)(2,1)S(1)} %copy-done, bf16[1152,128]{1,0:T(8,128)(2,1)S(1)} %collective-permute-done.1.ra, bf16[1152,128]{1,0:T(8,128)(2,1)S(1)} %collective-permute-done.2.rb, bf16[2176,128]{1,0:T(8,128)(2,1)S(1)} %collective-permute-done.6.qa, ...), custom_call_target="tpu_custom_call" | custom-call | flops 1000 | bytes 1000000 | tf_op jit(solution)/shard_map/near_field/pallas_call | solution.py:493
  47.6 0.6 %collective-permute-done.5.received = bf16[1152,128]{1,0:T(8,128)(2,1)S(1)} collective-permute-done((bf16[1152,128]{1,0:T(8,128)(2,1)S(1)}, bf16[1152,128]{1,0:T(8,128)(2,1)S(1)}, u32[]{:S(2)}, u32[]{:S(2)}) %collective-permute-start.5) | collective-permute-done | bytes 294944 | tf_op jit(solution)/shard_map/ppermute | solution.py:475
  48.3 5.4 %collective-permute-start.8 = (bf16[2304,128]{1,0:T(8,128)(2,1)S(1)}, bf16[2304,128]{1,0:T(8,128)(2,1)S(1)}, u32[]{:S(2)}, u32[]{:S(2)}) collective-permute-start(bf16[2304,128]{1,0:T(8,128)(2,1)S(1)} %table_join.5.own), channel_id=1, source_target_pairs={{0,8},{8,0},{16,24},{24,16},{32,40},{40,32},{48,56},{56,48},{64,72... | collective-permute-start | bytes 1769480 | tf_op jit(solution)/shard_map/ppermute | solution.py:475
  53.7 0.0 copy-done.8
  53.7 0.0 copy-done.12
  53.7 0.0 copy-done.14
  53.7 3.1 %far_field.1 = (f32[2048,128]{1,0:T(8,128)S(1)}, f32[256,128]{1,0:T(8,128)S(1)}) custom-call(s32[16,64]{1,0:T(8,128)S(1)} %copy-done.12, s32[8,16]{1,0:T(8,128)S(1)} %copy-done.14, bf16[1024,128]{1,0:T(8,128)(2,1)S(1)} %copy-done.1, bf16[128,128]{1,0:T(8,128)(2,1)S(1)} %copy-done.8, bf16[1152,128]{1,0:T(8,128)(2,1)S(1)} %collective-permute-done.1.ra, ...), custom_call_target="tpu_custom_call" | custom-call | flops 1000 | bytes 1000000 | tf_op jit(solution)/shard_map/far_field/pallas_call | solution.py:511
  56.8 0.0 collective-permute-done.8.other
  56.9 0.0 copy-done.3
  56.9 0.0 copy-done.4
  56.9 0.0 copy-done.5
  56.9 0.0 copy-done.11
  56.9 0.0 copy-done.15
  56.9 0.0 copy-done.16
  56.9 2.6 %down_pass.1 = bf16[64,4096]{1,0:T(8,128)(2,1)} custom-call(s32[1,16]{1,0:T(1,128)S(1)} %bitcast.18, s32[1,8]{1,0:T(1,128)S(1)} %bitcast.19, bf16[2304,128]{1,0:T(8,128)(2,1)S(1)} %table_join.5.own, bf16[2304,128]{1,0:T(8,128)(2,1)S(1)} %collective-permute-done.8.other, bf16[32,512]{1,0:T(8,128)(2,1)S(1)} %get-tuple-element.33.zd, ...), custom_call_target="tpu_custom_call" | custom-call | flops 1000000 | bytes 100000 | tf_op jit(solution)/shard_map/down_pass/pallas_call | solution.py:528
  (4 shorter events, 0.1 us)
Async XLA Ops:
  0.0 34.3 %copy-start.2 = (bf16[16,32,32,8]{2,3,1,0:T(8,128)(2,1)S(1)}, bf16[16,32,32,8]{2,3,1,0:T(8,128)(2,1)}, u32[]{:S(2)}) copy-start(bf16[16,32,32,8]{2,3,1,0:T(8,128)(2,1)} %param.25) | copy-start | bytes 786436
  4.3 22.0 %copy-start.1 = (bf16[1024,128]{1,0:T(8,128)(2,1)S(1)}, bf16[1024,128]{1,0:T(8,128)(2,1)}, u32[]{:S(2)}) copy-start(bf16[1024,128]{1,0:T(8,128)(2,1)} %get-tuple-element.25.cown) | copy-start | bytes 786436
  4.3 22.0 %collective-permute-start.1 = (bf16[1152,128]{1,0:T(8,128)(2,1)}, bf16[1152,128]{1,0:T(8,128)(2,1)S(1)}, u32[]{:S(2)}, u32[]{:S(2)}) collective-permute-start(bf16[1152,128]{1,0:T(8,128)(2,1)} %get-tuple-element.27), channel_id=1, source_target_pairs={{0,8},{16,24},{32,40},{48,56},{64,72},{80,88},{96,104},{112,120},{... | collective-permute-start | bytes 884744 | tf_op jit(solution)/shard_map/ppermute | solution.py:422
  7.6 18.6 %collective-permute-start.2 = (bf16[1152,128]{1,0:T(8,128)(2,1)}, bf16[1152,128]{1,0:T(8,128)(2,1)S(1)}, u32[]{:S(2)}, u32[]{:S(2)}) collective-permute-start(bf16[1152,128]{1,0:T(8,128)(2,1)} %get-tuple-element.28), channel_id=1, source_target_pairs={{8,16},{24,32},{40,48},{56,64},{72,80},{88,96},{104,112},{120,128}... | collective-permute-start | bytes 884744 | tf_op jit(solution)/shard_map/ppermute | solution.py:422
  9.5 14.8 %all-to-all-start = ((bf16[8,32,128]{2,1,0:T(8,128)(2,1)}), bf16[8,32,128]{2,1,0:T(8,128)(2,1)S(1)}, u32[]{:S(2)}, u32[]{:S(2)}) async-start(bf16[8,32,128]{2,1,0:T(8,128)(2,1)} %get-tuple-element.23), calls=%async_computation | async-start | bytes 131072 | tf_op jit(solution)/shard_map/all_to_all | solution.py:417
  17.1 25.8 %copy-start = (bf16[64,4096]{1,0:T(8,128)(2,1)S(1)}, bf16[64,4096]{1,0:T(8,128)(2,1)}, u32[]{:S(2)}) copy-start(bf16[64,4096]{1,0:T(8,128)(2,1)} %v.1) | copy-start | bytes 1572868
  17.1 25.8 %copy-start.13 = (s32[12,64]{1,0:T(8,128)S(1)}, s32[12,64]{1,0:T(8,128)}, u32[]{:S(2)}) copy-start(s32[12,64]{1,0:T(8,128)} %get-tuple-element.31.ix_any) | copy-start | bytes 9220
  24.4 3.6 %collective-permute-start = (bf16[144,128]{1,0:T(8,128)(2,1)S(1)}, bf16[144,128]{1,0:T(8,128)(2,1)S(1)}, u32[]{:S(2)}, u32[]{:S(2)}) collective-permute-start(bf16[144,128]{1,0:T(8,128)(2,1)S(1)} %group_sum.1.y), channel_id=1, source_target_pairs={{0,16},{8,24},{16,0},{24,8},{32,48},{40,56},{48,32},{56,40},{64,80... | collective-permute-start | bytes 110600 | tf_op jit(solution)/shard_map/ppermute | solution.py:475
  26.3 1.0 %copy-start.6 = (bf16[1024,128]{1,0:T(8,128)(2,1)S(1)}, bf16[1024,128]{1,0:T(8,128)(2,1)}, u32[]{:S(2)}) copy-start(bf16[1024,128]{1,0:T(8,128)(2,1)} %get-tuple-element.24.faces) | copy-start | bytes 786436
  27.2 0.8 %copy-start.7 = (bf16[128,128]{1,0:T(8,128)(2,1)S(1)}, bf16[128,128]{1,0:T(8,128)(2,1)}, u32[]{:S(2)}) copy-start(bf16[128,128]{1,0:T(8,128)(2,1)} %get-tuple-element.26.nown) | copy-start | bytes 98308
  28.1 4.8 %collective-permute-start.3 = (bf16[288,128]{1,0:T(8,128)(2,1)S(1)}, bf16[288,128]{1,0:T(8,128)(2,1)S(1)}, u32[]{:S(2)}, u32[]{:S(2)}) collective-permute-start(bf16[288,128]{1,0:T(8,128)(2,1)S(1)} %table_join.3), channel_id=1, source_target_pairs={{0,32},{8,40},{16,48},{24,56},{32,0},{40,8},{48,16},{56,24},{64,96... | collective-permute-start | bytes 221192 | tf_op jit(solution)/shard_map/ppermute | solution.py:475
  30.1 12.7 %collective-permute-start.6 = (bf16[2176,128]{1,0:T(8,128)(2,1)S(1)}, bf16[2176,128]{1,0:T(8,128)(2,1)S(1)}, u32[]{:S(2)}, u32[]{:S(2)}) collective-permute-start(bf16[2176,128]{1,0:T(8,128)(2,1)S(1)} %get-tuple-element.29.after), channel_id=1, source_target_pairs={{0,1},{2,3},{4,5},{6,7},{1,0},{3,2},{5,4},{7,6},{8,9},{10,11},{12,... | collective-permute-start | bytes 1671176 | tf_op jit(solution)/shard_map/ppermute | solution.py:422
  30.6 12.2 %collective-permute-start.7 = (bf16[2176,128]{1,0:T(8,128)(2,1)S(1)}, bf16[2176,128]{1,0:T(8,128)(2,1)S(1)}, u32[]{:S(2)}, u32[]{:S(2)}) collective-permute-start(bf16[2176,128]{1,0:T(8,128)(2,1)S(1)} %get-tuple-element.32), channel_id=1, source_target_pairs={{1,2},{3,4},{5,6},{2,1},{4,3},{6,5},{9,10},{11,12},{13,14},{10,9},... | collective-permute-start | bytes 1671176 | tf_op jit(solution)/shard_map/ppermute | solution.py:422
  32.9 7.2 %collective-permute-start.4 = (bf16[576,128]{1,0:T(8,128)(2,1)S(1)}, bf16[576,128]{1,0:T(8,128)(2,1)S(1)}, u32[]{:S(2)}, u32[]{:S(2)}) collective-permute-start(bf16[576,128]{1,0:T(8,128)(2,1)S(1)} %pad_maximum_fusion.y), channel_id=1, source_target_pairs={{0,64},{8,72},{16,80},{24,88},{32,96},{40,104},{48,112},{56,120},{... | collective-permute-start | bytes 442376 | tf_op jit(solution)/shard_map/ppermute | solution.py:475
  34.3 0.9 %copy-start.9 = (bf16[16,32,32,1]{2,1,3,0:T(8,128)(2,1)S(1)}, bf16[16,32,32,1]{2,1,3,0:T(8,128)(2,1)}, u32[]{:S(2)}) copy-start(bf16[16,32,32,1]{2,1,3,0:T(8,128)(2,1)} %param.27) | copy-start | bytes 98308
  35.2 0.8 %copy-start.10 = (bf16[8,32,32,1]{2,1,3,0:T(8,128)(2,1)S(1)}, bf16[8,32,32,1]{2,1,3,0:T(8,128)(2,1)}, u32[]{:S(2)}) copy-start(bf16[8,32,32,1]{2,1,3,0:T(8,128)(2,1)} %param.29) | copy-start | bytes 49156
  40.1 13.7 %copy-start.8 = (bf16[128,128]{1,0:T(8,128)(2,1)S(1)}, bf16[128,128]{1,0:T(8,128)(2,1)}, u32[]{:S(2)}) copy-start(bf16[128,128]{1,0:T(8,128)(2,1)} %get-tuple-element.26.nown) | copy-start | bytes 98308
  40.1 13.6 %copy-start.12 = (s32[16,64]{1,0:T(8,128)S(1)}, s32[16,64]{1,0:T(8,128)}, u32[]{:S(2)}) copy-start(s32[16,64]{1,0:T(8,128)} %get-tuple-element.36.li_any) | copy-start | bytes 12292
  40.1 13.6 %copy-start.14 = (s32[8,16]{1,0:T(8,128)S(1)}, s32[8,16]{1,0:T(8,128)}, u32[]{:S(2)}) copy-start(s32[8,16]{1,0:T(8,128)} %get-tuple-element.37.mi_any) | copy-start | bytes 1540
  40.1 8.1 %collective-permute-start.5 = (bf16[1152,128]{1,0:T(8,128)(2,1)S(1)}, bf16[1152,128]{1,0:T(8,128)(2,1)S(1)}, u32[]{:S(2)}, u32[]{:S(2)}) collective-permute-start(bf16[1152,128]{1,0:T(8,128)(2,1)S(1)} %table_join.4.y), channel_id=1, source_target_pairs={{0,128},{8,136},{16,144},{24,152},{32,160},{40,168},{48,176},{56,1... | collective-permute-start | bytes 884744 | tf_op jit(solution)/shard_map/ppermute | solution.py:475
  42.9 14.0 %copy-start.3 = (bf16[32,4096]{1,0:T(8,128)(2,1)S(1)}, bf16[32,4096]{1,0:T(8,128)(2,1)}, u32[]{:S(2)}) copy-start(bf16[32,4096]{1,0:T(8,128)(2,1)} %b.1) | copy-start | bytes 786436
  42.9 14.0 %copy-start.4 = (bf16[2048,128]{1,0:T(8,128)(2,1)S(1)}, bf16[2048,128]{1,0:T(8,128)(2,1)}, u32[]{:S(2)}) copy-start(bf16[2048,128]{1,0:T(8,128)(2,1)} %get-tuple-element.35.tl) | copy-start | bytes 1572868
  42.9 14.0 %copy-start.5 = (bf16[32,32,8]{1,2,0:T(8,128)(2,1)S(1)}, bf16[32,32,8]{1,2,0:T(8,128)(2,1)}, u32[]{:S(2)}) copy-start(bf16[32,32,8]{1,2,0:T(8,128)(2,1)} %param.20) | copy-start | bytes 49156
  42.9 14.0 %copy-start.11 = (bf16[32,32,1]{1,0,2:T(8,128)(2,1)S(1)}, bf16[32,32,1]{1,0,2:T(8,128)(2,1)}, u32[]{:S(2)}) copy-start(bf16[32,32,1]{1,0,2:T(8,128)(2,1)} %param.21) | copy-start | bytes 6148
  42.9 14.0 %copy-start.15 = (s32[16,1]{0,1:T(1,128)S(1)}, s32[16,1]{0,1:T(1,128)}, u32[]{:S(2)}) copy-start(s32[16,1]{0,1:T(1,128)} %param.26) | copy-start | bytes 196
  42.9 14.0 %copy-start.16 = (s32[8,1]{0,1:T(1,128)S(1)}, s32[8,1]{0,1:T(1,128)}, u32[]{:S(2)}) copy-start(s32[8,1]{0,1:T(1,128)} %param.28) | copy-start | bytes 100
  48.3 8.6 %collective-permute-start.8 = (bf16[2304,128]{1,0:T(8,128)(2,1)S(1)}, bf16[2304,128]{1,0:T(8,128)(2,1)S(1)}, u32[]{:S(2)}, u32[]{:S(2)}) collective-permute-start(bf16[2304,128]{1,0:T(8,128)(2,1)S(1)} %table_join.5.own), channel_id=1, source_target_pairs={{0,8},{8,0},{16,24},{24,16},{32,40},{40,32},{48,56},{56,48},{64,72... | collective-permute-start | bytes 1769480 | tf_op jit(solution)/shard_map/ppermute | solution.py:475

commit v3 on v2

--- a/solution.py
+++ b/solution.py
@@ -61,10 +61,10 @@
     )
     ident = eye(64)
     loads[0].wait()
-    for k in range(32):
-        tls[pl.ds(k, 64, stride=32), :] = dot(
-            ident, jnp.concatenate([lt[k], jnp.zeros((96, 64), BF)], axis=0), 1, 1
-        )
+    for q in range(8):
+        t = dot(ident, lt[4 * q:4 * q + 4].reshape(128, 64), 1, 1)
+        for i in range(4):
+            tls[pl.ds(4 * q + i, 64, stride=32), :] = pltpu.roll(t, (128 - 32 * i) % 128, 1) if i else t
     tl[...] = tls[...].astype(BF)
     for c in loads[1:]:
         c.wait()
@@ -331,7 +331,9 @@
     own[half:, :] = received[...]
 
 
-def down_kernel(dl, gl, own, other, zd, zg, dt, nt, tl, b, far, nfar, near, out, nds):
+def down_kernel(
+    dl, gl, own, other, zd, zg, dt, nt, tl, b, far, nfar, near, out_hbm, nds, out, sems
+):
     cp = lax.axis_index("coarse")
 
     def pick(coarse, row, count):
@@ -364,6 +366,11 @@
             bd = jnp.concatenate([bg, bg, bg, bg], axis=0) * mask
             x = dot(lf[h * 128:(h + 1) * 128, :64], bd, 0, 0)
             out[:, lanes] = (x + near[:, lanes]).astype(BF)
+        lanes = pl.ds(n * 512, 512)
+        pltpu.make_async_copy(out.at[:, lanes], out_hbm.at[:, lanes], sems.at[n]).start()
+    for n in range(8):
+        lanes = pl.ds(n * 512, 512)
+        pltpu.make_async_copy(out.at[:, lanes], out_hbm.at[:, lanes], sems.at[n]).wait()
 
 
 AN = pl.BlockSpec(memory_space=pl.ANY)
@@ -529,8 +536,10 @@
         down_kernel,
         out_shape=shape((64, 4096)),
         in_specs=[SM] * 2 + [VM] * 11,
-        out_specs=VM,
-        scratch_shapes=[pltpu.VMEM((256, 128), F32)],
+        out_specs=HB,
+        scratch_shapes=[
+            pltpu.VMEM((256, 128), F32), pltpu.VMEM((64, 4096), BF), pltpu.SemaphoreType.DMA((8,)),
+        ],
         compiler_params=params(32),
         cost_estimate=cost(10**6, 10**5),
         name="down_pass",

time: 60 us -> 60 us (level)
  no operation moved by 1% of the time
where the time goes in v3:
time: 60 us; the launch traced here: 59.5 us
  starting transfers between devices  27.4 us (46%)
  Pallas kernels  22.2 us (37%)
  waiting for transfers between devices  5.98 us (10%)
  local copies, waits for them, and re-layouts  3.51 us (6%)
    ppermute x5, starting transfers between devices, body(): lax.ppermute(x, 'coarse', [(i, i ^ bit) for i in range(coarse)])  13.4 us
    all_to_all x1, starting transfers between devices, body(): r = lax.all_to_all(pay, 'leaf', 0, 0, tiled=True)  7.57 us
    ppermute x4, starting transfers between devices, swap(): return lax.ppermute(x, axis, pairs + [(j, i) for i, j in pairs])  6.44 us
    pallas_call x1, Pallas kernels, body(): pl.pallas_call(near_kernel, out_shape=shape((64, 4096), F32), in_specs=[A...  4.68 us
    pallas_call x1, Pallas kernels, body(): pl.pallas_call(up_kernel, out_shape=[shape((8, 32, 128)), shape((1024, 12...  4.2 us
    pallas_call x1, Pallas kernels, body(): pl.pallas_call(second_layout_kernel, out_shape=[shape((2048, 256)), shape...  4.05 us
    all_to_all x1, waiting for transfers between devices, body(): r = lax.all_to_all(pay, 'leaf', 0, 0, tiled=True)  3.81 us
    unnamed x34, local copies, waits for them, and re-layouts  3.51 us
  transfers between devices with their start and end apart: 10, of which 3 were waited for; matrix products, arithmetic and copies ran while one was open for 0% of the time, Pallas kernels for 26%

profile of v3, /device:TPU:1, one launch (start us, length us, event | category | flops | bytes accessed | tf_op | source)
XLA Modules:
  0.0 59.5 jit_solution(9307747355172362620)
XLA Ops:
  0.0 0.0 copy-start.2
  0.0 4.2 %up_pass.1 = (bf16[8,32,128]{2,1,0:T(8,128)(2,1)}, bf16[1024,128]{1,0:T(8,128)(2,1)}, bf16[128,128]{1,0:T(8,128)(2,1)}, bf16[1152,128]{1,0:T(8,128)(2,1)}, bf16[...) custom-call(bf16[64,4096]{1,0:T(8,128)(2,1)} %v.1, ...), custom_call_target="tpu_custom_call" | custom-call | flops 1000000 | bytes 100000 | tf_op jit(solution)/shard_map/up_pass/pallas_call | solution.py:401
  4.2 0.0 copy-start.1
  4.2 3.3 %collective-permute-start.1 = (bf16[1152,128]{1,0:T(8,128)(2,1)}, bf16[1152,128]{1,0:T(8,128)(2,1)S(1)}, u32[]{:S(2)}, u32[]{:S(2)}) collective-permute-start(bf16[1152,128]{1,0:T(8,128)(2,1)} %get-tuple-element.27), channel_id=1, source_target_pairs={{0,8},{16,24},{32,40},{48,56},{64,72},{80,88},{96,104},{112,120},{... | collective-permute-start | bytes 884744 | tf_op jit(solution)/shard_map/ppermute | solution.py:429
  7.5 1.9 %collective-permute-start.2 = (bf16[1152,128]{1,0:T(8,128)(2,1)}, bf16[1152,128]{1,0:T(8,128)(2,1)S(1)}, u32[]{:S(2)}, u32[]{:S(2)}) collective-permute-start(bf16[1152,128]{1,0:T(8,128)(2,1)} %get-tuple-element.28), channel_id=1, source_target_pairs={{8,16},{24,32},{40,48},{56,64},{72,80},{88,96},{104,112},{120,128}... | collective-permute-start | bytes 884744 | tf_op jit(solution)/shard_map/ppermute | solution.py:429
  9.5 7.6 %all-to-all-start = ((bf16[8,32,128]{2,1,0:T(8,128)(2,1)}), bf16[8,32,128]{2,1,0:T(8,128)(2,1)S(1)}, u32[]{:S(2)}, u32[]{:S(2)}) async-start(bf16[8,32,128]{2,1,0:T(8,128)(2,1)} %get-tuple-element.23), calls=%async_computation | async-start | bytes 131072 | tf_op jit(solution)/shard_map/all_to_all | solution.py:424
  17.0 0.0 copy-start
  17.0 0.0 copy-start.13
  17.0 3.4 %first_layout.1.after.za = bf16[2048,256]{1,0:T(8,128)(2,1)S(1)} custom-call(bf16[16,32,32,64]{3,2,1,0:T(8,128)(2,1)} %s_hbm.3), custom_call_target="tpu_custom_call" | custom-call | flops 1000 | bytes 1000000 | tf_op jit(solution)/shard_map/first_layout/pallas_call | solution.py:434
  20.4 3.8 %all-to-all-done.r = bf16[8,32,128]{2,1,0:T(8,128)(2,1)S(1)} async-done(((bf16[8,32,128]{2,1,0:T(8,128)(2,1)}), bf16[8,32,128]{2,1,0:T(8,128)(2,1)S(1)}, u32[]{:S(2)}, u32[]{:S(2)}) %all-to-all-start) | async-done | bytes 65568 | tf_op jit(solution)/shard_map/all_to_all | solution.py:424
  24.3 0.1 group_sum.1.y
  24.3 1.8 %collective-permute-start = (bf16[144,128]{1,0:T(8,128)(2,1)S(1)}, bf16[144,128]{1,0:T(8,128)(2,1)S(1)}, u32[]{:S(2)}, u32[]{:S(2)}) collective-permute-start(bf16[144,128]{1,0:T(8,128)(2,1)S(1)} %group_sum.1.y), channel_id=1, source_target_pairs={{0,16},{8,24},{16,0},{24,8},{32,48},{40,56},{48,32},{56,40},{64,80... | collective-permute-start | bytes 110600 | tf_op jit(solution)/shard_map/ppermute | solution.py:482
  26.2 0.0 collective-permute-done.1.ra
  26.2 0.0 collective-permute-done.2.rb
  26.2 0.0 copy-done.1
  26.2 0.0 copy-start.6
  26.2 0.9 %copy-done.6 = bf16[1024,128]{1,0:T(8,128)(2,1)S(1)} copy-done((bf16[1024,128]{1,0:T(8,128)(2,1)S(1)}, bf16[1024,128]{1,0:T(8,128)(2,1)}, u32[]{:S(2)}) %copy-start.6) | copy-done | bytes 262168
  27.1 0.0 copy-start.7
  27.1 0.8 %copy-done.7 = bf16[128,128]{1,0:T(8,128)(2,1)S(1)} copy-done((bf16[128,128]{1,0:T(8,128)(2,1)S(1)}, bf16[128,128]{1,0:T(8,128)(2,1)}, u32[]{:S(2)}) %copy-start.7) | copy-done | bytes 32792
  27.9 0.1 halo_pack.1
  28.0 0.0 collective-permute-done.received
  28.0 2.0 %collective-permute-start.3 = (bf16[288,128]{1,0:T(8,128)(2,1)S(1)}, bf16[288,128]{1,0:T(8,128)(2,1)S(1)}, u32[]{:S(2)}, u32[]{:S(2)}) collective-permute-start(bf16[288,128]{1,0:T(8,128)(2,1)S(1)} %table_join.3), channel_id=1, source_target_pairs={{0,32},{8,40},{16,48},{24,56},{32,0},{40,8},{48,16},{56,24},{64,96... | collective-permute-start | bytes 221192 | tf_op jit(solution)/shard_map/ppermute | solution.py:482
  30.0 0.5 collective-permute-start.6
  30.6 0.7 %collective-permute-start.7 = (bf16[2176,128]{1,0:T(8,128)(2,1)S(1)}, bf16[2176,128]{1,0:T(8,128)(2,1)S(1)}, u32[]{:S(2)}, u32[]{:S(2)}) collective-permute-start(bf16[2176,128]{1,0:T(8,128)(2,1)S(1)} %get-tuple-element.32), channel_id=1, source_target_pairs={{1,2},{3,4},{5,6},{2,1},{4,3},{6,5},{9,10},{11,12},{13,14},{10,9},... | collective-permute-start | bytes 1671176 | tf_op jit(solution)/shard_map/ppermute | solution.py:429
  31.3 1.5 %collective-permute-done.3 = bf16[288,128]{1,0:T(8,128)(2,1)S(1)} collective-permute-done((bf16[288,128]{1,0:T(8,128)(2,1)S(1)}, bf16[288,128]{1,0:T(8,128)(2,1)S(1)}, u32[]{:S(2)}, u32[]{:S(2)}) %collective-permute-start.3) | collective-permute-done | bytes 73760 | tf_op jit(solution)/shard_map/ppermute | solution.py:482
  32.8 1.4 %collective-permute-start.4 = (bf16[576,128]{1,0:T(8,128)(2,1)S(1)}, bf16[576,128]{1,0:T(8,128)(2,1)S(1)}, u32[]{:S(2)}, u32[]{:S(2)}) collective-permute-start(bf16[576,128]{1,0:T(8,128)(2,1)S(1)} %pad_maximum_fusion.y), channel_id=1, source_target_pairs={{0,64},{8,72},{16,80},{24,88},{32,96},{40,104},{48,112},{56,120},{... | collective-permute-start | bytes 442376 | tf_op jit(solution)/shard_map/ppermute | solution.py:482
  34.2 0.0 copy-done.2
  34.2 0.0 copy-start.9
  34.2 0.9 %copy-done.9 = bf16[16,32,32,1]{2,1,3,0:T(8,128)(2,1)S(1)} copy-done((bf16[16,32,32,1]{2,1,3,0:T(8,128)(2,1)S(1)}, bf16[16,32,32,1]{2,1,3,0:T(8,128)(2,1)}, u32[]{:S(2)}) %copy-start.9) | copy-done | bytes 32792
  35.1 0.0 copy-start.10
  35.1 0.8 %copy-done.10 = bf16[8,32,32,1]{2,1,3,0:T(8,128)(2,1)S(1)} copy-done((bf16[8,32,32,1]{2,1,3,0:T(8,128)(2,1)S(1)}, bf16[8,32,32,1]{2,1,3,0:T(8,128)(2,1)}, u32[]{:S(2)}) %copy-start.10) | copy-done | bytes 16408
  35.9 4.1 %second_layout.1 = (bf16[2048,256]{1,0:T(8,128)(2,1)S(1)}, bf16[256,512]{1,0:T(8,128)(2,1)S(1)}, bf16[32,512]{1,0:T(8,128)(2,1)S(1)}, bf16[32,256]{1,0:T(8,128)(2,1)S(1)}) custom-call(bf16[16,32,32,64]{3,2,1,0:T(8,128)(2,1)} %s_hbm.3, bf16[16,32,8,32]{3,2,1,0:T(8,128)(2,1)S(1)} %bitcast.11, bf16[16,32,32]{2,1,0:T(8,128)(2,1)S(1)} %bitcast.14, ...), custom_call_target="tpu_custom_call" | custom-call | flops 1000 | bytes 1000000 | tf_op jit(solution)/shard_map/second_layout/pallas_call | solution.py:444
  40.0 0.0 collective-permute-done.4.received
  40.0 0.0 copy-start.8
  40.0 0.0 copy-start.12
  40.0 0.0 copy-start.14
  40.1 2.7 %collective-permute-start.5 = (bf16[1152,128]{1,0:T(8,128)(2,1)S(1)}, bf16[1152,128]{1,0:T(8,128)(2,1)S(1)}, u32[]{:S(2)}, u32[]{:S(2)}) collective-permute-start(bf16[1152,128]{1,0:T(8,128)(2,1)S(1)} %table_join.4.y), channel_id=1, source_target_pairs={{0,128},{8,136},{16,144},{24,152},{32,160},{40,168},{48,176},{56,1... | collective-permute-start | bytes 884744 | tf_op jit(solution)/shard_map/ppermute | solution.py:482
  42.8 0.0 collective-permute-done.7.qb
  42.8 0.0 collective-permute-done.6.qa
  42.8 0.0 copy-done
  42.8 0.0 copy-done.13
  42.8 0.0 copy-start.3
  42.8 0.0 copy-start.4
  42.8 0.0 copy-start.5
  42.8 0.0 copy-start.11
  42.9 0.0 copy-start.15
  42.9 0.0 copy-start.16
  42.9 4.7 %near_field.1.after.near = f32[64,4096]{1,0:T(8,128)S(1)} custom-call(s32[12,64]{1,0:T(8,128)S(1)} %copy-done.13, bf16[64,4096]{1,0:T(8,128)(2,1)S(1)} %copy-done, bf16[1152,128]{1,0:T(8,128)(2,1)S(1)} %collective-permute-done.1.ra, bf16[1152,128]{1,0:T(8,128)(2,1)S(1)} %collective-permute-done.2.rb, bf16[2176,128]{1,0:T(8,128)(2,1)S(1)} %collective-permute-done.6.qa, ...), custom_call_target="tpu_custom_call" | custom-call | flops 1000 | bytes 1000000 | tf_op jit(solution)/shard_map/near_field/pallas_call | solution.py:500
  47.6 0.6 %collective-permute-done.5.received = bf16[1152,128]{1,0:T(8,128)(2,1)S(1)} collective-permute-done((bf16[1152,128]{1,0:T(8,128)(2,1)S(1)}, bf16[1152,128]{1,0:T(8,128)(2,1)S(1)}, u32[]{:S(2)}, u32[]{:S(2)}) %collective-permute-start.5) | collective-permute-done | bytes 294944 | tf_op jit(solution)/shard_map/ppermute | solution.py:482
  48.2 5.4 %collective-permute-start.8 = (bf16[2304,128]{1,0:T(8,128)(2,1)S(1)}, bf16[2304,128]{1,0:T(8,128)(2,1)S(1)}, u32[]{:S(2)}, u32[]{:S(2)}) collective-permute-start(bf16[2304,128]{1,0:T(8,128)(2,1)S(1)} %table_join.5.own), channel_id=1, source_target_pairs={{0,8},{8,0},{16,24},{24,16},{32,40},{40,32},{48,56},{56,48},{64,72... | collective-permute-start | bytes 1769480 | tf_op jit(solution)/shard_map/ppermute | solution.py:482
  53.7 0.0 copy-done.8
  53.7 0.0 copy-done.12
  53.7 0.0 copy-done.14
  53.7 3.1 %far_field.1 = (f32[2048,128]{1,0:T(8,128)S(1)}, f32[256,128]{1,0:T(8,128)S(1)}) custom-call(s32[16,64]{1,0:T(8,128)S(1)} %copy-done.12, s32[8,16]{1,0:T(8,128)S(1)} %copy-done.14, bf16[1024,128]{1,0:T(8,128)(2,1)S(1)} %copy-done.1, bf16[128,128]{1,0:T(8,128)(2,1)S(1)} %copy-done.8, bf16[1152,128]{1,0:T(8,128)(2,1)S(1)} %collective-permute-done.1.ra, ...), custom_call_target="tpu_custom_call" | custom-call | flops 1000 | bytes 1000000 | tf_op jit(solution)/shard_map/far_field/pallas_call | solution.py:518
  56.8 0.0 collective-permute-done.8.other
  56.8 0.0 copy-done.3
  56.8 0.0 copy-done.4
  56.8 0.0 copy-done.5
  56.8 0.0 copy-done.11
  56.8 0.0 copy-done.15
  56.8 0.0 copy-done.16
  56.9 2.5 %down_pass.1 = bf16[64,4096]{1,0:T(8,128)(2,1)} custom-call(s32[1,16]{1,0:T(1,128)S(1)} %bitcast.18, s32[1,8]{1,0:T(1,128)S(1)} %bitcast.19, bf16[2304,128]{1,0:T(8,128)(2,1)S(1)} %table_join.5.own, bf16[2304,128]{1,0:T(8,128)(2,1)S(1)} %collective-permute-done.8.other, bf16[32,512]{1,0:T(8,128)(2,1)S(1)} %get-tuple-element.33.zd, ...), custom_call_target="tpu_custom_call" | custom-call | flops 1000000 | bytes 100000 | tf_op jit(solution)/shard_map/down_pass/pallas_call | solution.py:535
  (4 shorter events, 0.1 us)
Async XLA Ops:
  0.0 34.2 %copy-start.2 = (bf16[16,32,32,8]{2,3,1,0:T(8,128)(2,1)S(1)}, bf16[16,32,32,8]{2,3,1,0:T(8,128)(2,1)}, u32[]{:S(2)}) copy-start(bf16[16,32,32,8]{2,3,1,0:T(8,128)(2,1)} %param.25) | copy-start | bytes 786436
  4.2 22.0 %copy-start.1 = (bf16[1024,128]{1,0:T(8,128)(2,1)S(1)}, bf16[1024,128]{1,0:T(8,128)(2,1)}, u32[]{:S(2)}) copy-start(bf16[1024,128]{1,0:T(8,128)(2,1)} %get-tuple-element.25.cown) | copy-start | bytes 786436
  4.2 22.0 %collective-permute-start.1 = (bf16[1152,128]{1,0:T(8,128)(2,1)}, bf16[1152,128]{1,0:T(8,128)(2,1)S(1)}, u32[]{:S(2)}, u32[]{:S(2)}) collective-permute-start(bf16[1152,128]{1,0:T(8,128)(2,1)} %get-tuple-element.27), channel_id=1, source_target_pairs={{0,8},{16,24},{32,40},{48,56},{64,72},{80,88},{96,104},{112,120},{... | collective-permute-start | bytes 884744 | tf_op jit(solution)/shard_map/ppermute | solution.py:429
  7.5 18.6 %collective-permute-start.2 = (bf16[1152,128]{1,0:T(8,128)(2,1)}, bf16[1152,128]{1,0:T(8,128)(2,1)S(1)}, u32[]{:S(2)}, u32[]{:S(2)}) collective-permute-start(bf16[1152,128]{1,0:T(8,128)(2,1)} %get-tuple-element.28), channel_id=1, source_target_pairs={{8,16},{24,32},{40,48},{56,64},{72,80},{88,96},{104,112},{120,128}... | collective-permute-start | bytes 884744 | tf_op jit(solution)/shard_map/ppermute | solution.py:429
  9.5 14.8 %all-to-all-start = ((bf16[8,32,128]{2,1,0:T(8,128)(2,1)}), bf16[8,32,128]{2,1,0:T(8,128)(2,1)S(1)}, u32[]{:S(2)}, u32[]{:S(2)}) async-start(bf16[8,32,128]{2,1,0:T(8,128)(2,1)} %get-tuple-element.23), calls=%async_computation | async-start | bytes 131072 | tf_op jit(solution)/shard_map/all_to_all | solution.py:424
  17.0 25.8 %copy-start = (bf16[64,4096]{1,0:T(8,128)(2,1)S(1)}, bf16[64,4096]{1,0:T(8,128)(2,1)}, u32[]{:S(2)}) copy-start(bf16[64,4096]{1,0:T(8,128)(2,1)} %v.1) | copy-start | bytes 1572868
  17.0 25.8 %copy-start.13 = (s32[12,64]{1,0:T(8,128)S(1)}, s32[12,64]{1,0:T(8,128)}, u32[]{:S(2)}) copy-start(s32[12,64]{1,0:T(8,128)} %get-tuple-element.31.ix_any) | copy-start | bytes 9220
  24.3 3.6 %collective-permute-start = (bf16[144,128]{1,0:T(8,128)(2,1)S(1)}, bf16[144,128]{1,0:T(8,128)(2,1)S(1)}, u32[]{:S(2)}, u32[]{:S(2)}) collective-permute-start(bf16[144,128]{1,0:T(8,128)(2,1)S(1)} %group_sum.1.y), channel_id=1, source_target_pairs={{0,16},{8,24},{16,0},{24,8},{32,48},{40,56},{48,32},{56,40},{64,80... | collective-permute-start | bytes 110600 | tf_op jit(solution)/shard_map/ppermute | solution.py:482
  26.2 1.0 %copy-start.6 = (bf16[1024,128]{1,0:T(8,128)(2,1)S(1)}, bf16[1024,128]{1,0:T(8,128)(2,1)}, u32[]{:S(2)}) copy-start(bf16[1024,128]{1,0:T(8,128)(2,1)} %get-tuple-element.24.faces) | copy-start | bytes 786436
  27.1 0.8 %copy-start.7 = (bf16[128,128]{1,0:T(8,128)(2,1)S(1)}, bf16[128,128]{1,0:T(8,128)(2,1)}, u32[]{:S(2)}) copy-start(bf16[128,128]{1,0:T(8,128)(2,1)} %get-tuple-element.26.nown) | copy-start | bytes 98308
  28.0 4.8 %collective-permute-start.3 = (bf16[288,128]{1,0:T(8,128)(2,1)S(1)}, bf16[288,128]{1,0:T(8,128)(2,1)S(1)}, u32[]{:S(2)}, u32[]{:S(2)}) collective-permute-start(bf16[288,128]{1,0:T(8,128)(2,1)S(1)} %table_join.3), channel_id=1, source_target_pairs={{0,32},{8,40},{16,48},{24,56},{32,0},{40,8},{48,16},{56,24},{64,96... | collective-permute-start | bytes 221192 | tf_op jit(solution)/shard_map/ppermute | solution.py:482
  30.0 12.7 %collective-permute-start.6 = (bf16[2176,128]{1,0:T(8,128)(2,1)S(1)}, bf16[2176,128]{1,0:T(8,128)(2,1)S(1)}, u32[]{:S(2)}, u32[]{:S(2)}) collective-permute-start(bf16[2176,128]{1,0:T(8,128)(2,1)S(1)} %get-tuple-element.29.after), channel_id=1, source_target_pairs={{0,1},{2,3},{4,5},{6,7},{1,0},{3,2},{5,4},{7,6},{8,9},{10,11},{12,... | collective-permute-start | bytes 1671176 | tf_op jit(solution)/shard_map/ppermute | solution.py:429
  30.6 12.2 %collective-permute-start.7 = (bf16[2176,128]{1,0:T(8,128)(2,1)S(1)}, bf16[2176,128]{1,0:T(8,128)(2,1)S(1)}, u32[]{:S(2)}, u32[]{:S(2)}) collective-permute-start(bf16[2176,128]{1,0:T(8,128)(2,1)S(1)} %get-tuple-element.32), channel_id=1, source_target_pairs={{1,2},{3,4},{5,6},{2,1},{4,3},{6,5},{9,10},{11,12},{13,14},{10,9},... | collective-permute-start | bytes 1671176 | tf_op jit(solution)/shard_map/ppermute | solution.py:429
  32.8 7.2 %collective-permute-start.4 = (bf16[576,128]{1,0:T(8,128)(2,1)S(1)}, bf16[576,128]{1,0:T(8,128)(2,1)S(1)}, u32[]{:S(2)}, u32[]{:S(2)}) collective-permute-start(bf16[576,128]{1,0:T(8,128)(2,1)S(1)} %pad_maximum_fusion.y), channel_id=1, source_target_pairs={{0,64},{8,72},{16,80},{24,88},{32,96},{40,104},{48,112},{56,120},{... | collective-permute-start | bytes 442376 | tf_op jit(solution)/shard_map/ppermute | solution.py:482
  34.2 0.9 %copy-start.9 = (bf16[16,32,32,1]{2,1,3,0:T(8,128)(2,1)S(1)}, bf16[16,32,32,1]{2,1,3,0:T(8,128)(2,1)}, u32[]{:S(2)}) copy-start(bf16[16,32,32,1]{2,1,3,0:T(8,128)(2,1)} %param.27) | copy-start | bytes 98308
  35.1 0.8 %copy-start.10 = (bf16[8,32,32,1]{2,1,3,0:T(8,128)(2,1)S(1)}, bf16[8,32,32,1]{2,1,3,0:T(8,128)(2,1)}, u32[]{:S(2)}) copy-start(bf16[8,32,32,1]{2,1,3,0:T(8,128)(2,1)} %param.29) | copy-start | bytes 49156
  40.0 13.6 %copy-start.8 = (bf16[128,128]{1,0:T(8,128)(2,1)S(1)}, bf16[128,128]{1,0:T(8,128)(2,1)}, u32[]{:S(2)}) copy-start(bf16[128,128]{1,0:T(8,128)(2,1)} %get-tuple-element.26.nown) | copy-start | bytes 98308
  40.0 13.6 %copy-start.12 = (s32[16,64]{1,0:T(8,128)S(1)}, s32[16,64]{1,0:T(8,128)}, u32[]{:S(2)}) copy-start(s32[16,64]{1,0:T(8,128)} %get-tuple-element.36.li_any) | copy-start | bytes 12292
  40.0 13.6 %copy-start.14 = (s32[8,16]{1,0:T(8,128)S(1)}, s32[8,16]{1,0:T(8,128)}, u32[]{:S(2)}) copy-start(s32[8,16]{1,0:T(8,128)} %get-tuple-element.37.mi_any) | copy-start | bytes 1540
  40.1 8.1 %collective-permute-start.5 = (bf16[1152,128]{1,0:T(8,128)(2,1)S(1)}, bf16[1152,128]{1,0:T(8,128)(2,1)S(1)}, u32[]{:S(2)}, u32[]{:S(2)}) collective-permute-start(bf16[1152,128]{1,0:T(8,128)(2,1)S(1)} %table_join.4.y), channel_id=1, source_target_pairs={{0,128},{8,136},{16,144},{24,152},{32,160},{40,168},{48,176},{56,1... | collective-permute-start | bytes 884744 | tf_op jit(solution)/shard_map/ppermute | solution.py:482
  42.8 14.0 %copy-start.3 = (bf16[32,4096]{1,0:T(8,128)(2,1)S(1)}, bf16[32,4096]{1,0:T(8,128)(2,1)}, u32[]{:S(2)}) copy-start(bf16[32,4096]{1,0:T(8,128)(2,1)} %b.1) | copy-start | bytes 786436
  42.8 14.0 %copy-start.4 = (bf16[2048,128]{1,0:T(8,128)(2,1)S(1)}, bf16[2048,128]{1,0:T(8,128)(2,1)}, u32[]{:S(2)}) copy-start(bf16[2048,128]{1,0:T(8,128)(2,1)} %get-tuple-element.35.tl) | copy-start | bytes 1572868
  42.8 14.0 %copy-start.5 = (bf16[32,32,8]{1,2,0:T(8,128)(2,1)S(1)}, bf16[32,32,8]{1,2,0:T(8,128)(2,1)}, u32[]{:S(2)}) copy-start(bf16[32,32,8]{1,2,0:T(8,128)(2,1)} %param.20) | copy-start | bytes 49156
  42.8 14.0 %copy-start.11 = (bf16[32,32,1]{1,0,2:T(8,128)(2,1)S(1)}, bf16[32,32,1]{1,0,2:T(8,128)(2,1)}, u32[]{:S(2)}) copy-start(bf16[32,32,1]{1,0,2:T(8,128)(2,1)} %param.21) | copy-start | bytes 6148
  42.9 14.0 %copy-start.15 = (s32[16,1]{0,1:T(1,128)S(1)}, s32[16,1]{0,1:T(1,128)}, u32[]{:S(2)}) copy-start(s32[16,1]{0,1:T(1,128)} %param.26) | copy-start | bytes 196
  42.9 14.0 %copy-start.16 = (s32[8,1]{0,1:T(1,128)S(1)}, s32[8,1]{0,1:T(1,128)}, u32[]{:S(2)}) copy-start(s32[8,1]{0,1:T(1,128)} %param.28) | copy-start | bytes 100
  48.2 8.6 %collective-permute-start.8 = (bf16[2304,128]{1,0:T(8,128)(2,1)S(1)}, bf16[2304,128]{1,0:T(8,128)(2,1)S(1)}, u32[]{:S(2)}, u32[]{:S(2)}) collective-permute-start(bf16[2304,128]{1,0:T(8,128)(2,1)S(1)} %table_join.5.own), channel_id=1, source_target_pairs={{0,8},{8,0},{16,24},{24,16},{32,40},{40,32},{48,56},{56,48},{64,72... | collective-permute-start | bytes 1769480 | tf_op jit(solution)/shard_map/ppermute | solution.py:482

commit v4 on v3

--- a/solution.py
+++ b/solution.py
@@ -256,7 +256,7 @@
             out[:, lanes] = jnp.where(mask, r[:64], r[64:])
         return carry
 
-    lax.fori_loop(0, 8, chunk, 0, unroll=2)
+    lax.fori_loop(0, 8, chunk, 0, unroll=4)
 
 
 def far_kernel(

time: 60 us -> 60 us (level)
  no operation moved by 1% of the time
where the time goes in v4:
time: 60 us; the launch traced here: 59.5 us
  starting transfers between devices  27.4 us (46%)
  Pallas kernels  22.2 us (37%)
  waiting for transfers between devices  5.97 us (10%)
  local copies, waits for them, and re-layouts  3.51 us (6%)
    ppermute x5, starting transfers between devices, body(): lax.ppermute(x, 'coarse', [(i, i ^ bit) for i in range(coarse)])  13.4 us
    all_to_all x1, starting transfers between devices, body(): r = lax.all_to_all(pay, 'leaf', 0, 0, tiled=True)  7.57 us
    ppermute x4, starting transfers between devices, swap(): return lax.ppermute(x, axis, pairs + [(j, i) for i, j in pairs])  6.44 us
    pallas_call x1, Pallas kernels, body(): pl.pallas_call(near_kernel, out_shape=shape((64, 4096), F32), in_specs=[A...  4.69 us
    pallas_call x1, Pallas kernels, body(): pl.pallas_call(up_kernel, out_shape=[shape((8, 32, 128)), shape((1024, 12...  4.2 us
    pallas_call x1, Pallas kernels, body(): pl.pallas_call(second_layout_kernel, out_shape=[shape((2048, 256)), shape...  4.05 us
    all_to_all x1, waiting for transfers between devices, body(): r = lax.all_to_all(pay, 'leaf', 0, 0, tiled=True)  3.81 us
    unnamed x34, local copies, waits for them, and re-layouts  3.51 us
  transfers between devices with their start and end apart: 10, of which 3 were waited for; matrix products, arithmetic and copies ran while one was open for 0% of the time, Pallas kernels for 26%

profile of v4, /device:TPU:1, one launch (start us, length us, event | category | flops | bytes accessed | tf_op | source)
XLA Modules:
  0.0 59.5 jit_solution(6918755782116187250)
XLA Ops:
  0.0 0.0 copy-start.2
  0.0 4.2 %up_pass.1 = (bf16[8,32,128]{2,1,0:T(8,128)(2,1)}, bf16[1024,128]{1,0:T(8,128)(2,1)}, bf16[128,128]{1,0:T(8,128)(2,1)}, bf16[1152,128]{1,0:T(8,128)(2,1)}, bf16[...) custom-call(bf16[64,4096]{1,0:T(8,128)(2,1)} %v.1, ...), custom_call_target="tpu_custom_call" | custom-call | flops 1000000 | bytes 100000 | tf_op jit(solution)/shard_map/up_pass/pallas_call | solution.py:401
  4.2 0.0 copy-start.1
  4.2 3.3 %collective-permute-start.1 = (bf16[1152,128]{1,0:T(8,128)(2,1)}, bf16[1152,128]{1,0:T(8,128)(2,1)S(1)}, u32[]{:S(2)}, u32[]{:S(2)}) collective-permute-start(bf16[1152,128]{1,0:T(8,128)(2,1)} %get-tuple-element.27), channel_id=1, source_target_pairs={{0,8},{16,24},{32,40},{48,56},{64,72},{80,88},{96,104},{112,120},{... | collective-permute-start | bytes 884744 | tf_op jit(solution)/shard_map/ppermute | solution.py:429
  7.5 1.9 %collective-permute-start.2 = (bf16[1152,128]{1,0:T(8,128)(2,1)}, bf16[1152,128]{1,0:T(8,128)(2,1)S(1)}, u32[]{:S(2)}, u32[]{:S(2)}) collective-permute-start(bf16[1152,128]{1,0:T(8,128)(2,1)} %get-tuple-element.28), channel_id=1, source_target_pairs={{8,16},{24,32},{40,48},{56,64},{72,80},{88,96},{104,112},{120,128}... | collective-permute-start | bytes 884744 | tf_op jit(solution)/shard_map/ppermute | solution.py:429
  9.5 7.6 %all-to-all-start = ((bf16[8,32,128]{2,1,0:T(8,128)(2,1)}), bf16[8,32,128]{2,1,0:T(8,128)(2,1)S(1)}, u32[]{:S(2)}, u32[]{:S(2)}) async-start(bf16[8,32,128]{2,1,0:T(8,128)(2,1)} %get-tuple-element.23), calls=%async_computation | async-start | bytes 131072 | tf_op jit(solution)/shard_map/all_to_all | solution.py:424
  17.0 0.0 copy-start
  17.0 0.0 copy-start.13
  17.0 3.4 %first_layout.1.after.za = bf16[2048,256]{1,0:T(8,128)(2,1)S(1)} custom-call(bf16[16,32,32,64]{3,2,1,0:T(8,128)(2,1)} %s_hbm.3), custom_call_target="tpu_custom_call" | custom-call | flops 1000 | bytes 1000000 | tf_op jit(solution)/shard_map/first_layout/pallas_call | solution.py:434
  20.4 3.8 %all-to-all-done.r = bf16[8,32,128]{2,1,0:T(8,128)(2,1)S(1)} async-done(((bf16[8,32,128]{2,1,0:T(8,128)(2,1)}), bf16[8,32,128]{2,1,0:T(8,128)(2,1)S(1)}, u32[]{:S(2)}, u32[]{:S(2)}) %all-to-all-start) | async-done | bytes 65568 | tf_op jit(solution)/shard_map/all_to_all | solution.py:424
  24.3 0.1 group_sum.1.y
  24.3 1.8 %collective-permute-start = (bf16[144,128]{1,0:T(8,128)(2,1)S(1)}, bf16[144,128]{1,0:T(8,128)(2,1)S(1)}, u32[]{:S(2)}, u32[]{:S(2)}) collective-permute-start(bf16[144,128]{1,0:T(8,128)(2,1)S(1)} %group_sum.1.y), channel_id=1, source_target_pairs={{0,16},{8,24},{16,0},{24,8},{32,48},{40,56},{48,32},{56,40},{64,80... | collective-permute-start | bytes 110600 | tf_op jit(solution)/shard_map/ppermute | solution.py:482
  26.2 0.0 collective-permute-done.1.ra
  26.2 0.0 collective-permute-done.2.rb
  26.2 0.0 copy-done.1
  26.2 0.0 copy-start.6
  26.2 0.9 %copy-done.6 = bf16[1024,128]{1,0:T(8,128)(2,1)S(1)} copy-done((bf16[1024,128]{1,0:T(8,128)(2,1)S(1)}, bf16[1024,128]{1,0:T(8,128)(2,1)}, u32[]{:S(2)}) %copy-start.6) | copy-done | bytes 262168
  27.1 0.0 copy-start.7
  27.1 0.8 %copy-done.7 = bf16[128,128]{1,0:T(8,128)(2,1)S(1)} copy-done((bf16[128,128]{1,0:T(8,128)(2,1)S(1)}, bf16[128,128]{1,0:T(8,128)(2,1)}, u32[]{:S(2)}) %copy-start.7) | copy-done | bytes 32792
  27.9 0.1 halo_pack.1
  28.0 0.0 collective-permute-done.received
  28.0 2.0 %collective-permute-start.3 = (bf16[288,128]{1,0:T(8,128)(2,1)S(1)}, bf16[288,128]{1,0:T(8,128)(2,1)S(1)}, u32[]{:S(2)}, u32[]{:S(2)}) collective-permute-start(bf16[288,128]{1,0:T(8,128)(2,1)S(1)} %table_join.3), channel_id=1, source_target_pairs={{0,32},{8,40},{16,48},{24,56},{32,0},{40,8},{48,16},{56,24},{64,96... | collective-permute-start | bytes 221192 | tf_op jit(solution)/shard_map/ppermute | solution.py:482
  30.0 0.5 collective-permute-start.6
  30.6 0.7 %collective-permute-start.7 = (bf16[2176,128]{1,0:T(8,128)(2,1)S(1)}, bf16[2176,128]{1,0:T(8,128)(2,1)S(1)}, u32[]{:S(2)}, u32[]{:S(2)}) collective-permute-start(bf16[2176,128]{1,0:T(8,128)(2,1)S(1)} %get-tuple-element.32), channel_id=1, source_target_pairs={{1,2},{3,4},{5,6},{2,1},{4,3},{6,5},{9,10},{11,12},{13,14},{10,9},... | collective-permute-start | bytes 1671176 | tf_op jit(solution)/shard_map/ppermute | solution.py:429
  31.3 1.5 %collective-permute-done.3 = bf16[288,128]{1,0:T(8,128)(2,1)S(1)} collective-permute-done((bf16[288,128]{1,0:T(8,128)(2,1)S(1)}, bf16[288,128]{1,0:T(8,128)(2,1)S(1)}, u32[]{:S(2)}, u32[]{:S(2)}) %collective-permute-start.3) | collective-permute-done | bytes 73760 | tf_op jit(solution)/shard_map/ppermute | solution.py:482
  32.8 1.4 %collective-permute-start.4 = (bf16[576,128]{1,0:T(8,128)(2,1)S(1)}, bf16[576,128]{1,0:T(8,128)(2,1)S(1)}, u32[]{:S(2)}, u32[]{:S(2)}) collective-permute-start(bf16[576,128]{1,0:T(8,128)(2,1)S(1)} %pad_maximum_fusion.y), channel_id=1, source_target_pairs={{0,64},{8,72},{16,80},{24,88},{32,96},{40,104},{48,112},{56,120},{... | collective-permute-start | bytes 442376 | tf_op jit(solution)/shard_map/ppermute | solution.py:482
  34.2 0.0 copy-done.2
  34.2 0.0 copy-start.9
  34.2 0.9 %copy-done.9 = bf16[16,32,32,1]{2,1,3,0:T(8,128)(2,1)S(1)} copy-done((bf16[16,32,32,1]{2,1,3,0:T(8,128)(2,1)S(1)}, bf16[16,32,32,1]{2,1,3,0:T(8,128)(2,1)}, u32[]{:S(2)}) %copy-start.9) | copy-done | bytes 32792
  35.1 0.0 copy-start.10
  35.1 0.8 %copy-done.10 = bf16[8,32,32,1]{2,1,3,0:T(8,128)(2,1)S(1)} copy-done((bf16[8,32,32,1]{2,1,3,0:T(8,128)(2,1)S(1)}, bf16[8,32,32,1]{2,1,3,0:T(8,128)(2,1)}, u32[]{:S(2)}) %copy-start.10) | copy-done | bytes 16408
  35.9 4.1 %second_layout.1 = (bf16[2048,256]{1,0:T(8,128)(2,1)S(1)}, bf16[256,512]{1,0:T(8,128)(2,1)S(1)}, bf16[32,512]{1,0:T(8,128)(2,1)S(1)}, bf16[32,256]{1,0:T(8,128)(2,1)S(1)}) custom-call(bf16[16,32,32,64]{3,2,1,0:T(8,128)(2,1)} %s_hbm.3, bf16[16,32,8,32]{3,2,1,0:T(8,128)(2,1)S(1)} %bitcast.11, bf16[16,32,32]{2,1,0:T(8,128)(2,1)S(1)} %bitcast.14, ...), custom_call_target="tpu_custom_call" | custom-call | flops 1000 | bytes 1000000 | tf_op jit(solution)/shard_map/second_layout/pallas_call | solution.py:444
  40.0 0.0 collective-permute-done.4.received
  40.0 0.0 copy-start.8
  40.0 0.0 copy-start.12
  40.0 0.0 copy-start.14
  40.1 2.7 %collective-permute-start.5 = (bf16[1152,128]{1,0:T(8,128)(2,1)S(1)}, bf16[1152,128]{1,0:T(8,128)(2,1)S(1)}, u32[]{:S(2)}, u32[]{:S(2)}) collective-permute-start(bf16[1152,128]{1,0:T(8,128)(2,1)S(1)} %table_join.4.y), channel_id=1, source_target_pairs={{0,128},{8,136},{16,144},{24,152},{32,160},{40,168},{48,176},{56,1... | collective-permute-start | bytes 884744 | tf_op jit(solution)/shard_map/ppermute | solution.py:482
  42.8 0.0 collective-permute-done.7.qb
  42.8 0.0 collective-permute-done.6.qa
  42.8 0.0 copy-done
  42.8 0.0 copy-done.13
  42.8 0.0 copy-start.3
  42.8 0.0 copy-start.4
  42.8 0.0 copy-start.5
  42.8 0.0 copy-start.11
  42.9 0.0 copy-start.15
  42.9 0.0 copy-start.16
  42.9 4.7 %near_field.1.after.near = f32[64,4096]{1,0:T(8,128)S(1)} custom-call(s32[12,64]{1,0:T(8,128)S(1)} %copy-done.13, bf16[64,4096]{1,0:T(8,128)(2,1)S(1)} %copy-done, bf16[1152,128]{1,0:T(8,128)(2,1)S(1)} %collective-permute-done.1.ra, bf16[1152,128]{1,0:T(8,128)(2,1)S(1)} %collective-permute-done.2.rb, bf16[2176,128]{1,0:T(8,128)(2,1)S(1)} %collective-permute-done.6.qa, ...), custom_call_target="tpu_custom_call" | custom-call | flops 1000 | bytes 1000000 | tf_op jit(solution)/shard_map/near_field/pallas_call | solution.py:500
  47.6 0.6 %collective-permute-done.5.received = bf16[1152,128]{1,0:T(8,128)(2,1)S(1)} collective-permute-done((bf16[1152,128]{1,0:T(8,128)(2,1)S(1)}, bf16[1152,128]{1,0:T(8,128)(2,1)S(1)}, u32[]{:S(2)}, u32[]{:S(2)}) %collective-permute-start.5) | collective-permute-done | bytes 294944 | tf_op jit(solution)/shard_map/ppermute | solution.py:482
  48.2 5.4 %collective-permute-start.8 = (bf16[2304,128]{1,0:T(8,128)(2,1)S(1)}, bf16[2304,128]{1,0:T(8,128)(2,1)S(1)}, u32[]{:S(2)}, u32[]{:S(2)}) collective-permute-start(bf16[2304,128]{1,0:T(8,128)(2,1)S(1)} %table_join.5.own), channel_id=1, source_target_pairs={{0,8},{8,0},{16,24},{24,16},{32,40},{40,32},{48,56},{56,48},{64,72... | collective-permute-start | bytes 1769480 | tf_op jit(solution)/shard_map/ppermute | solution.py:482
  53.7 0.0 copy-done.8
  53.7 0.0 copy-done.12
  53.7 0.0 copy-done.14
  53.7 3.1 %far_field.1 = (f32[2048,128]{1,0:T(8,128)S(1)}, f32[256,128]{1,0:T(8,128)S(1)}) custom-call(s32[16,64]{1,0:T(8,128)S(1)} %copy-done.12, s32[8,16]{1,0:T(8,128)S(1)} %copy-done.14, bf16[1024,128]{1,0:T(8,128)(2,1)S(1)} %copy-done.1, bf16[128,128]{1,0:T(8,128)(2,1)S(1)} %copy-done.8, bf16[1152,128]{1,0:T(8,128)(2,1)S(1)} %collective-permute-done.1.ra, ...), custom_call_target="tpu_custom_call" | custom-call | flops 1000 | bytes 1000000 | tf_op jit(solution)/shard_map/far_field/pallas_call | solution.py:518
  56.8 0.0 collective-permute-done.8.other
  56.8 0.0 copy-done.3
  56.8 0.0 copy-done.4
  56.8 0.0 copy-done.5
  56.8 0.0 copy-done.11
  56.8 0.0 copy-done.15
  56.8 0.0 copy-done.16
  56.8 2.5 %down_pass.1 = bf16[64,4096]{1,0:T(8,128)(2,1)} custom-call(s32[1,16]{1,0:T(1,128)S(1)} %bitcast.18, s32[1,8]{1,0:T(1,128)S(1)} %bitcast.19, bf16[2304,128]{1,0:T(8,128)(2,1)S(1)} %table_join.5.own, bf16[2304,128]{1,0:T(8,128)(2,1)S(1)} %collective-permute-done.8.other, bf16[32,512]{1,0:T(8,128)(2,1)S(1)} %get-tuple-element.33.zd, ...), custom_call_target="tpu_custom_call" | custom-call | flops 1000000 | bytes 100000 | tf_op jit(solution)/shard_map/down_pass/pallas_call | solution.py:535
  (4 shorter events, 0.1 us)
Async XLA Ops:
  0.0 34.2 %copy-start.2 = (bf16[16,32,32,8]{2,3,1,0:T(8,128)(2,1)S(1)}, bf16[16,32,32,8]{2,3,1,0:T(8,128)(2,1)}, u32[]{:S(2)}) copy-start(bf16[16,32,32,8]{2,3,1,0:T(8,128)(2,1)} %param.25) | copy-start | bytes 786436
  4.2 22.0 %copy-start.1 = (bf16[1024,128]{1,0:T(8,128)(2,1)S(1)}, bf16[1024,128]{1,0:T(8,128)(2,1)}, u32[]{:S(2)}) copy-start(bf16[1024,128]{1,0:T(8,128)(2,1)} %get-tuple-element.25.cown) | copy-start | bytes 786436
  4.2 22.0 %collective-permute-start.1 = (bf16[1152,128]{1,0:T(8,128)(2,1)}, bf16[1152,128]{1,0:T(8,128)(2,1)S(1)}, u32[]{:S(2)}, u32[]{:S(2)}) collective-permute-start(bf16[1152,128]{1,0:T(8,128)(2,1)} %get-tuple-element.27), channel_id=1, source_target_pairs={{0,8},{16,24},{32,40},{48,56},{64,72},{80,88},{96,104},{112,120},{... | collective-permute-start | bytes 884744 | tf_op jit(solution)/shard_map/ppermute | solution.py:429
  7.5 18.6 %collective-permute-start.2 = (bf16[1152,128]{1,0:T(8,128)(2,1)}, bf16[1152,128]{1,0:T(8,128)(2,1)S(1)}, u32[]{:S(2)}, u32[]{:S(2)}) collective-permute-start(bf16[1152,128]{1,0:T(8,128)(2,1)} %get-tuple-element.28), channel_id=1, source_target_pairs={{8,16},{24,32},{40,48},{56,64},{72,80},{88,96},{104,112},{120,128}... | collective-permute-start | bytes 884744 | tf_op jit(solution)/shard_map/ppermute | solution.py:429
  9.5 14.8 %all-to-all-start = ((bf16[8,32,128]{2,1,0:T(8,128)(2,1)}), bf16[8,32,128]{2,1,0:T(8,128)(2,1)S(1)}, u32[]{:S(2)}, u32[]{:S(2)}) async-start(bf16[8,32,128]{2,1,0:T(8,128)(2,1)} %get-tuple-element.23), calls=%async_computation | async-start | bytes 131072 | tf_op jit(solution)/shard_map/all_to_all | solution.py:424
  17.0 25.8 %copy-start = (bf16[64,4096]{1,0:T(8,128)(2,1)S(1)}, bf16[64,4096]{1,0:T(8,128)(2,1)}, u32[]{:S(2)}) copy-start(bf16[64,4096]{1,0:T(8,128)(2,1)} %v.1) | copy-start | bytes 1572868
  17.0 25.8 %copy-start.13 = (s32[12,64]{1,0:T(8,128)S(1)}, s32[12,64]{1,0:T(8,128)}, u32[]{:S(2)}) copy-start(s32[12,64]{1,0:T(8,128)} %get-tuple-element.31.ix_any) | copy-start | bytes 9220
  24.3 3.6 %collective-permute-start = (bf16[144,128]{1,0:T(8,128)(2,1)S(1)}, bf16[144,128]{1,0:T(8,128)(2,1)S(1)}, u32[]{:S(2)}, u32[]{:S(2)}) collective-permute-start(bf16[144,128]{1,0:T(8,128)(2,1)S(1)} %group_sum.1.y), channel_id=1, source_target_pairs={{0,16},{8,24},{16,0},{24,8},{32,48},{40,56},{48,32},{56,40},{64,80... | collective-permute-start | bytes 110600 | tf_op jit(solution)/shard_map/ppermute | solution.py:482
  26.2 1.0 %copy-start.6 = (bf16[1024,128]{1,0:T(8,128)(2,1)S(1)}, bf16[1024,128]{1,0:T(8,128)(2,1)}, u32[]{:S(2)}) copy-start(bf16[1024,128]{1,0:T(8,128)(2,1)} %get-tuple-element.24.faces) | copy-start | bytes 786436
  27.1 0.8 %copy-start.7 = (bf16[128,128]{1,0:T(8,128)(2,1)S(1)}, bf16[128,128]{1,0:T(8,128)(2,1)}, u32[]{:S(2)}) copy-start(bf16[128,128]{1,0:T(8,128)(2,1)} %get-tuple-element.26.nown) | copy-start | bytes 98308
  28.0 4.8 %collective-permute-start.3 = (bf16[288,128]{1,0:T(8,128)(2,1)S(1)}, bf16[288,128]{1,0:T(8,128)(2,1)S(1)}, u32[]{:S(2)}, u32[]{:S(2)}) collective-permute-start(bf16[288,128]{1,0:T(8,128)(2,1)S(1)} %table_join.3), channel_id=1, source_target_pairs={{0,32},{8,40},{16,48},{24,56},{32,0},{40,8},{48,16},{56,24},{64,96... | collective-permute-start | bytes 221192 | tf_op jit(solution)/shard_map/ppermute | solution.py:482
  30.0 12.7 %collective-permute-start.6 = (bf16[2176,128]{1,0:T(8,128)(2,1)S(1)}, bf16[2176,128]{1,0:T(8,128)(2,1)S(1)}, u32[]{:S(2)}, u32[]{:S(2)}) collective-permute-start(bf16[2176,128]{1,0:T(8,128)(2,1)S(1)} %get-tuple-element.29.after), channel_id=1, source_target_pairs={{0,1},{2,3},{4,5},{6,7},{1,0},{3,2},{5,4},{7,6},{8,9},{10,11},{12,... | collective-permute-start | bytes 1671176 | tf_op jit(solution)/shard_map/ppermute | solution.py:429
  30.6 12.2 %collective-permute-start.7 = (bf16[2176,128]{1,0:T(8,128)(2,1)S(1)}, bf16[2176,128]{1,0:T(8,128)(2,1)S(1)}, u32[]{:S(2)}, u32[]{:S(2)}) collective-permute-start(bf16[2176,128]{1,0:T(8,128)(2,1)S(1)} %get-tuple-element.32), channel_id=1, source_target_pairs={{1,2},{3,4},{5,6},{2,1},{4,3},{6,5},{9,10},{11,12},{13,14},{10,9},... | collective-permute-start | bytes 1671176 | tf_op jit(solution)/shard_map/ppermute | solution.py:429
  32.8 7.2 %collective-permute-start.4 = (bf16[576,128]{1,0:T(8,128)(2,1)S(1)}, bf16[576,128]{1,0:T(8,128)(2,1)S(1)}, u32[]{:S(2)}, u32[]{:S(2)}) collective-permute-start(bf16[576,128]{1,0:T(8,128)(2,1)S(1)} %pad_maximum_fusion.y), channel_id=1, source_target_pairs={{0,64},{8,72},{16,80},{24,88},{32,96},{40,104},{48,112},{56,120},{... | collective-permute-start | bytes 442376 | tf_op jit(solution)/shard_map/ppermute | solution.py:482
  34.2 0.9 %copy-start.9 = (bf16[16,32,32,1]{2,1,3,0:T(8,128)(2,1)S(1)}, bf16[16,32,32,1]{2,1,3,0:T(8,128)(2,1)}, u32[]{:S(2)}) copy-start(bf16[16,32,32,1]{2,1,3,0:T(8,128)(2,1)} %param.27) | copy-start | bytes 98308
  35.1 0.8 %copy-start.10 = (bf16[8,32,32,1]{2,1,3,0:T(8,128)(2,1)S(1)}, bf16[8,32,32,1]{2,1,3,0:T(8,128)(2,1)}, u32[]{:S(2)}) copy-start(bf16[8,32,32,1]{2,1,3,0:T(8,128)(2,1)} %param.29) | copy-start | bytes 49156
  40.0 13.7 %copy-start.8 = (bf16[128,128]{1,0:T(8,128)(2,1)S(1)}, bf16[128,128]{1,0:T(8,128)(2,1)}, u32[]{:S(2)}) copy-start(bf16[128,128]{1,0:T(8,128)(2,1)} %get-tuple-element.26.nown) | copy-start | bytes 98308
  40.0 13.6 %copy-start.12 = (s32[16,64]{1,0:T(8,128)S(1)}, s32[16,64]{1,0:T(8,128)}, u32[]{:S(2)}) copy-start(s32[16,64]{1,0:T(8,128)} %get-tuple-element.36.li_any) | copy-start | bytes 12292
  40.0 13.6 %copy-start.14 = (s32[8,16]{1,0:T(8,128)S(1)}, s32[8,16]{1,0:T(8,128)}, u32[]{:S(2)}) copy-start(s32[8,16]{1,0:T(8,128)} %get-tuple-element.37.mi_any) | copy-start | bytes 1540
  40.1 8.1 %collective-permute-start.5 = (bf16[1152,128]{1,0:T(8,128)(2,1)S(1)}, bf16[1152,128]{1,0:T(8,128)(2,1)S(1)}, u32[]{:S(2)}, u32[]{:S(2)}) collective-permute-start(bf16[1152,128]{1,0:T(8,128)(2,1)S(1)} %table_join.4.y), channel_id=1, source_target_pairs={{0,128},{8,136},{16,144},{24,152},{32,160},{40,168},{48,176},{56,1... | collective-permute-start | bytes 884744 | tf_op jit(solution)/shard_map/ppermute | solution.py:482
  42.8 14.0 %copy-start.3 = (bf16[32,4096]{1,0:T(8,128)(2,1)S(1)}, bf16[32,4096]{1,0:T(8,128)(2,1)}, u32[]{:S(2)}) copy-start(bf16[32,4096]{1,0:T(8,128)(2,1)} %b.1) | copy-start | bytes 786436
  42.8 14.0 %copy-start.4 = (bf16[2048,128]{1,0:T(8,128)(2,1)S(1)}, bf16[2048,128]{1,0:T(8,128)(2,1)}, u32[]{:S(2)}) copy-start(bf16[2048,128]{1,0:T(8,128)(2,1)} %get-tuple-element.35.tl) | copy-start | bytes 1572868
  42.8 14.0 %copy-start.5 = (bf16[32,32,8]{1,2,0:T(8,128)(2,1)S(1)}, bf16[32,32,8]{1,2,0:T(8,128)(2,1)}, u32[]{:S(2)}) copy-start(bf16[32,32,8]{1,2,0:T(8,128)(2,1)} %param.20) | copy-start | bytes 49156
  42.8 14.0 %copy-start.11 = (bf16[32,32,1]{1,0,2:T(8,128)(2,1)S(1)}, bf16[32,32,1]{1,0,2:T(8,128)(2,1)}, u32[]{:S(2)}) copy-start(bf16[32,32,1]{1,0,2:T(8,128)(2,1)} %param.21) | copy-start | bytes 6148
  42.9 14.0 %copy-start.15 = (s32[16,1]{0,1:T(1,128)S(1)}, s32[16,1]{0,1:T(1,128)}, u32[]{:S(2)}) copy-start(s32[16,1]{0,1:T(1,128)} %param.26) | copy-start | bytes 196
  42.9 14.0 %copy-start.16 = (s32[8,1]{0,1:T(1,128)S(1)}, s32[8,1]{0,1:T(1,128)}, u32[]{:S(2)}) copy-start(s32[8,1]{0,1:T(1,128)} %param.28) | copy-start | bytes 100
  48.2 8.6 %collective-permute-start.8 = (bf16[2304,128]{1,0:T(8,128)(2,1)S(1)}, bf16[2304,128]{1,0:T(8,128)(2,1)S(1)}, u32[]{:S(2)}, u32[]{:S(2)}) collective-permute-start(bf16[2304,128]{1,0:T(8,128)(2,1)S(1)} %table_join.5.own), channel_id=1, source_target_pairs={{0,8},{8,0},{16,24},{24,16},{32,40},{40,32},{48,56},{56,48},{64,72... | collective-permute-start | bytes 1769480 | tf_op jit(solution)/shard_map/ppermute | solution.py:482
